TPU v7x, 1024 devices: a whole 4x8x16 slice. The times are simulated.
1024 devices in a mesh: ctx: 16 (over x, y_lo, core), section: 64 (over z, y_hi).
Axes of the slice: x: 4, y: 8 (y_hi: 4, y_lo: 2; y = y_hi * 2 + y_lo), z: 16, core: 2. Of those that a mesh axis runs over, the one named last changes fastest.
Arguments:
- query_in: bfloat16 [64, 2, 2048, 1024], P('section', None, 'ctx'), may hold values from -200 to 200
- key_in: bfloat16 [64, 2, 2048, 128], P('section', None, 'ctx'), may hold values from -5 to 5
- value_in: bfloat16 [64, 2, 2048, 128], P('section', None, 'ctx'), may hold values from -24 to 24
- forward_out: bfloat16 [64, 2, 2048, 1024], P('section', None, 'ctx'), may hold values from -6 to 6
- log_sum: float32 [64, 2, 8, 2048], P('section', None, None, 'ctx'), as said below
- grad_out: bfloat16 [64, 2, 2048, 1024], P('section', None, 'ctx'), may hold values from -6 to 6
- block_order: int32 [32], replicated, may hold values from 0 to 31, each once
Outputs:
- grad_query: bfloat16 [64, 2, 2048, 1024], P('section', None, 'ctx')
- grad_key: bfloat16 [64, 2, 2048, 128], P('section', None, 'ctx')
- grad_value: bfloat16 [64, 2, 2048, 128], P('section', None, 'ctx')
Inputs may be any that keep to these rules, and one draw needn't show every extreme that they name: For every layer, micro-batch, head and row, log_sum is at least the logarithm of the sum of exp(score) over all key rows of that row's window, masked or not. block_order is a permutation: slot j, rows j * 64 to j * 64 + 63 of the token dimension, holds sequence positions block_order[j] * 64 onward in order.
All inputs are finite; a program needn't handle non-finite values.
Results may differ from a plain program's by a relative error of at most 0.008.
Values may be sent and summed in bfloat16 or wider, within the bound.
No kernel may reach another device: no remote copies, remote signals or barrier semaphores. Data moves between devices by JAX's collectives and lax.ppermute only.
A program may use at most 32 MiB of HBM per device.

v0:
```python
import math

import jax
import jax.numpy as jnp
from jax import lax
from jax.sharding import PartitionSpec as P

WINDOW = 3


def shifted(block, axis, distance):
    devices = range(lax.axis_size(axis))
    route = [((i - distance) % len(devices), i) for i in devices]
    return lax.ppermute(block, axis, route)


def shifted_2(value, axis, steps):
    count = lax.axis_size(axis)
    first, last = (max(0, -steps), min(count, count - steps))
    return lax.ppermute(value, axis, [(source, source + steps) for source in range(first, last)])


def place_rows(block_order, first_row, length, half_rows):
    row_ids = first_row + jnp.arange(length, dtype=jnp.int32)
    slot_ids = row_ids // half_rows
    lookup = (
        slot_ids[:, None] == jnp.arange(block_order.shape[0], dtype=jnp.int32)[None, :]
    ).astype(jnp.int32)
    return jnp.sum(lookup * block_order[None, :], axis=1) * half_rows + row_ids % half_rows


def pair_tile(
    query_heads, grad_heads, log_rows, row_dot, pair_block, query_places, key_places, factor
):
    key_block = pair_block[0]
    value_block = pair_block[1]
    scores = (
        jnp.einsum("qhd,kd->hqk", query_heads, key_block, preferred_element_type=jnp.float32)
        * factor
    )
    visible = query_places[:, None] >= key_places[None, :]
    probs = jnp.where(visible[None], jnp.exp(scores - log_rows[..., None]), 0.0)
    grad_probs = jnp.einsum(
        "qhd,kd->hqk", grad_heads, value_block, preferred_element_type=jnp.float32
    )
    grad_scores = (probs * (grad_probs - row_dot[..., None])).astype(jnp.bfloat16)
    probs_low = probs.astype(jnp.bfloat16)
    query_part = (
        jnp.einsum("hqk,kd->qhd", grad_scores, key_block, preferred_element_type=jnp.float32)
        * factor
    )
    key_part = (
        jnp.einsum("hqk,qhd->kd", grad_scores, query_heads, preferred_element_type=jnp.float32)
        * factor
    )
    value_part = jnp.einsum(
        "hqk,qhd->kd", probs_low, grad_heads, preferred_element_type=jnp.float32
    )
    return (query_part, jnp.stack([key_part, value_part], axis=0))


def shards(query_in, key_in, value_in, forward_out, log_sum, grad_out, block_order):
    local_rows = query_in.shape[2]
    head_size = key_in.shape[3]
    head_count = query_in.shape[3] // head_size
    members = lax.axis_size("ctx")
    half_rows = local_rows // 2
    factor = 1.0 / math.sqrt(head_size)
    own_index = lax.axis_index("ctx")
    query_places = place_rows(block_order, own_index * local_rows, local_rows, half_rows)

    def shard_places(offset):
        source = (own_index - offset + members) % members
        return place_rows(block_order, source * local_rows, local_rows, half_rows)

    def fetch(which):
        pair_list = [jnp.stack([key_in[0, which], value_in[0, which]], axis=0)]
        for offset in range(1, WINDOW):
            pair_list.append(shifted(pair_list[-1], "ctx", 1))
        return pair_list

    def backward(which, upstream):
        query_heads = query_in[0, which].reshape(local_rows, head_count, head_size)
        grad_heads = upstream.reshape(local_rows, head_count, head_size)
        out_heads = (
            forward_out[0, which].astype(jnp.float32).reshape(local_rows, head_count, head_size)
        )
        row_dot = jnp.transpose(
            jnp.sum(grad_heads.astype(jnp.float32) * out_heads, axis=-1), (1, 0)
        )
        log_rows = log_sum[0, which]
        pair_list = fetch(which)
        query_total = jnp.zeros((local_rows, head_count, head_size), jnp.float32)
        parts = []
        for offset in range(WINDOW):
            query_part, key_part = pair_tile(
                query_heads,
                grad_heads,
                log_rows,
                row_dot,
                pair_list[offset],
                query_places,
                shard_places(offset),
                factor,
            )
            query_total = query_total + query_part
            parts.append(key_part)
        carried = parts[WINDOW - 1]
        for offset in range(WINDOW - 1, 0, -1):
            carried = (
                shifted(carried.astype(jnp.bfloat16), "ctx", -1).astype(carried.dtype)
                + parts[offset - 1]
            )
        grad_query = query_total.reshape(local_rows, head_count * head_size).astype(jnp.bfloat16)
        return (grad_query, carried[0].astype(jnp.bfloat16), carried[1].astype(jnp.bfloat16))

    first = backward(0, grad_out[0, 0])
    passed = shifted_2(first[0], "section", -1)
    upstream = (grad_out[0, 1].astype(jnp.float32) + passed.astype(jnp.float32)).astype(
        jnp.bfloat16
    )
    second = backward(1, upstream)
    grad_query = jnp.stack([first[0], second[0]], axis=0)[None]
    grad_key = jnp.stack([first[1], second[1]], axis=0)[None]
    grad_value = jnp.stack([first[2], second[2]], axis=0)[None]
    return (grad_query, grad_key, grad_value)


def solution(mesh):
    in_specs = (
        P("section", None, "ctx", None),
        P("section", None, "ctx", None),
        P("section", None, "ctx", None),
        P("section", None, "ctx", None),
        P("section", None, None, "ctx"),
        P("section", None, "ctx", None),
        P(),
    )
    out_specs = (
        P("section", None, "ctx", None),
        P("section", None, "ctx", None),
        P("section", None, "ctx", None),
    )
    return jax.shard_map(shards, mesh=mesh, in_specs=in_specs, out_specs=out_specs, check_vma=False)
```

profile of v0, /device:TPU:13, one launch (start us, length us, event | category | flops | bytes accessed | tf_op | source)
XLA Modules:
  0.0 74.7 jit_solution(100234804565855963)
XLA Ops:
  0.6 0.9 %slice_bitcast_fusion.20 = (bf16[1,128,128]{2,1,0:T(8,128)(2,1)S(1)}, bf16[1,128,128]{2,1,0:T(8,128)(2,1)S(1)}, bf16[1,128,128]{2,1,0:T(8,128)(2,1)S(1)}, bf16[1,128,128]{2,1,0:T(8,128)(2,1)S(1)}) fusion(bf16[1,2,128,128]{3,2,1,0:T(8,128)(2,1)} %param.9, bf16[1,2,128,128]{3,2,1,0:T(8,128)(2,1)} %param.8), kind=kLoop, calls=%fused_computation.160 | loop fusion | bytes 262144 | tf_op jit(solution)/shard_map/stack;squeeze | solution.py:77
  1.5 0.6 pad_maximum_fusion
  2.2 3.3 %collective-permute-start = (bf16[2,128,128]{2,1,0:T(8,128)(2,1)}, bf16[2,128,128]{2,1,0:T(8,128)(2,1)}, u32[]{:S(2)}, u32[]{:S(2)}) collective-permute-start(bf16[2,128,128]{2,1,0:T(8,128)(2,1)} %pad_maximum_fusion), channel_id=1, source_target_pairs={{960,0},{0,64},{64,128},{128,192},{192,256},{256,320},{320,384},{3... | collective-permute-start | bytes 196616 | tf_op jit(solution)/shard_map/ppermute | solution.py:14
  5.4 0.6 pad_maximum_fusion.1
  6.1 1.9 %collective-permute-start.3 = (bf16[2,128,128]{2,1,0:T(8,128)(2,1)}, bf16[2,128,128]{2,1,0:T(8,128)(2,1)}, u32[]{:S(2)}, u32[]{:S(2)}) collective-permute-start(bf16[2,128,128]{2,1,0:T(8,128)(2,1)} %pad_maximum_fusion.1), channel_id=1, source_target_pairs={{960,0},{0,64},{64,128},{128,192},{192,256},{256,320},{320,384},{3... | collective-permute-start | bytes 196616 | tf_op jit(solution)/shard_map/ppermute | solution.py:14
  8.9 0.9 %slice-done = bf16[1,1,128,1024]{3,2,1,0:T(8,128)(2,1)S(1)} async-done(((bf16[1,2,128,1024]{3,2,1,0:T(8,128)(2,1)}), bf16[1,1,128,1024]{3,2,1,0:T(8,128)(2,1)S(1)}, s32[]{:S(2)}) %slice-start) | async-done | bytes 262168 | tf_op jit(solution)/shard_map/slice | solution.py:117
  12.0 0.9 %convolution_bitcast_fusion.12 = f32[1,128,128]{2,1,0:T(8,128)} fusion(bf16[128,8,128]{0,2,1:T(8,128)(2,1)S(1)} %bitcast.359, f32[8,128,128]{1,2,0:T(8,128)S(1)} %fusion.20), kind=kOutput, calls=%fused_computation.83 | convolution fusion | flops 33685504 | bytes 851968 | tf_op jit(solution)/shard_map/hqk,qhd->kd/dot_general | solution.py:56
  13.7 0.9 %fusion.60 = f32[1,128,128]{2,1,0:T(8,128)} fusion(bf16[8,128,128]{1,2,0:T(8,128)(2,1)S(1)} %fusion.53, bf16[128,8,128]{0,2,1:T(8,128)(2,1)S(1)} %bitcast.372), kind=kOutput, calls=%fused_computation.86 | convolution fusion | flops 33570816 | bytes 589824 | tf_op jit(solution)/shard_map/hqk,qhd->kd/dot_general | solution.py:53
  14.7 3.6 %collective-permute-start.1 = (bf16[2,128,128]{2,1,0:T(8,128)(2,1)}, bf16[2,128,128]{2,1,0:T(8,128)(2,1)S(1)}, u32[]{:S(2)}, u32[]{:S(2)}) collective-permute-start(bf16[2,128,128]{2,1,0:T(8,128)(2,1)} %collective-permute-done), channel_id=1, source_target_pairs={{960,0},{0,64},{64,128},{128,192},{192,256},{256,320},{320,384},{3... | collective-permute-start | bytes 196616 | tf_op jit(solution)/shard_map/ppermute | solution.py:14
  18.3 1.0 %fusion.24 = f32[8,128,128]{1,2,0:T(8,128)S(1)} fusion(bf16[128,8,128]{0,2,1:T(8,128)(2,1)S(1)} %bitcast.373, f32[8,128]{1,0:T(8,128)S(1)} %get-tuple-element.21, pred[128,128]{0,1:T(8,128)(4,1)S(1)} %get-tuple-element.24, bf16[2,128,128]{2,1,0:T(8,128)(2,1)} %collective-permute-done), kind=kOutput, calls=%fused_computation.42 | convolution fusion | flops 33947648 | bytes 839680 | tf_op jit(solution)/shard_map/qhd,kd->hqk/dot_general | solution.py:38
  19.3 1.0 %fusion.52 = bf16[8,128,128]{1,2,0:T(8,128)(2,1)S(1)} fusion(f32[8,128,128]{1,2,0:T(8,128)S(1)} %fusion.24, bf16[128,8,128]{0,2,1:T(8,128)(2,1)S(1)} %bitcast.361, f32[8,128]{1,0:T(8,128)S(1)} %bitcast.385, bf16[2,128,128]{2,1,0:T(8,128)(2,1)} %collective-permute-done), kind=kOutput, calls=%fused_computation.70 | convolution fusion | flops 33947648 | bytes 1085440 | tf_op jit(solution)/shard_map/qhd,kd->hqk/dot_general | solution.py:43
  20.6 1.9 %collective-permute-start.4 = (bf16[2,128,128]{2,1,0:T(8,128)(2,1)}, bf16[2,128,128]{2,1,0:T(8,128)(2,1)S(1)}, u32[]{:S(2)}, u32[]{:S(2)}) collective-permute-start(bf16[2,128,128]{2,1,0:T(8,128)(2,1)} %collective-permute-done.3), channel_id=1, source_target_pairs={{960,0},{0,64},{64,128},{128,192},{192,256},{256,320},{320,384},{3... | collective-permute-start | bytes 196616 | tf_op jit(solution)/shard_map/ppermute | solution.py:14
  22.5 1.0 %fusion.38 = f32[8,128,128]{1,2,0:T(8,128)S(1)} fusion(bf16[128,8,128]{0,2,1:T(8,128)(2,1)S(1)} %bitcast.366, f32[8,128]{1,0:T(8,128)S(1)} %get-tuple-element.22, pred[128,128]{0,1:T(8,128)(4,1)S(1)} %get-tuple-element.24, bf16[2,128,128]{2,1,0:T(8,128)(2,1)} %collective-permute-done.3), kind=kOutput, calls=%fused_computation.56 | convolution fusion | flops 33947648 | bytes 839680 | tf_op jit(solution)/shard_map/qhd,kd->hqk/dot_general | solution.py:38
  23.5 1.0 %fusion.26 = f32[128,8,128]{0,2,1:T(8,128)S(1)} fusion(f32[128,8,128]{0,2,1:T(8,128)S(1)} %fusion.15, bf16[8,128,128]{1,2,0:T(8,128)(2,1)S(1)} %fusion.52, bf16[2,128,128]{2,1,0:T(8,128)(2,1)} %collective-permute-done), kind=kOutput, calls=%fused_computation.44 | convolution fusion | flops 33816576 | bytes 1343488 | tf_op jit(solution)/shard_map/hqk,kd->qhd/dot_general | solution.py:49
  25.7 2.4 %collective-permute-start.5 = (bf16[2,128,128]{2,1,0:T(8,128)(2,1)S(1)}, bf16[2,128,128]{2,1,0:T(8,128)(2,1)S(1)}, u32[]{:S(2)}, u32[]{:S(2)}) collective-permute-start(bf16[2,128,128]{2,1,0:T(8,128)(2,1)S(1)} %pad_maximum_fusion.2), channel_id=1, source_target_pairs={{64,0},{128,64},{192,128},{256,192},{320,256},{384,320},{448,384},... | collective-permute-start | bytes 196616 | tf_op jit(solution)/shard_map/ppermute | solution.py:14
  28.4 0.9 %copy.138 = bf16[128,1024]{1,0:T(8,128)(2,1)} copy(bf16[128,1024]{0,1:T(8,128)(2,1)S(1)} %bitcast.377) | data formatting | bytes 524288 | tf_op jit(solution)/shard_map/convert_element_type | solution.py:114
  29.2 1.3 %collective-permute-start.2 = (bf16[128,1024]{1,0:T(8,128)(2,1)}, bf16[128,1024]{1,0:T(8,128)(2,1)}, u32[]{:S(2)}, u32[]{:S(2)}) collective-permute-start(bf16[128,1024]{1,0:T(8,128)(2,1)} %copy.138), channel_id=1, source_target_pairs={{1,0},{2,1},{3,2},{4,3},{5,4},{6,5},{7,6},{8,7},{9,8},{10,9},{11,1... | collective-permute-start | bytes 786440 | tf_op jit(solution)/shard_map/ppermute | solution.py:20
  30.5 12.2 %collective-permute-done.5 = bf16[2,128,128]{2,1,0:T(8,128)(2,1)S(1)} collective-permute-done((bf16[2,128,128]{2,1,0:T(8,128)(2,1)S(1)}, bf16[2,128,128]{2,1,0:T(8,128)(2,1)S(1)}, u32[]{:S(2)}, u32[]{:S(2)}) %collective-permute-start.5) | collective-permute-done | bytes 65568 | tf_op jit(solution)/shard_map/ppermute | solution.py:14
  42.7 0.6 fusion.86
  43.3 1.9 %collective-permute-start.6 = (bf16[2,128,128]{2,1,0:T(8,128)(2,1)}, bf16[2,128,128]{2,1,0:T(8,128)(2,1)}, u32[]{:S(2)}, u32[]{:S(2)}) collective-permute-start(bf16[2,128,128]{2,1,0:T(8,128)(2,1)} %fusion.86), channel_id=1, source_target_pairs={{64,0},{128,64},{192,128},{256,192},{320,256},{384,320},{448,384},... | collective-permute-start | bytes 196616 | tf_op jit(solution)/shard_map/ppermute | solution.py:14
  46.0 4.1 %collective-permute-done.6 = bf16[2,128,128]{2,1,0:T(8,128)(2,1)} collective-permute-done((bf16[2,128,128]{2,1,0:T(8,128)(2,1)}, bf16[2,128,128]{2,1,0:T(8,128)(2,1)}, u32[]{:S(2)}, u32[]{:S(2)}) %collective-permute-start.6) | collective-permute-done | bytes 65568 | tf_op jit(solution)/shard_map/ppermute | solution.py:14
  50.1 0.9 %fusion.87 = bf16[2,128,128]{2,1,0:T(8,128)(2,1)S(1)} fusion(f32[1,128,128]{2,1,0:T(8,128)} %convolution_bitcast_fusion.12, f32[1,128,128]{2,1,0:T(8,128)} %fusion.60, bf16[2,128,128]{2,1,0:T(8,128)(2,1)} %collective-permute-done.6), kind=kLoop, calls=%fused_computation.124 | loop fusion | flops 131072 | bytes 262144 | tf_op jit(solution)/shard_map/convert.10
  51.7 1.0 %fusion.96 = (bf16[16,8,8,128]{3,2,1,0:T(8,128)(2,1)S(1)}, bf16[16,8,8,128]{3,1,2,0:T(8,128)(2,1)S(1)}) fusion(bf16[128,1024]{1,0:T(8,128)(2,1)} %collective-permute-done.2, bf16[1,2,128,1024]{3,2,1,0:T(8,128)(2,1)S(1)} %copy-done), kind=kLoop, calls=%fused_computation.135 | loop fusion | flops 524288 | bytes 1048576
  54.8 1.9 %collective-permute-start.7 = (bf16[2,128,128]{2,1,0:T(8,128)(2,1)S(1)}, bf16[2,128,128]{2,1,0:T(8,128)(2,1)S(1)}, u32[]{:S(2)}, u32[]{:S(2)}) collective-permute-start(bf16[2,128,128]{2,1,0:T(8,128)(2,1)S(1)} %pad_maximum_fusion.3), channel_id=1, source_target_pairs={{64,0},{128,64},{192,128},{256,192},{320,256},{384,320},{448,384},... | collective-permute-start | bytes 196616 | tf_op jit(solution)/shard_map/ppermute | solution.py:14
  57.0 1.0 %fusion.48 = bf16[8,128,128]{1,2,0:T(8,128)(2,1)S(1)} fusion(f32[8,128,128]{1,2,0:T(8,128)S(1)} %fusion.38, f32[8,128]{1,0:T(8,128)S(1)} %copy.141, bf16[16,8,8,128]{3,2,1,0:T(8,128)(2,1)S(1)} %get-tuple-element.7, bf16[2,128,128]{2,1,0:T(8,128)(2,1)} %collective-permute-done.3), kind=kOutput, calls=%fused_computation.66 | convolution fusion | flops 33947648 | bytes 1085440 | tf_op jit(solution)/shard_map/qhd,kd->hqk/dot_general | solution.py:43
  58.5 1.0 %fusion.40 = f32[128,8,128]{0,2,1:T(8,128)S(1)} fusion(f32[128,8,128]{0,2,1:T(8,128)S(1)} %fusion.6, bf16[8,128,128]{1,2,0:T(8,128)(2,1)S(1)} %fusion.48, bf16[2,128,128]{2,1,0:T(8,128)(2,1)} %collective-permute-done.3), kind=kOutput, calls=%fused_computation.58 | convolution fusion | flops 33816576 | bytes 1343488 | tf_op jit(solution)/shard_map/hqk,kd->qhd/dot_general | solution.py:49
  60.1 5.9 %collective-permute-done.7 = bf16[2,128,128]{2,1,0:T(8,128)(2,1)S(1)} collective-permute-done((bf16[2,128,128]{2,1,0:T(8,128)(2,1)S(1)}, bf16[2,128,128]{2,1,0:T(8,128)(2,1)S(1)}, u32[]{:S(2)}, u32[]{:S(2)}) %collective-permute-start.7) | collective-permute-done | bytes 65568 | tf_op jit(solution)/shard_map/ppermute | solution.py:14
  66.0 1.9 %collective-permute-start.8 = (bf16[2,128,128]{2,1,0:T(8,128)(2,1)S(1)}, bf16[2,128,128]{2,1,0:T(8,128)(2,1)S(1)}, u32[]{:S(2)}, u32[]{:S(2)}) collective-permute-start(bf16[2,128,128]{2,1,0:T(8,128)(2,1)S(1)} %fusion.88), channel_id=1, source_target_pairs={{64,0},{128,64},{192,128},{256,192},{320,256},{384,320},{448,384},... | collective-permute-start | bytes 196616 | tf_op jit(solution)/shard_map/ppermute | solution.py:14
  67.9 0.8 %maximum_bitcast_fusion = bf16[1,2,128,1024]{3,2,1,0:T(8,128)(2,1)} fusion(bf16[1,128,1024]{2,1,0:T(8,128)(2,1)S(1)} %copy.153, bf16[1,128,1024]{2,1,0:T(8,128)(2,1)S(1)} %copy.152), kind=kLoop, calls=%fused_computation.102 | loop fusion | flops 262144 | bytes 1048576 | tf_op jit(solution)/shard_map/broadcast_in_dim | solution.py:123
  68.8 3.7 %collective-permute-done.8 = bf16[2,128,128]{2,1,0:T(8,128)(2,1)S(1)} collective-permute-done((bf16[2,128,128]{2,1,0:T(8,128)(2,1)S(1)}, bf16[2,128,128]{2,1,0:T(8,128)(2,1)S(1)}, u32[]{:S(2)}, u32[]{:S(2)}) %collective-permute-start.8) | collective-permute-done | bytes 65568 | tf_op jit(solution)/shard_map/ppermute | solution.py:14
  72.5 0.7 copy-done.8
  73.3 0.6 maximum_bitcast_fusion.2
  (78 shorter events, 11.1 us)
Async XLA Ops:
  0.6 7.5 %copy-start.2 = (bf16[1,2,128,1024]{3,2,1,0:T(8,128)(2,1)S(1)}, bf16[1,2,128,1024]{3,2,1,0:T(8,128)(2,1)}, u32[]{:S(2)}) copy-start(bf16[1,2,128,1024]{3,2,1,0:T(8,128)(2,1)} %param.7) | copy-start | bytes 1572868
  2.2 12.5 %collective-permute-start = (bf16[2,128,128]{2,1,0:T(8,128)(2,1)}, bf16[2,128,128]{2,1,0:T(8,128)(2,1)}, u32[]{:S(2)}, u32[]{:S(2)}) collective-permute-start(bf16[2,128,128]{2,1,0:T(8,128)(2,1)} %pad_maximum_fusion), channel_id=1, source_target_pairs={{960,0},{0,64},{64,128},{128,192},{192,256},{256,320},{320,384},{3... | collective-permute-start | bytes 196616 | tf_op jit(solution)/shard_map/ppermute | solution.py:14
  6.1 14.5 %collective-permute-start.3 = (bf16[2,128,128]{2,1,0:T(8,128)(2,1)}, bf16[2,128,128]{2,1,0:T(8,128)(2,1)}, u32[]{:S(2)}, u32[]{:S(2)}) collective-permute-start(bf16[2,128,128]{2,1,0:T(8,128)(2,1)} %pad_maximum_fusion.1), channel_id=1, source_target_pairs={{960,0},{0,64},{64,128},{128,192},{192,256},{256,320},{320,384},{3... | collective-permute-start | bytes 196616 | tf_op jit(solution)/shard_map/ppermute | solution.py:14
  8.2 0.7 copy-start.9
  8.9 0.9 %slice-start = ((bf16[1,2,128,1024]{3,2,1,0:T(8,128)(2,1)}), bf16[1,1,128,1024]{3,2,1,0:T(8,128)(2,1)S(1)}, s32[]{:S(2)}) async-start(bf16[1,2,128,1024]{3,2,1,0:T(8,128)(2,1)} %param.12), calls=%async_computation | async-start | bytes 524288 | tf_op jit(solution)/shard_map/slice | solution.py:117
  8.9 1.1 %copy-start.3 = (bf16[1,2,128,1024]{3,2,1,0:T(8,128)(2,1)S(1)}, bf16[1,2,128,1024]{3,2,1,0:T(8,128)(2,1)}, u32[]{:S(2)}) copy-start(bf16[1,2,128,1024]{3,2,1,0:T(8,128)(2,1)} %param.10) | copy-start | bytes 1572868
  10.1 0.7 copy-start.10
  10.8 0.8 %copy-start.1 = (bf16[1,2,128,128]{3,2,1,0:T(8,128)(2,1)S(1)}, bf16[1,2,128,128]{3,2,1,0:T(8,128)(2,1)}, u32[]{:S(2)}) copy-start(bf16[1,2,128,128]{3,2,1,0:T(8,128)(2,1)} %param.8) | copy-start | bytes 196612
  11.9 0.9 %copy-start.4 = (bf16[1,2,128,128]{3,2,1,0:T(8,128)(2,1)S(1)}, bf16[1,2,128,128]{3,2,1,0:T(8,128)(2,1)}, u32[]{:S(2)}) copy-start(bf16[1,2,128,128]{3,2,1,0:T(8,128)(2,1)} %param.9) | copy-start | bytes 196612
  14.7 10.0 %collective-permute-start.1 = (bf16[2,128,128]{2,1,0:T(8,128)(2,1)}, bf16[2,128,128]{2,1,0:T(8,128)(2,1)S(1)}, u32[]{:S(2)}, u32[]{:S(2)}) collective-permute-start(bf16[2,128,128]{2,1,0:T(8,128)(2,1)} %collective-permute-done), channel_id=1, source_target_pairs={{960,0},{0,64},{64,128},{128,192},{192,256},{256,320},{320,384},{3... | collective-permute-start | bytes 196616 | tf_op jit(solution)/shard_map/ppermute | solution.py:14
  20.6 24.7 %collective-permute-start.4 = (bf16[2,128,128]{2,1,0:T(8,128)(2,1)}, bf16[2,128,128]{2,1,0:T(8,128)(2,1)S(1)}, u32[]{:S(2)}, u32[]{:S(2)}) collective-permute-start(bf16[2,128,128]{2,1,0:T(8,128)(2,1)} %collective-permute-done.3), channel_id=1, source_target_pairs={{960,0},{0,64},{64,128},{128,192},{192,256},{256,320},{320,384},{3... | collective-permute-start | bytes 196616 | tf_op jit(solution)/shard_map/ppermute | solution.py:14
  25.7 17.0 %collective-permute-start.5 = (bf16[2,128,128]{2,1,0:T(8,128)(2,1)S(1)}, bf16[2,128,128]{2,1,0:T(8,128)(2,1)S(1)}, u32[]{:S(2)}, u32[]{:S(2)}) collective-permute-start(bf16[2,128,128]{2,1,0:T(8,128)(2,1)S(1)} %pad_maximum_fusion.2), channel_id=1, source_target_pairs={{64,0},{128,64},{192,128},{256,192},{320,256},{384,320},{448,384},... | collective-permute-start | bytes 196616 | tf_op jit(solution)/shard_map/ppermute | solution.py:14
  29.2 22.4 %collective-permute-start.2 = (bf16[128,1024]{1,0:T(8,128)(2,1)}, bf16[128,1024]{1,0:T(8,128)(2,1)}, u32[]{:S(2)}, u32[]{:S(2)}) collective-permute-start(bf16[128,1024]{1,0:T(8,128)(2,1)} %copy.138), channel_id=1, source_target_pairs={{1,0},{2,1},{3,2},{4,3},{5,4},{6,5},{7,6},{8,7},{9,8},{10,9},{11,1... | collective-permute-start | bytes 786440 | tf_op jit(solution)/shard_map/ppermute | solution.py:20
  43.3 6.8 %collective-permute-start.6 = (bf16[2,128,128]{2,1,0:T(8,128)(2,1)}, bf16[2,128,128]{2,1,0:T(8,128)(2,1)}, u32[]{:S(2)}, u32[]{:S(2)}) collective-permute-start(bf16[2,128,128]{2,1,0:T(8,128)(2,1)} %fusion.86), channel_id=1, source_target_pairs={{64,0},{128,64},{192,128},{256,192},{320,256},{384,320},{448,384},... | collective-permute-start | bytes 196616 | tf_op jit(solution)/shard_map/ppermute | solution.py:14
  45.2 0.6 copy-start.5
  45.9 5.8 %copy-start = (bf16[1,2,128,1024]{3,2,1,0:T(8,128)(2,1)S(1)}, bf16[1,2,128,1024]{3,2,1,0:T(8,128)(2,1)}, u32[]{:S(2)}) copy-start(bf16[1,2,128,1024]{3,2,1,0:T(8,128)(2,1)} %param.12) | copy-start | bytes 1572868
  53.5 0.8 %copy-start.6 = (bf16[2,128,128]{2,1,0:T(8,128)(2,1)S(1)}, bf16[2,128,128]{2,1,0:T(8,128)(2,1)}, u32[]{:S(2)}) copy-start(bf16[2,128,128]{2,1,0:T(8,128)(2,1)} %copy-done.5) | copy-start | bytes 196612
  54.8 11.2 %collective-permute-start.7 = (bf16[2,128,128]{2,1,0:T(8,128)(2,1)S(1)}, bf16[2,128,128]{2,1,0:T(8,128)(2,1)S(1)}, u32[]{:S(2)}, u32[]{:S(2)}) collective-permute-start(bf16[2,128,128]{2,1,0:T(8,128)(2,1)S(1)} %pad_maximum_fusion.3), channel_id=1, source_target_pairs={{64,0},{128,64},{192,128},{256,192},{320,256},{384,320},{448,384},... | collective-permute-start | bytes 196616 | tf_op jit(solution)/shard_map/ppermute | solution.py:14
  66.0 6.5 %collective-permute-start.8 = (bf16[2,128,128]{2,1,0:T(8,128)(2,1)S(1)}, bf16[2,128,128]{2,1,0:T(8,128)(2,1)S(1)}, u32[]{:S(2)}, u32[]{:S(2)}) collective-permute-start(bf16[2,128,128]{2,1,0:T(8,128)(2,1)S(1)} %fusion.88), channel_id=1, source_target_pairs={{64,0},{128,64},{192,128},{256,192},{320,256},{384,320},{448,384},... | collective-permute-start | bytes 196616 | tf_op jit(solution)/shard_map/ppermute | solution.py:14
  72.5 0.8 %copy-start.8 = (bf16[1,128,128]{2,1,0:T(8,128)(2,1)S(1)}, bf16[1,128,128]{2,1,0:T(8,128)(2,1)}, u32[]{:S(2)}) copy-start(bf16[1,128,128]{2,1,0:T(8,128)(2,1)} %get-tuple-element.13) | copy-start | bytes 98308
  73.3 0.8 %copy-start.7 = (bf16[1,128,128]{2,1,0:T(8,128)(2,1)S(1)}, bf16[1,128,128]{2,1,0:T(8,128)(2,1)}, u32[]{:S(2)}) copy-start(bf16[1,128,128]{2,1,0:T(8,128)(2,1)} %get-tuple-element.14) | copy-start | bytes 98308
where the time goes:
time: 75.8 us; the launch traced here: 74.7 us
  waiting for transfers between devices  25.8 us (34%)
  starting transfers between devices  20.1 us (27%)
  matrix products  12.9 us (17%)
  local copies, waits for them, and re-layouts  7.94 us (10%)
  other arithmetic  6.68 us (9%)
  between operations  1.25 us (2%)
    ppermute x8, waiting for transfers between devices, shifted(): return lax.ppermute(block, axis, route)  25.8 us
    ppermute x8, starting transfers between devices, shifted(): return lax.ppermute(block, axis, route)  18.8 us
    unnamed x28, local copies, waits for them, and re-layouts  4.27 us
    dot_general x6, matrix products, pair_tile(): jnp.einsum('hqk,kd->qhd', grad_scores, key_block, preferred_element_type=...  3.05 us
    dot_general x6, matrix products, pair_tile(): jnp.einsum('qhd,kd->hqk', query_heads, key_block, preferred_element_type=...  3 us
    dot_general x6, matrix products, pair_tile(): jnp.einsum('qhd,kd->hqk', grad_heads, value_block, preferred_element_type...  2.86 us
    dot_general x6, matrix products, pair_tile(): jnp.einsum('hqk,qhd->kd', probs_low, grad_heads, preferred_element_type=j...  2 us
    dot_general x6, matrix products, pair_tile(): jnp.einsum('hqk,qhd->kd', grad_scores, query_heads, preferred_element_typ...  1.98 us
  transfers between devices with their start and end apart: 9, of which 4 were waited for; matrix products, arithmetic and copies ran while one was open for 24% of the time, Pallas kernels for 0%

commit v1 on v0

v1 whole, which is shorter than its diff:
```python
import functools
import math

import jax
import jax.numpy as jnp
from jax import lax
from jax.experimental import pallas as pl
from jax.experimental.pallas import tpu as pltpu
from jax.sharding import PartitionSpec as P

WINDOW = 3
PAIR = 2
NT = (((1,), (1,)), ((), ()))
NN = (((1,), (0,)), ((), ()))


def dot(a, b, dims):
    return lax.dot_general(a, b, dims, preferred_element_type=jnp.float32)


def ring(value, steps):
    count = lax.axis_size("ctx")
    return lax.ppermute(value, "ctx", [(i, (i + steps) % count) for i in range(count)])


def down(value):
    count = lax.axis_size("section")
    return lax.ppermute(value, "section", [(i, i - 1) for i in range(1, count)])


def mask_bias(order_ref, rows):
    half = rows // 2
    slots = order_ref.shape[0]
    own = lax.axis_index("ctx")
    lane = lax.broadcasted_iota(jnp.int32, (half, rows), 1)
    sub = lax.broadcasted_iota(jnp.int32, (half, rows), 0)
    query = jnp.where(
        lane < half,
        order_ref[2 * own] * half + lane,
        order_ref[2 * own + 1] * half + lane - half,
    )
    blocks = []
    for offset in range(WINDOW):
        for part in range(2):
            slot = lax.rem(2 * (own - offset) + part + slots, slots)
            blocks.append(jnp.where(order_ref[slot] * half + sub <= query, 0.0, -1e30))
    return jnp.concatenate(blocks, axis=0)


def stacked(block, first, size):
    return jnp.concatenate(
        [block[:, (first + i) * size : (first + i + 1) * size] for i in range(PAIR)], axis=0
    )


def head_rows(table, first):
    return jnp.concatenate([table[first + i : first + i + 1] for i in range(PAIR)], axis=1)


def dots_of_rows(upstream, out, heads, size):
    product = upstream.astype(jnp.float32) * out.astype(jnp.float32)
    high = product.astype(jnp.bfloat16)
    low = (product - high.astype(jnp.float32)).astype(jnp.bfloat16)
    pick = (
        lax.broadcasted_iota(jnp.int32, (heads, heads * size), 1) // size
        == lax.broadcasted_iota(jnp.int32, (heads, heads * size), 0)
    ).astype(jnp.float32).astype(jnp.bfloat16)
    return dot(pick, high, NT) + dot(pick, low, NT)


def window_of(refs, which):
    return jnp.concatenate([ref[0, which] for ref in refs], axis=0)


def scores_back(query, grad, keys, values, bias, log_row, dot_row, factor):
    scores = dot(keys, query, NT)
    probs = jnp.exp(scores * factor + (bias - log_row))
    grad_probs = dot(values, grad, NT)
    return probs.astype(jnp.bfloat16), (probs * (grad_probs - dot_row)).astype(jnp.bfloat16)


def query_kernel(factor, order_ref, q_ref, g_ref, o_ref, log_ref, kv0, kv1, kv2, dq_ref):
    query, grad, log_rows = q_ref[0, 0], g_ref[0, 0], log_ref[0, 0]
    rows, size = query.shape[0], kv0.shape[3]
    heads = query.shape[1] // size
    keys, values = window_of((kv0, kv1, kv2), 0), window_of((kv0, kv1, kv2), 1)
    keys_t = keys.T
    bias = mask_bias(order_ref, rows)
    bias = jnp.concatenate([bias] * PAIR, axis=1)
    dot_rows = dots_of_rows(grad, o_ref[0, 0], heads, size)
    for first in range(0, heads, PAIR):
        _, grad_scores = scores_back(
            stacked(query, first, size),
            stacked(grad, first, size),
            keys,
            values,
            bias,
            head_rows(log_rows, first),
            head_rows(dot_rows, first),
            factor,
        )
        part = (dot(keys_t, grad_scores, NN) * factor).T.astype(jnp.bfloat16)
        for i in range(PAIR):
            dq_ref[:, (first + i) * size : (first + i + 1) * size] = part[i * rows : (i + 1) * rows]


def pair_kernel(factor, micro, order_ref, q_ref, g_ref, o_ref, log_ref, kv0, kv1, kv2, *refs):
    if micro:
        r_ref, _, gq_ref, own_ref, near_ref, far_ref = refs
    else:
        dq_ref, gq_ref, own_ref, near_ref, far_ref = refs
    query, grad, log_rows = q_ref[0, 0], g_ref[0, 0], log_ref[0, 0]
    if micro:
        grad = (grad.astype(jnp.float32) + r_ref[...].astype(jnp.float32)).astype(jnp.bfloat16)
    else:
        gq_ref[0, 0] = dq_ref[...]
    rows, size = query.shape[0], kv0.shape[3]
    heads = query.shape[1] // size
    keys, values = window_of((kv0, kv1, kv2), 0), window_of((kv0, kv1, kv2), 1)
    keys_t = keys.T
    bias = mask_bias(order_ref, rows)
    bias = jnp.concatenate([bias] * PAIR, axis=1)
    dot_rows = dots_of_rows(grad, o_ref[0, 0], heads, size)
    key_sum = value_sum = None
    for first in range(0, heads, PAIR):
        query_pair, grad_pair = stacked(query, first, size), stacked(grad, first, size)
        probs, grad_scores = scores_back(
            query_pair,
            grad_pair,
            keys,
            values,
            bias,
            head_rows(log_rows, first),
            head_rows(dot_rows, first),
            factor,
        )
        key_part = dot(grad_scores, query_pair, NN)
        value_part = dot(probs, grad_pair, NN)
        key_sum = key_part if key_sum is None else key_sum + key_part
        value_sum = value_part if value_sum is None else value_sum + value_part
        if micro:
            part = (dot(keys_t, grad_scores, NN) * factor).T.astype(jnp.bfloat16)
            for i in range(PAIR):
                gq_ref[0, 0, :, (first + i) * size : (first + i + 1) * size] = part[
                    i * rows : (i + 1) * rows
                ]
    key_sum = key_sum * factor
    own_ref[0], own_ref[1] = key_sum[:rows], value_sum[:rows]
    for offset, ref in ((1, near_ref), (2, far_ref)):
        ref[0] = key_sum[offset * rows : (offset + 1) * rows].astype(jnp.bfloat16)
        ref[1] = value_sum[offset * rows : (offset + 1) * rows].astype(jnp.bfloat16)


def sum_kernel(own0, near0, far0, own1, near1, far1, gk_ref, gv_ref):
    for micro, (own, near, far) in enumerate(((own0, near0, far0), (own1, near1, far1))):
        for which, ref in ((0, gk_ref), (1, gv_ref)):
            total = own[which] + near[which].astype(jnp.float32) + far[which].astype(jnp.float32)
            ref[0, micro] = total.astype(jnp.bfloat16)


def cost(rows, heads, size, products):
    flops = 2 * rows * heads * WINDOW * rows * size * products
    return pl.CostEstimate(
        flops=flops, bytes_accessed=4 * rows * heads * size * 2, transcendentals=rows * heads * WINDOW * rows
    )


def shards(query_in, key_in, value_in, forward_out, log_sum, grad_out, block_order):
    rows, width = query_in.shape[2:]
    size = key_in.shape[3]
    heads = width // size
    factor = 1.0 / math.sqrt(size)
    params = pltpu.CompilerParams(vmem_limit_bytes=48 * 2**20)

    def whole(shape):
        return pl.BlockSpec(shape, lambda i: (0,) * len(shape))

    def at(shape, micro):
        return pl.BlockSpec(shape, lambda i: (0, micro) + (0,) * (len(shape) - 2))

    def pair_at(micro):
        return pl.BlockSpec((1, 2, rows, size), lambda i: (micro, 0, 0, 0))

    def in_specs(micro):
        return [
            pl.BlockSpec(memory_space=pltpu.SMEM),
            at((1, 1, rows, width), micro),
            at((1, 1, rows, width), micro),
            at((1, 1, rows, width), micro),
            at((1, 1, heads, rows), micro),
        ] + [pair_at(micro)] * WINDOW

    key_value = jnp.stack([key_in[0], value_in[0]], axis=1)
    window = (key_value, ring(key_value, 1), ring(key_value, 2))
    common = (block_order, query_in, grad_out, forward_out, log_sum, *window)

    dq = pl.pallas_call(
        functools.partial(query_kernel, factor),
        grid=(1,),
        in_specs=in_specs(0),
        out_specs=whole((rows, width)),
        out_shape=jax.ShapeDtypeStruct((rows, width), jnp.bfloat16),
        compiler_params=params,
        cost_estimate=cost(rows, heads, size, 3),
        name="query_first",
    )(*common)
    received = down(dq)

    terms_shape = [
        jax.ShapeDtypeStruct((1, 2, rows, width), jnp.bfloat16),
        jax.ShapeDtypeStruct((2, rows, size), jnp.float32),
        jax.ShapeDtypeStruct((2, rows, size), jnp.bfloat16),
        jax.ShapeDtypeStruct((2, rows, size), jnp.bfloat16),
    ]
    term_specs = [whole((2, rows, size))] * 3
    grad_query, own0, near0, far0 = pl.pallas_call(
        functools.partial(pair_kernel, factor, 0),
        grid=(1,),
        in_specs=in_specs(0) + [whole((rows, width))],
        out_specs=[at((1, 1, rows, width), 0)] + term_specs,
        out_shape=terms_shape,
        compiler_params=params,
        cost_estimate=cost(rows, heads, size, 4),
        name="pairs_first",
    )(*common, dq)
    far0, near0 = ring(far0, -2), ring(near0, -1)

    grad_query, own1, near1, far1 = pl.pallas_call(
        functools.partial(pair_kernel, factor, 1),
        grid=(1,),
        in_specs=in_specs(1) + [whole((rows, width)), pl.BlockSpec(memory_space=pl.ANY)],
        out_specs=[at((1, 1, rows, width), 1)] + term_specs,
        out_shape=terms_shape,
        input_output_aliases={9: 0},
        compiler_params=params,
        cost_estimate=cost(rows, heads, size, 5),
        name="pairs_second",
    )(*common, received, grad_query)
    far1, near1 = ring(far1, -2), ring(near1, -1)

    grad_key, grad_value = pl.pallas_call(
        sum_kernel,
        out_shape=[jax.ShapeDtypeStruct((1, 2, rows, size), jnp.bfloat16)] * 2,
        compiler_params=params,
        name="sums",
    )(own0, near0, far0, own1, near1, far1)
    return (grad_query, grad_key, grad_value)


def solution(mesh):
    split = P("section", None, "ctx", None)
    return jax.shard_map(
        shards,
        mesh=mesh,
        in_specs=(split, split, split, split, P("section", None, None, "ctx"), split, P()),
        out_specs=(split, split, split),
        check_vma=False,
    )
```

time: 75.8 us -> 54.9 us (0.72)
  the two profiles are of different devices: /device:TPU:13 before, /device:TPU:14 now
where the time goes in v1:
time: 54.9 us; the launch traced here: 54.4 us
  starting transfers between devices  27.5 us (50%)
  waiting for transfers between devices  14 us (26%)
  Pallas kernels  8.16 us (15%)
  local copies, waits for them, and re-layouts  3.13 us (6%)
  other arithmetic  0.9 us (2%)
  between operations  0.74 us (1%)
    ppermute x6, starting transfers between devices, ring(): lax.ppermute(value, 'ctx', [(i, (i + steps) % count) for i in range(count)])  26.2 us
    ppermute x6, waiting for transfers between devices, ring(): lax.ppermute(value, 'ctx', [(i, (i + steps) % count) for i in range(count)])  10.7 us
    ppermute x1, waiting for transfers between devices, down(): return lax.ppermute(value, 'section', [(i, i - 1) for i in range(1, count)])  3.36 us
    unnamed x10, local copies, waits for them, and re-layouts  3.13 us
    pallas_call x1, Pallas kernels, shards(): pl.pallas_call(functools.partial(pair_kernel, factor, 1), grid=(1,), in_s...  2.96 us
    pallas_call x1, Pallas kernels, shards(): pl.pallas_call(functools.partial(pair_kernel, factor, 0), grid=(1,), in_s...  2.49 us
    pallas_call x1, Pallas kernels, shards(): pl.pallas_call(functools.partial(query_kernel, factor), grid=(1,), in_spe...  2.03 us
    ppermute x1, starting transfers between devices, down(): return lax.ppermute(value, 'section', [(i, i - 1) for i in range(1, count)])  1.29 us
  transfers between devices with their start and end apart: 7, of which 4 were waited for; matrix products, arithmetic and copies ran while one was open for 0% of the time, Pallas kernels for 10%

profile of v1, /device:TPU:14, one launch (start us, length us, event | category | flops | bytes accessed | tf_op | source)
XLA Modules:
  0.0 54.4 jit_solution(6321203971130222588)
XLA Ops:
  0.6 0.0 copy-start.3
  0.6 0.0 copy-start.4
  0.7 0.9 %pad_maximum_fusion.kv0 = bf16[2,2,128,128]{3,2,1,0:T(8,128)(2,1)S(1)} fusion(bf16[2,1,128,128]{3,2,1,0:T(8,128)(2,1)} %bitcast.2, bf16[2,1,128,128]{3,2,1,0:T(8,128)(2,1)} %bitcast.3), kind=kLoop, calls=%fused_computation | loop fusion | flops 65536 | bytes 262144 | tf_op jit(solution)/shard_map/stack | solution.py:193
  1.6 14.9 %collective-permute-start.1 = (bf16[2,2,128,128]{3,2,1,0:T(8,128)(2,1)S(1)}, bf16[2,2,128,128]{3,2,1,0:T(8,128)(2,1)S(1)}, u32[]{:S(2)}, u32[]{:S(2)}) collective-permute-start(bf16[2,2,128,128]{3,2,1,0:T(8,128)(2,1)S(1)} %pad_maximum_fusion.kv0), channel_id=1, source_target_pairs={{0,128},{64,192},{128,256},{192,320},{256,384},{320,448},{384,512}... | collective-permute-start | bytes 393224 | tf_op jit(solution)/shard_map/ppermute | solution.py:23
  16.5 1.9 %collective-permute-start = (bf16[2,2,128,128]{3,2,1,0:T(8,128)(2,1)S(1)}, bf16[2,2,128,128]{3,2,1,0:T(8,128)(2,1)S(1)}, u32[]{:S(2)}, u32[]{:S(2)}) collective-permute-start(bf16[2,2,128,128]{3,2,1,0:T(8,128)(2,1)S(1)} %pad_maximum_fusion.kv0), channel_id=1, source_target_pairs={{0,64},{64,128},{128,192},{192,256},{256,320},{320,384},{384,448},... | collective-permute-start | bytes 393224 | tf_op jit(solution)/shard_map/ppermute | solution.py:23
  18.4 0.6 %collective-permute-done.1.kv2 = bf16[2,2,128,128]{3,2,1,0:T(8,128)(2,1)S(1)} collective-permute-done((bf16[2,2,128,128]{3,2,1,0:T(8,128)(2,1)S(1)}, bf16[2,2,128,128]{3,2,1,0:T(8,128)(2,1)S(1)}, u32[]{:S(2)}, u32[]{:S(2)}) %collective-permute-start.1) | collective-permute-done | bytes 131104 | tf_op jit(solution)/shard_map/ppermute | solution.py:23
  19.0 3.8 %collective-permute-done.kv1 = bf16[2,2,128,128]{3,2,1,0:T(8,128)(2,1)S(1)} collective-permute-done((bf16[2,2,128,128]{3,2,1,0:T(8,128)(2,1)S(1)}, bf16[2,2,128,128]{3,2,1,0:T(8,128)(2,1)S(1)}, u32[]{:S(2)}, u32[]{:S(2)}) %collective-permute-start) | collective-permute-done | bytes 131104 | tf_op jit(solution)/shard_map/ppermute | solution.py:23
  22.8 0.0 copy-done.3
  22.8 0.0 copy-done.4
  22.8 0.0 copy-start
  22.8 1.0 %copy-done = bf16[1,2,128,1024]{3,2,1,0:T(8,128)(2,1)S(1)} copy-done((bf16[1,2,128,1024]{3,2,1,0:T(8,128)(2,1)S(1)}, bf16[1,2,128,1024]{3,2,1,0:T(8,128)(2,1)}, u32[]{:S(2)}) %copy-start) | copy-done | bytes 524312
  23.8 0.0 copy-start.1
  23.8 1.0 %copy-done.1 = bf16[1,2,128,1024]{3,2,1,0:T(8,128)(2,1)S(1)} copy-done((bf16[1,2,128,1024]{3,2,1,0:T(8,128)(2,1)S(1)}, bf16[1,2,128,1024]{3,2,1,0:T(8,128)(2,1)}, u32[]{:S(2)}) %copy-start.1) | copy-done | bytes 524312
  24.9 0.0 copy-start.2
  24.9 1.0 %copy-done.2 = bf16[1,2,128,1024]{3,2,1,0:T(8,128)(2,1)S(1)} copy-done((bf16[1,2,128,1024]{3,2,1,0:T(8,128)(2,1)S(1)}, bf16[1,2,128,1024]{3,2,1,0:T(8,128)(2,1)}, u32[]{:S(2)}) %copy-start.2) | copy-done | bytes 524312
  25.9 2.0 %query_first.1.refs_0_ = bf16[128,1024]{1,0:T(8,128)(2,1)S(1)} custom-call(s32[32]{0:T(128)S(1)} %copy-done.4, bf16[1,2,128,1024]{3,2,1,0:T(8,128)(2,1)S(1)} %copy-done, bf16[1,2,128,1024]{3,2,1,0:T(8,128)(2,1)S(1)} %copy-done.1, bf16[1,2,128,1024]{3,2,1,0:T(8,128)(2,1)S(1)} %copy-done.2, f32[1,2,8,128]{3,2,1,0:T(8,128)S(1)} %copy-done.3, ...), custom_call_target="tpu_custom_call" | custom-call | flops 301989888 | bytes 1048576 | tf_op jit(solution)/shard_map/query_first/pallas_call | solution.py:197
  27.9 1.3 %collective-permute-start.2 = (bf16[128,1024]{1,0:T(8,128)(2,1)S(1)}, bf16[128,1024]{1,0:T(8,128)(2,1)S(1)}, u32[]{:S(2)}, u32[]{:S(2)}) collective-permute-start(bf16[128,1024]{1,0:T(8,128)(2,1)S(1)} %query_first.1.refs_0_), channel_id=1, source_target_pairs={{1,0},{2,1},{3,2},{4,3},{5,4},{6,5},{7,6},{8,7},{9,8},{10,9},{11,1... | collective-permute-start | bytes 786440 | tf_op jit(solution)/shard_map/ppermute | solution.py:28
  29.2 2.5 %pairs_first.1 = (bf16[1,2,128,1024]{3,2,1,0:T(8,128)(2,1)}, f32[2,128,128]{2,1,0:T(8,128)S(1)}, bf16[2,128,128]{2,1,0:T(8,128)(2,1)S(1)}, bf16[2,128,128]{2,1,0:T(8,128)(2,1)S(1)}) custom-call(s32[32]{0:T(128)S(1)} %copy-done.4, bf16[1,2,128,1024]{3,2,1,0:T(8,128)(2,1)S(1)} %copy-done, bf16[1,2,128,1024]{3,2,1,0:T(8,128)(2,1)S(1)} %copy-done.1, ...), custom_call_target="tpu_custom_call" | custom-call | flops 402653184 | bytes 1048576 | tf_op jit(solution)/shard_map/pairs_first/pallas_call | solution.py:216
  31.7 1.9 %collective-permute-start.3 = (bf16[2,128,128]{2,1,0:T(8,128)(2,1)S(1)}, bf16[2,128,128]{2,1,0:T(8,128)(2,1)S(1)}, u32[]{:S(2)}, u32[]{:S(2)}) collective-permute-start(bf16[2,128,128]{2,1,0:T(8,128)(2,1)S(1)} %get-tuple-element.16), channel_id=1, source_target_pairs={{0,960},{64,0},{128,64},{192,128},{256,192},{320,256},{384,320},{4... | collective-permute-start | bytes 196616 | tf_op jit(solution)/shard_map/ppermute | solution.py:23
  33.6 1.9 %collective-permute-start.4 = (bf16[2,128,128]{2,1,0:T(8,128)(2,1)S(1)}, bf16[2,128,128]{2,1,0:T(8,128)(2,1)S(1)}, u32[]{:S(2)}, u32[]{:S(2)}) collective-permute-start(bf16[2,128,128]{2,1,0:T(8,128)(2,1)S(1)} %get-tuple-element.17), channel_id=1, source_target_pairs={{0,896},{64,960},{128,0},{192,64},{256,128},{320,192},{384,256},{4... | collective-permute-start | bytes 196616 | tf_op jit(solution)/shard_map/ppermute | solution.py:23
  35.6 3.4 %collective-permute-done.2.refs_0_ = bf16[128,1024]{1,0:T(8,128)(2,1)S(1)} collective-permute-done((bf16[128,1024]{1,0:T(8,128)(2,1)S(1)}, bf16[128,1024]{1,0:T(8,128)(2,1)S(1)}, u32[]{:S(2)}, u32[]{:S(2)}) %collective-permute-start.2) | collective-permute-done | bytes 262176 | tf_op jit(solution)/shard_map/ppermute | solution.py:28
  38.9 3.0 %pairs_second.1 = (bf16[1,2,128,1024]{3,2,1,0:T(8,128)(2,1)}, f32[2,128,128]{2,1,0:T(8,128)S(1)}, bf16[2,128,128]{2,1,0:T(8,128)(2,1)S(1)}, bf16[2,128,128]{2,1,0:T(8,128)(2,1)S(1)}) custom-call(s32[32]{0:T(128)S(1)} %copy-done.4, bf16[1,2,128,1024]{3,2,1,0:T(8,128)(2,1)S(1)} %copy-done, ...), custom_call_target="tpu_custom_call", output_to_operand_aliasing={{0}: (9, {})} | custom-call | flops 503316480 | bytes 1048576 | tf_op jit(solution)/shard_map/pairs_second/pallas_call | solution.py:228
  41.9 3.6 %collective-permute-start.5 = (bf16[2,128,128]{2,1,0:T(8,128)(2,1)S(1)}, bf16[2,128,128]{2,1,0:T(8,128)(2,1)S(1)}, u32[]{:S(2)}, u32[]{:S(2)}) collective-permute-start(bf16[2,128,128]{2,1,0:T(8,128)(2,1)S(1)} %get-tuple-element.19), channel_id=1, source_target_pairs={{0,960},{64,0},{128,64},{192,128},{256,192},{320,256},{384,320},{4... | collective-permute-start | bytes 196616 | tf_op jit(solution)/shard_map/ppermute | solution.py:23
  45.5 1.9 %collective-permute-start.6 = (bf16[2,128,128]{2,1,0:T(8,128)(2,1)S(1)}, bf16[2,128,128]{2,1,0:T(8,128)(2,1)S(1)}, u32[]{:S(2)}, u32[]{:S(2)}) collective-permute-start(bf16[2,128,128]{2,1,0:T(8,128)(2,1)S(1)} %get-tuple-element.20), channel_id=1, source_target_pairs={{0,896},{64,960},{128,0},{192,64},{256,128},{320,192},{384,256},{4... | collective-permute-start | bytes 196616 | tf_op jit(solution)/shard_map/ppermute | solution.py:23
  47.4 0.0 collective-permute-done.3.near0
  47.4 0.0 collective-permute-done.4.far0
  47.4 0.0 collective-permute-done.5.near1
  47.4 6.3 %collective-permute-done.6.far1 = bf16[2,128,128]{2,1,0:T(8,128)(2,1)S(1)} collective-permute-done((bf16[2,128,128]{2,1,0:T(8,128)(2,1)S(1)}, bf16[2,128,128]{2,1,0:T(8,128)(2,1)S(1)}, u32[]{:S(2)}, u32[]{:S(2)}) %collective-permute-start.6) | collective-permute-done | bytes 65568 | tf_op jit(solution)/shard_map/ppermute | solution.py:23
  53.7 0.7 %sums.1 = (bf16[1,2,128,128]{3,2,1,0:T(8,128)(2,1)}, bf16[1,2,128,128]{3,2,1,0:T(8,128)(2,1)}) custom-call(f32[2,128,128]{2,1,0:T(8,128)S(1)} %get-tuple-element.15.own0, bf16[2,128,128]{2,1,0:T(8,128)(2,1)S(1)} %collective-permute-done.3.near0, bf16[2,128,128]{2,1,0:T(8,128)(2,1)S(1)} %collective-permute-done.4.far0, ...), custom_call_target="tpu_custom_call" | custom-call | tf_op jit(solution)/shard_map/sums/pallas_call | solution.py:241
Async XLA Ops:
  0.6 22.1 %copy-start.3 = (f32[1,2,8,128]{3,2,1,0:T(8,128)S(1)}, f32[1,2,8,128]{3,2,1,0:T(8,128)}, u32[]{:S(2)}) copy-start(f32[1,2,8,128]{3,2,1,0:T(8,128)} %log_ref.5) | copy-start | bytes 24580
  0.6 22.1 %copy-start.4 = (s32[32]{0:T(128)S(1)}, s32[32]{0:T(128)}, u32[]{:S(2)}) copy-start(s32[32]{0:T(128)} %order_ref.5) | copy-start | bytes 388
  1.6 17.4 %collective-permute-start.1 = (bf16[2,2,128,128]{3,2,1,0:T(8,128)(2,1)S(1)}, bf16[2,2,128,128]{3,2,1,0:T(8,128)(2,1)S(1)}, u32[]{:S(2)}, u32[]{:S(2)}) collective-permute-start(bf16[2,2,128,128]{3,2,1,0:T(8,128)(2,1)S(1)} %pad_maximum_fusion.kv0), channel_id=1, source_target_pairs={{0,128},{64,192},{128,256},{192,320},{256,384},{320,448},{384,512}... | collective-permute-start | bytes 393224 | tf_op jit(solution)/shard_map/ppermute | solution.py:23
  16.5 6.3 %collective-permute-start = (bf16[2,2,128,128]{3,2,1,0:T(8,128)(2,1)S(1)}, bf16[2,2,128,128]{3,2,1,0:T(8,128)(2,1)S(1)}, u32[]{:S(2)}, u32[]{:S(2)}) collective-permute-start(bf16[2,2,128,128]{3,2,1,0:T(8,128)(2,1)S(1)} %pad_maximum_fusion.kv0), channel_id=1, source_target_pairs={{0,64},{64,128},{128,192},{192,256},{256,320},{320,384},{384,448},... | collective-permute-start | bytes 393224 | tf_op jit(solution)/shard_map/ppermute | solution.py:23
  22.8 1.0 %copy-start = (bf16[1,2,128,1024]{3,2,1,0:T(8,128)(2,1)S(1)}, bf16[1,2,128,1024]{3,2,1,0:T(8,128)(2,1)}, u32[]{:S(2)}) copy-start(bf16[1,2,128,1024]{3,2,1,0:T(8,128)(2,1)} %q_ref.5) | copy-start | bytes 1572868
  23.8 1.0 %copy-start.1 = (bf16[1,2,128,1024]{3,2,1,0:T(8,128)(2,1)S(1)}, bf16[1,2,128,1024]{3,2,1,0:T(8,128)(2,1)}, u32[]{:S(2)}) copy-start(bf16[1,2,128,1024]{3,2,1,0:T(8,128)(2,1)} %g_ref.5) | copy-start | bytes 1572868
  24.9 1.0 %copy-start.2 = (bf16[1,2,128,1024]{3,2,1,0:T(8,128)(2,1)S(1)}, bf16[1,2,128,1024]{3,2,1,0:T(8,128)(2,1)}, u32[]{:S(2)}) copy-start(bf16[1,2,128,1024]{3,2,1,0:T(8,128)(2,1)} %o_ref.5) | copy-start | bytes 1572868
  27.9 11.0 %collective-permute-start.2 = (bf16[128,1024]{1,0:T(8,128)(2,1)S(1)}, bf16[128,1024]{1,0:T(8,128)(2,1)S(1)}, u32[]{:S(2)}, u32[]{:S(2)}) collective-permute-start(bf16[128,1024]{1,0:T(8,128)(2,1)S(1)} %query_first.1.refs_0_), channel_id=1, source_target_pairs={{1,0},{2,1},{3,2},{4,3},{5,4},{6,5},{7,6},{8,7},{9,8},{10,9},{11,1... | collective-permute-start | bytes 786440 | tf_op jit(solution)/shard_map/ppermute | solution.py:28
  31.7 15.7 %collective-permute-start.3 = (bf16[2,128,128]{2,1,0:T(8,128)(2,1)S(1)}, bf16[2,128,128]{2,1,0:T(8,128)(2,1)S(1)}, u32[]{:S(2)}, u32[]{:S(2)}) collective-permute-start(bf16[2,128,128]{2,1,0:T(8,128)(2,1)S(1)} %get-tuple-element.16), channel_id=1, source_target_pairs={{0,960},{64,0},{128,64},{192,128},{256,192},{320,256},{384,320},{4... | collective-permute-start | bytes 196616 | tf_op jit(solution)/shard_map/ppermute | solution.py:23
  33.6 13.8 %collective-permute-start.4 = (bf16[2,128,128]{2,1,0:T(8,128)(2,1)S(1)}, bf16[2,128,128]{2,1,0:T(8,128)(2,1)S(1)}, u32[]{:S(2)}, u32[]{:S(2)}) collective-permute-start(bf16[2,128,128]{2,1,0:T(8,128)(2,1)S(1)} %get-tuple-element.17), channel_id=1, source_target_pairs={{0,896},{64,960},{128,0},{192,64},{256,128},{320,192},{384,256},{4... | collective-permute-start | bytes 196616 | tf_op jit(solution)/shard_map/ppermute | solution.py:23
  41.9 5.5 %collective-permute-start.5 = (bf16[2,128,128]{2,1,0:T(8,128)(2,1)S(1)}, bf16[2,128,128]{2,1,0:T(8,128)(2,1)S(1)}, u32[]{:S(2)}, u32[]{:S(2)}) collective-permute-start(bf16[2,128,128]{2,1,0:T(8,128)(2,1)S(1)} %get-tuple-element.19), channel_id=1, source_target_pairs={{0,960},{64,0},{128,64},{192,128},{256,192},{320,256},{384,320},{4... | collective-permute-start | bytes 196616 | tf_op jit(solution)/shard_map/ppermute | solution.py:23
  45.5 8.3 %collective-permute-start.6 = (bf16[2,128,128]{2,1,0:T(8,128)(2,1)S(1)}, bf16[2,128,128]{2,1,0:T(8,128)(2,1)S(1)}, u32[]{:S(2)}, u32[]{:S(2)}) collective-permute-start(bf16[2,128,128]{2,1,0:T(8,128)(2,1)S(1)} %get-tuple-element.20), channel_id=1, source_target_pairs={{0,896},{64,960},{128,0},{192,64},{256,128},{320,192},{384,256},{4... | collective-permute-start | bytes 196616 | tf_op jit(solution)/shard_map/ppermute | solution.py:23

commit v2 on v1

v2 whole, which is shorter than its diff:
```python
import functools
import math

import jax
import jax.numpy as jnp
from jax import lax
from jax.experimental import pallas as pl
from jax.experimental.pallas import tpu as pltpu
from jax.sharding import PartitionSpec as P

WINDOW = 3
PAIR = 2
NT = (((1,), (1,)), ((), ()))
NN = (((1,), (0,)), ((), ()))
LOW = jnp.bfloat16
WIDE = jnp.float32


def dot(a, b, dims=NN):
    return lax.dot_general(a, b, dims, preferred_element_type=WIDE)


def ring(value, steps):
    count = lax.axis_size("ctx")
    return lax.ppermute(value, "ctx", [(i, (i + steps) % count) for i in range(count)])


def down(value):
    count = lax.axis_size("section")
    return lax.ppermute(value, "section", [(i, i - 1) for i in range(1, count)])


def mask_bias(order_ref, rows, offsets):
    half = rows // 2
    slots = order_ref.shape[0]
    own = lax.axis_index("ctx")
    lane = lax.broadcasted_iota(jnp.int32, (half, rows), 1)
    sub = lax.broadcasted_iota(jnp.int32, (half, rows), 0)
    query = jnp.where(
        lane < half,
        order_ref[2 * own] * half + lane,
        order_ref[2 * own + 1] * half + lane - half,
    )
    blocks = []
    for offset in offsets:
        for part in range(2):
            slot = lax.rem(2 * (own - offset) + part + slots, slots)
            blocks.append(jnp.where(order_ref[slot] * half + sub <= query, 0.0, -1e30))
    bias = jnp.concatenate(blocks, axis=0)
    return jnp.concatenate([bias] * PAIR, axis=1)


def stacked(block, size):
    return jnp.concatenate(
        [block[:, i * size : (i + 1) * size] for i in range(block.shape[1] // size)], axis=0
    )


def head_rows(table, first):
    return jnp.concatenate([table[first + i : first + i + 1] for i in range(PAIR)], axis=1)


def dots_of_rows(upstream, out, size):
    product = upstream.astype(WIDE) * out.astype(WIDE)
    high = product.astype(LOW)
    low = (product - high.astype(WIDE)).astype(LOW)
    shape = (8, product.shape[1])
    pick = (lax.broadcasted_iota(jnp.int32, shape, 1) // size == lax.broadcasted_iota(jnp.int32, shape, 0)).astype(WIDE).astype(LOW)
    return dot(pick, high, NT) + dot(pick, low, NT)


def turned(part, rows):
    count = part.shape[1] // rows
    return jnp.concatenate([part[:, i * rows : (i + 1) * rows].T for i in range(count)], axis=1)


def joined(refs, micro, which):
    return jnp.concatenate([ref[micro, which] for ref in refs], axis=0)


def own_kernel(factor, order_ref, log_ref, kv_ref, q_hbm, g_hbm, o_hbm, qs_ref, gs_ref, rd_ref, dqt_ref, own_ref, q_v, g_v, o_v, sems):
    copies = [
        pltpu.make_async_copy(source.at[0, 0], target, sems.at[i])
        for i, (source, target) in enumerate(((g_hbm, g_v), (o_hbm, o_v), (q_hbm, q_v)))
    ]
    for copy in copies:
        copy.start()
    rows, size = kv_ref.shape[2], kv_ref.shape[3]
    keys, values = kv_ref[0, 0], kv_ref[0, 1]
    keys_t = keys.T
    bias = mask_bias(order_ref, rows, (0,))
    log_rows = log_ref[0, 0]
    copies[0].wait()
    copies[1].wait()
    grad = stacked(g_v[...], size)
    gs_ref[...] = grad
    dot_rows = dots_of_rows(g_v[...], o_v[...], size)
    rd_ref[...] = dot_rows
    copies[2].wait()
    query = stacked(q_v[...], size)
    qs_ref[...] = query
    step = PAIR * rows
    key_sum = value_sum = 0.0
    for first in range(0, query.shape[0] // rows, PAIR):
        cut = slice(first * rows, first * rows + step)
        probs = jnp.exp(dot(keys, query[cut], NT) * factor + (bias - head_rows(log_rows, first)))
        grad_scores = (probs * (dot(values, grad[cut], NT) - head_rows(dot_rows, first))).astype(LOW)
        dqt_ref[:, cut] = dot(keys_t, grad_scores)
        key_sum += dot(grad_scores, query[cut])
        value_sum += dot(probs.astype(LOW), grad[cut])
    own_ref[0] = key_sum * factor
    own_ref[1] = value_sum


def query_kernel(factor, start, order_ref, log_ref, kv1, kv2, qs_ref, gs_ref, rd_ref, dqt_ref, dq_ref):
    rows, size = kv1.shape[2], kv1.shape[3]
    keys, values = joined((kv1, kv2), 0, 0), joined((kv1, kv2), 0, 1)
    keys_t = keys.T
    bias = mask_bias(order_ref, rows, (1, 2))
    log_rows, dot_rows = log_ref[0, 0], rd_ref[...]
    step = PAIR * rows
    for first in range(start, start + dq_ref.shape[1] // size, PAIR):
        cut = slice(first * rows, first * rows + step)
        probs = jnp.exp(dot(keys, qs_ref[cut], NT) * factor + (bias - head_rows(log_rows, first)))
        grad_scores = (probs * (dot(values, gs_ref[cut], NT) - head_rows(dot_rows, first))).astype(LOW)
        part = (dot(keys_t, grad_scores) + dqt_ref[:, cut]) * factor
        at = (first - start) * size
        dq_ref[:, at : at + PAIR * size] = turned(part, rows).astype(LOW)


def middle_kernel(
    factor, order_ref, log_ref, kv0, kv1, kv2, qs_ref, gs_ref, rd_ref, dqa_ref, dqb_ref, q_hbm, g_hbm, o_hbm,
    gq_hbm, near_ref, far_ref, qs1_ref, g1_ref, o1_ref, probs_ref, q_v, sems,
):
    half = dqa_ref.shape[1]
    copies = [
        pltpu.make_async_copy(q_hbm.at[0, 1], q_v, sems.at[0]),
        pltpu.make_async_copy(g_hbm.at[0, 1], g1_ref, sems.at[1]),
        pltpu.make_async_copy(o_hbm.at[0, 1], o1_ref, sems.at[2]),
        pltpu.make_async_copy(dqa_ref, gq_hbm.at[0, 0, :, pl.ds(0, half)], sems.at[3]),
        pltpu.make_async_copy(dqb_ref, gq_hbm.at[0, 0, :, pl.ds(half, half)], sems.at[4]),
    ]
    for copy in copies:
        copy.start()
    rows, size = kv1.shape[2], kv1.shape[3]
    heads = qs_ref.shape[0] // rows
    keys, values = joined((kv1, kv2), 0, 0), joined((kv1, kv2), 0, 1)
    bias = mask_bias(order_ref, rows, (0, 1, 2))
    log_rows, dot_rows = log_ref[0, 0], rd_ref[...]
    step = PAIR * rows
    key_sum = value_sum = 0.0
    for first in range(0, heads, PAIR):
        cut = slice(first * rows, first * rows + step)
        query, grad = qs_ref[cut], gs_ref[cut]
        probs = jnp.exp(dot(keys, query, NT) * factor + (bias[rows:] - head_rows(log_rows, first)))
        grad_scores = (probs * (dot(values, grad, NT) - head_rows(dot_rows, first))).astype(LOW)
        key_sum += dot(grad_scores, query)
        value_sum += dot(probs.astype(LOW), grad)
    key_sum = key_sum * factor
    for i, ref in enumerate((near_ref, far_ref)):
        ref[0] = key_sum[i * rows : (i + 1) * rows].astype(LOW)
        ref[1] = value_sum[i * rows : (i + 1) * rows].astype(LOW)
    copies[0].wait()
    query = stacked(q_v[...], size)
    qs1_ref[...] = query
    keys = joined((kv0, kv1, kv2), 1, 0)
    log_rows = log_ref[0, 1]
    for first in range(0, heads, PAIR):
        cut = slice(first * rows, first * rows + step)
        scores = dot(keys, query[cut], NT)
        probs_ref[:, cut] = jnp.exp(scores * factor + (bias - head_rows(log_rows, first)))
    for copy in copies[1:]:
        copy.wait()


def second_kernel(factor, kv0, kv1, kv2, qs_ref, g_ref, o_ref, probs_ref, r_ref, dq_ref, sum_ref):
    rows, size = kv1.shape[2], kv1.shape[3]
    keys, values = joined((kv0, kv1, kv2), 1, 0), joined((kv0, kv1, kv2), 1, 1)
    keys_t = keys.T
    width = r_ref.shape[1]
    upstream = (g_ref[:, :width].astype(WIDE) + r_ref[...].astype(WIDE)).astype(LOW)
    dot_rows = dots_of_rows(upstream, o_ref[:, :width], size)
    upstream = stacked(upstream, size)
    step = PAIR * rows
    key_sum = value_sum = 0.0
    for first in range(0, width // size, PAIR):
        cut = slice(first * rows, first * rows + step)
        probs, grad = probs_ref[:, cut], upstream[cut]
        grad_scores = (probs * (dot(values, grad, NT) - head_rows(dot_rows, first))).astype(LOW)
        key_sum += dot(grad_scores, qs_ref[cut])
        value_sum += dot(probs.astype(LOW), grad)
        part = dot(keys_t, grad_scores) * factor
        dq_ref[:, first * size : (first + PAIR) * size] = turned(part, rows).astype(LOW)
    sum_ref[0] = key_sum
    sum_ref[1] = value_sum


def third_kernel(factor, kv0, kv1, kv2, qs_ref, g_ref, o_ref, probs_ref, sum_ref, r_ref, near_ref, far_ref, up_ref, gs_ref):
    rows, size = kv1.shape[2], kv1.shape[3]
    values = joined((kv0, kv1, kv2), 1, 1)
    width = r_ref.shape[1]
    upstream = (g_ref[:, width:].astype(WIDE) + r_ref[...].astype(WIDE)).astype(LOW)
    dot_rows = dots_of_rows(upstream, o_ref[:, width:], size)
    upstream = stacked(upstream, size)
    up_ref[...] = upstream
    step = PAIR * rows
    base = width // size * rows
    key_sum, value_sum = sum_ref[0, rows:], sum_ref[1, rows:]
    for first in range(0, width // size, PAIR):
        cut = slice(first * rows, first * rows + step)
        far = slice(base + first * rows, base + first * rows + step)
        probs, grad = probs_ref[:, far], upstream[cut]
        grad_scores = (probs * (dot(values, grad, NT) - head_rows(dot_rows, first))).astype(LOW)
        gs_ref[:, cut] = grad_scores
        key_sum += dot(grad_scores[rows:], qs_ref[far])
        value_sum += dot(probs[rows:].astype(LOW), grad)
    key_sum = key_sum * factor
    for i, ref in enumerate((near_ref, far_ref)):
        ref[0] = key_sum[i * rows : (i + 1) * rows].astype(LOW)
        ref[1] = value_sum[i * rows : (i + 1) * rows].astype(LOW)


def fourth_kernel(factor, kv0, kv1, kv2, qs_ref, probs_ref, sum_ref, up_ref, gs_ref, dqa_ref, _, own_ref, gq_hbm, dqb_v, sems):
    rows = kv1.shape[2]
    half = dqa_ref.shape[1]
    first_copy = pltpu.make_async_copy(dqa_ref, gq_hbm.at[0, 1, :, pl.ds(0, half)], sems.at[0])
    first_copy.start()
    keys_t = joined((kv0, kv1, kv2), 1, 0).T
    base = up_ref.shape[0]
    dqb_v[...] = turned(dot(keys_t, gs_ref[...]) * factor, rows).astype(LOW)
    last_copy = pltpu.make_async_copy(dqb_v, gq_hbm.at[0, 1, :, pl.ds(half, half)], sems.at[1])
    last_copy.start()
    own_ref[0] = (sum_ref[0, :rows] + dot(gs_ref[:rows], qs_ref[base:])) * factor
    own_ref[1] = sum_ref[1, :rows] + dot(probs_ref[:rows, base:].astype(LOW), up_ref[...])
    first_copy.wait()
    last_copy.wait()


def sum_kernel(own0, near0, far0, own1, near1, far1, gk_ref, gv_ref):
    for micro, (own, near, far) in enumerate(((own0, near0, far0), (own1, near1, far1))):
        for which, ref in ((0, gk_ref), (1, gv_ref)):
            total = own[which] + near[which].astype(WIDE) + far[which].astype(WIDE)
            ref[0, micro] = total.astype(LOW)


VM = pl.BlockSpec(memory_space=pltpu.VMEM)
SM = pl.BlockSpec(memory_space=pltpu.SMEM)
HB = pl.BlockSpec(memory_space=pltpu.HBM)


def shards(query_in, key_in, value_in, forward_out, log_sum, grad_out, block_order):
    rows, width = query_in.shape[2:]
    size = key_in.shape[3]
    heads = width // size
    half = width // 2
    near_rows = WINDOW * rows
    factor = 1.0 / math.sqrt(size)

    def low(*shape):
        return jax.ShapeDtypeStruct(shape, LOW)

    def wide(*shape):
        return jax.ShapeDtypeStruct(shape, WIDE)

    def call(body, name, ins, outs, in_specs=None, out_specs=None, scratch=(), share=1.0, **more):
        flops = int(2 * near_rows * heads * rows * size * share)
        return pl.pallas_call(
            body,
            in_specs=in_specs or [VM] * len(ins),
            out_specs=out_specs or [VM] * len(outs),
            out_shape=outs,
            scratch_shapes=list(scratch),
            compiler_params=pltpu.CompilerParams(vmem_limit_bytes=40 * 2**20),
            cost_estimate=pl.CostEstimate(flops=flops, bytes_accessed=2**20, transcendentals=near_rows * heads * rows),
            name=name,
            **more,
        )(*ins)

    dma = pltpu.SemaphoreType.DMA
    kv0 = jnp.stack([key_in[0], value_in[0]], axis=1)
    kv2, kv1 = ring(kv0, 2), ring(kv0, 1)
    pair = (2, rows, size)

    qs, gs, rd, dqt, own0 = call(
        functools.partial(own_kernel, factor),
        "own_terms",
        (block_order, log_sum, kv0, query_in, grad_out, forward_out),
        [low(heads * rows, size), low(heads * rows, size), wide(8, rows), wide(size, heads * rows), wide(*pair)],
        in_specs=[SM, VM, VM, HB, HB, HB],
        scratch=[pltpu.VMEM((rows, width), LOW)] * 3 + [dma((3,))],
        share=2,
    )
    parts, received = [], []
    for start in (0, heads // 2):
        (part,) = call(
            functools.partial(query_kernel, factor, start),
            "query_part",
            (block_order, log_sum, kv1, kv2, qs, gs, rd, dqt),
            [low(rows, half)],
            in_specs=[SM] + [VM] * 7,
        )
        parts.append(part)
        received.append(down(part))

    grad_query, near0, far0, qs1, g1, o1, probs = call(
        functools.partial(middle_kernel, factor),
        "middle_terms",
        (block_order, log_sum, kv0, kv1, kv2, qs, gs, rd, *parts, query_in, grad_out, forward_out),
        [low(*query_in.shape), low(*pair), low(*pair), low(heads * rows, size), low(rows, width), low(rows, width), wide(near_rows, heads * rows)],
        in_specs=[SM] + [VM] * 9 + [HB] * 3,
        out_specs=[HB] + [VM] * 6,
        scratch=[pltpu.VMEM((rows, width), LOW), dma((5,))],
        share=4,
    )
    far0, near0 = ring(far0, -2), ring(near0, -1)

    dqa, sums = call(
        functools.partial(second_kernel, factor),
        "second_all",
        (kv0, kv1, kv2, qs1, g1, o1, probs, received[0]),
        [low(rows, half), wide(2, near_rows, size)],
        share=2,
    )
    near1, far1, up, grad_scores = call(
        functools.partial(third_kernel, factor),
        "second_far",
        (kv0, kv1, kv2, qs1, g1, o1, probs, sums, received[1]),
        [low(*pair), low(*pair), low(heads // 2 * rows, size), low(near_rows, heads // 2 * rows)],
    )
    far1, near1 = ring(far1, -2), ring(near1, -1)
    own1, grad_query = call(
        functools.partial(fourth_kernel, factor),
        "second_own",
        (kv0, kv1, kv2, qs1, probs, sums, up, grad_scores, dqa, grad_query),
        [wide(*pair), low(*query_in.shape)],
        in_specs=[VM] * 9 + [HB],
        out_specs=[VM, HB],
        scratch=[pltpu.VMEM((rows, half), LOW), dma((2,))],
        input_output_aliases={9: 1},
    )
    grad_key, grad_value = call(
        sum_kernel,
        "sums",
        (own0, near0, far0, own1, near1, far1),
        [low(1, 2, rows, size)] * 2,
        share=0.01,
    )
    return (grad_query, grad_key, grad_value)


def solution(mesh):
    split = P("section", None, "ctx", None)
    return jax.shard_map(
        shards,
        mesh=mesh,
        in_specs=(split, split, split, split, P("section", None, None, "ctx"), split, P()),
        out_specs=(split, split, split),
        check_vma=False,
    )
```

time: 54.9 us -> 55 us (level)
  the two profiles are of different devices: /device:TPU:14 before, /device:TPU:40 now
where the time goes in v2:
time: 55 us; the launch traced here: 54.4 us
  starting transfers between devices  35.3 us (64%)
  Pallas kernels  10.2 us (19%)
  local copies, waits for them, and re-layouts  4.48 us (8%)
  waiting for transfers between devices  2.77 us (5%)
  other arithmetic  0.89 us (2%)
  between operations  0.84 us (2%)
    ppermute x6, starting transfers between devices, ring(): lax.ppermute(value, 'ctx', [(i, (i + steps) % count) for i in range(count)])  24.9 us
    ppermute x2, starting transfers between devices, down(): return lax.ppermute(value, 'section', [(i, i - 1) for i in range(1, count)])  10.4 us
    pallas_call x8, Pallas kernels, call(): pl.pallas_call(body, in_specs=in_specs or [VM] * len(ins), out_specs=out_...  10.2 us
    unnamed x14, local copies, waits for them, and re-layouts  4.48 us
    ppermute x6, waiting for transfers between devices, ring(): lax.ppermute(value, 'ctx', [(i, (i + steps) % count) for i in range(count)])  2.76 us
  transfers between devices with their start and end apart: 8, of which 1 were waited for; matrix products, arithmetic and copies ran while one was open for 0% of the time, Pallas kernels for 15%

profile of v2, /device:TPU:40, one launch (start us, length us, event | category | flops | bytes accessed | tf_op | source)
XLA Modules:
  0.0 54.4 jit_solution(1339934097942791326)
XLA Ops:
  0.6 0.9 %pad_maximum_fusion.kv_ref.kv0 = bf16[2,2,128,128]{3,2,1,0:T(8,128)(2,1)S(1)} fusion(bf16[2,1,128,128]{3,2,1,0:T(8,128)(2,1)} %bitcast.2, bf16[2,1,128,128]{3,2,1,0:T(8,128)(2,1)} %bitcast.3), kind=kLoop, calls=%fused_computation | loop fusion | flops 65536 | bytes 262144 | tf_op jit(solution)/shard_map/stack | solution.py:280
  1.5 4.2 %collective-permute-start.1 = (bf16[2,2,128,128]{3,2,1,0:T(8,128)(2,1)S(1)}, bf16[2,2,128,128]{3,2,1,0:T(8,128)(2,1)S(1)}, u32[]{:S(2)}, u32[]{:S(2)}) collective-permute-start(bf16[2,2,128,128]{3,2,1,0:T(8,128)(2,1)S(1)} %pad_maximum_fusion.kv_ref.kv0), channel_id=1, source_target_pairs={{0,128},{64,192},{128,256},{192,320},{256,384},{320,448},{384,512}... | collective-permute-start | bytes 393224 | tf_op jit(solution)/shard_map/ppermute | solution.py:25
  5.7 1.9 %collective-permute-start = (bf16[2,2,128,128]{3,2,1,0:T(8,128)(2,1)S(1)}, bf16[2,2,128,128]{3,2,1,0:T(8,128)(2,1)S(1)}, u32[]{:S(2)}, u32[]{:S(2)}) collective-permute-start(bf16[2,2,128,128]{3,2,1,0:T(8,128)(2,1)S(1)} %pad_maximum_fusion.kv_ref.kv0), channel_id=1, source_target_pairs={{0,64},{64,128},{128,192},{192,256},{256,320},{320,384},{384,448},... | collective-permute-start | bytes 393224 | tf_op jit(solution)/shard_map/ppermute | solution.py:25
  7.6 0.0 copy-start
  7.7 1.0 %copy-done = bf16[1,2,128,1024]{3,2,1,0:T(8,128)(2,1)S(1)} copy-done((bf16[1,2,128,1024]{3,2,1,0:T(8,128)(2,1)S(1)}, bf16[1,2,128,1024]{3,2,1,0:T(8,128)(2,1)}, u32[]{:S(2)}) %copy-start) | copy-done | bytes 524312
  8.7 1.0 %copy-done.1 = bf16[1,2,128,1024]{3,2,1,0:T(8,128)(2,1)S(1)} copy-done((bf16[1,2,128,1024]{3,2,1,0:T(8,128)(2,1)S(1)}, bf16[1,2,128,1024]{3,2,1,0:T(8,128)(2,1)}, u32[]{:S(2)}) %copy-start.1) | copy-done | bytes 524312
  9.7 1.0 %copy-done.3 = bf16[1,2,128,1024]{3,2,1,0:T(8,128)(2,1)S(1)} copy-done((bf16[1,2,128,1024]{3,2,1,0:T(8,128)(2,1)S(1)}, bf16[1,2,128,1024]{3,2,1,0:T(8,128)(2,1)}, u32[]{:S(2)}) %copy-start.3) | copy-done | bytes 524312
  10.8 0.7 %copy-done.5 = f32[1,2,8,128]{3,2,1,0:T(8,128)S(1)} copy-done((f32[1,2,8,128]{3,2,1,0:T(8,128)S(1)}, f32[1,2,8,128]{3,2,1,0:T(8,128)}, u32[]{:S(2)}) %copy-start.5) | copy-done | bytes 8216
  11.5 0.7 %copy-done.6 = s32[32]{0:T(128)S(1)} copy-done((s32[32]{0:T(128)S(1)}, s32[32]{0:T(128)}, u32[]{:S(2)}) %copy-start.6) | copy-done | bytes 152
  12.1 2.3 %own_terms.1 = (bf16[1024,128]{1,0:T(8,128)(2,1)S(1)}, bf16[1024,128]{1,0:T(8,128)(2,1)S(1)}, f32[8,128]{1,0:T(8,128)S(1)}, f32[128,1024]{1,0:T(8,128)S(1)}, f32[2,128,128]{2,1,0:T(8,128)S(1)}) custom-call(s32[32]{0:T(128)S(1)} %copy-done.6, f32[1,2,8,128]{3,2,1,0:T(8,128)S(1)} %copy-done.5, bf16[2,2,128,128]{3,2,1,0:T(8,128)(2,1)S(1)} %pad_maximum_fusion.kv_ref.kv0, ...), custom_call_target="tpu_custom_call" | custom-call | flops 201326592 | bytes 1048576 | tf_op jit(solution)/shard_map/own_terms/pallas_call | solution.py:267
  14.4 0.0 copy-start.2
  14.4 0.0 copy-start.4
  14.4 0.0 collective-permute-done.1.kv2
  14.5 0.0 collective-permute-done.kv1
  14.5 1.2 %query_part.2.dqa_ref = bf16[128,512]{1,0:T(8,128)(2,1)S(1)} custom-call(s32[32]{0:T(128)S(1)} %copy-done.6, f32[1,2,8,128]{3,2,1,0:T(8,128)S(1)} %copy-done.5, bf16[2,2,128,128]{3,2,1,0:T(8,128)(2,1)S(1)} %collective-permute-done.kv1, bf16[2,2,128,128]{3,2,1,0:T(8,128)(2,1)S(1)} %collective-permute-done.1.kv2, ...), custom_call_target="tpu_custom_call" | custom-call | flops 100663296 | bytes 1048576 | tf_op jit(solution)/shard_map/query_part/pallas_call | solution.py:267
  15.7 2.2 %collective-permute-start.2 = (bf16[128,512]{1,0:T(8,128)(2,1)S(1)}, bf16[128,512]{1,0:T(8,128)(2,1)S(1)}, u32[]{:S(2)}, u32[]{:S(2)}) collective-permute-start(bf16[128,512]{1,0:T(8,128)(2,1)S(1)} %query_part.2.dqa_ref), channel_id=1, source_target_pairs={{1,0},{2,1},{3,2},{4,3},{5,4},{6,5},{7,6},{8,7},{9,8},{10,9},{11,1... | collective-permute-start | bytes 393224 | tf_op jit(solution)/shard_map/ppermute | solution.py:30
  18.0 1.2 %query_part.3.dqb_ref = bf16[128,512]{1,0:T(8,128)(2,1)S(1)} custom-call(s32[32]{0:T(128)S(1)} %copy-done.6, f32[1,2,8,128]{3,2,1,0:T(8,128)S(1)} %copy-done.5, bf16[2,2,128,128]{3,2,1,0:T(8,128)(2,1)S(1)} %collective-permute-done.kv1, bf16[2,2,128,128]{3,2,1,0:T(8,128)(2,1)S(1)} %collective-permute-done.1.kv2, ...), custom_call_target="tpu_custom_call" | custom-call | flops 100663296 | bytes 1048576 | tf_op jit(solution)/shard_map/query_part/pallas_call | solution.py:267
  19.2 8.1 %collective-permute-start.3 = (bf16[128,512]{1,0:T(8,128)(2,1)S(1)}, bf16[128,512]{1,0:T(8,128)(2,1)S(1)}, u32[]{:S(2)}, u32[]{:S(2)}) collective-permute-start(bf16[128,512]{1,0:T(8,128)(2,1)S(1)} %query_part.3.dqb_ref), channel_id=1, source_target_pairs={{1,0},{2,1},{3,2},{4,3},{5,4},{6,5},{7,6},{8,7},{9,8},{10,9},{11,1... | collective-permute-start | bytes 393224 | tf_op jit(solution)/shard_map/ppermute | solution.py:30
  27.4 2.0 %middle_terms.1 = (bf16[1,2,128,1024]{3,2,1,0:T(8,128)(2,1)}, bf16[2,128,128]{2,1,0:T(8,128)(2,1)S(1)}, bf16[2,128,128]{2,1,0:T(8,128)(2,1)S(1)}, bf16[1024,128]...) custom-call(s32[32]{0:T(128)S(1)} %copy-done.6, ...), custom_call_target="tpu_custom_call" | custom-call | flops 402653184 | bytes 1048576 | tf_op jit(solution)/shard_map/middle_terms/pallas_call | solution.py:267
  29.4 1.9 %collective-permute-start.4 = (bf16[2,128,128]{2,1,0:T(8,128)(2,1)S(1)}, bf16[2,128,128]{2,1,0:T(8,128)(2,1)S(1)}, u32[]{:S(2)}, u32[]{:S(2)}) collective-permute-start(bf16[2,128,128]{2,1,0:T(8,128)(2,1)S(1)} %get-tuple-element.40), channel_id=1, source_target_pairs={{0,960},{64,0},{128,64},{192,128},{256,192},{320,256},{384,320},{4... | collective-permute-start | bytes 196616 | tf_op jit(solution)/shard_map/ppermute | solution.py:25
  31.3 11.0 %collective-permute-start.5 = (bf16[2,128,128]{2,1,0:T(8,128)(2,1)S(1)}, bf16[2,128,128]{2,1,0:T(8,128)(2,1)S(1)}, u32[]{:S(2)}, u32[]{:S(2)}) collective-permute-start(bf16[2,128,128]{2,1,0:T(8,128)(2,1)S(1)} %get-tuple-element.41), channel_id=1, source_target_pairs={{0,896},{64,960},{128,0},{192,64},{256,128},{320,192},{384,256},{4... | collective-permute-start | bytes 196616 | tf_op jit(solution)/shard_map/ppermute | solution.py:25
  42.4 0.0 collective-permute-done.2.r_ref
  42.4 0.9 %second_all.1 = (bf16[128,512]{1,0:T(8,128)(2,1)S(1)}, f32[2,384,128]{2,1,0:T(8,128)S(1)}) custom-call(bf16[2,2,128,128]{3,2,1,0:T(8,128)(2,1)S(1)} %pad_maximum_fusion.kv_ref.kv0, bf16[2,2,128,128]{3,2,1,0:T(8,128)(2,1)S(1)} %collective-permute-done.kv1, bf16[2,2,128,128]{3,2,1,0:T(8,128)(2,1)S(1)} %collective-permute-done.1.kv2, ...), custom_call_target="tpu_custom_call" | custom-call | flops 201326592 | bytes 1048576 | tf_op jit(solution)/shard_map/second_all/pallas_call | solution.py:267
  43.3 0.0 collective-permute-done.3.r_ref
  43.3 0.8 %second_far.1 = (bf16[2,128,128]{2,1,0:T(8,128)(2,1)S(1)}, bf16[2,128,128]{2,1,0:T(8,128)(2,1)S(1)}, bf16[512,128]{1,0:T(8,128)(2,1)S(1)}, bf16[384,512]{1,0:T(8,128)(2,1)S(1)}) custom-call(bf16[2,2,128,128]{3,2,1,0:T(8,128)(2,1)S(1)} %pad_maximum_fusion.kv_ref.kv0, bf16[2,2,128,128]{3,2,1,0:T(8,128)(2,1)S(1)} %collective-permute-done.kv1, ...), custom_call_target="tpu_custom_call" | custom-call | flops 100663296 | bytes 1048576 | tf_op jit(solution)/shard_map/second_far/pallas_call | solution.py:267
  44.1 2.6 %collective-permute-start.6 = (bf16[2,128,128]{2,1,0:T(8,128)(2,1)S(1)}, bf16[2,128,128]{2,1,0:T(8,128)(2,1)S(1)}, u32[]{:S(2)}, u32[]{:S(2)}) collective-permute-start(bf16[2,128,128]{2,1,0:T(8,128)(2,1)S(1)} %get-tuple-element.43), channel_id=1, source_target_pairs={{0,960},{64,0},{128,64},{192,128},{256,192},{320,256},{384,320},{4... | collective-permute-start | bytes 196616 | tf_op jit(solution)/shard_map/ppermute | solution.py:25
  46.7 3.3 %collective-permute-start.7 = (bf16[2,128,128]{2,1,0:T(8,128)(2,1)S(1)}, bf16[2,128,128]{2,1,0:T(8,128)(2,1)S(1)}, u32[]{:S(2)}, u32[]{:S(2)}) collective-permute-start(bf16[2,128,128]{2,1,0:T(8,128)(2,1)S(1)} %get-tuple-element.44), channel_id=1, source_target_pairs={{0,896},{64,960},{128,0},{192,64},{256,128},{320,192},{384,256},{4... | collective-permute-start | bytes 196616 | tf_op jit(solution)/shard_map/ppermute | solution.py:25
  49.9 1.0 %second_own.1 = (f32[2,128,128]{2,1,0:T(8,128)S(1)}, bf16[1,2,128,1024]{3,2,1,0:T(8,128)(2,1)}) custom-call(bf16[2,2,128,128]{3,2,1,0:T(8,128)(2,1)S(1)} %pad_maximum_fusion.kv_ref.kv0, bf16[2,2,128,128]{3,2,1,0:T(8,128)(2,1)S(1)} %collective-permute-done.kv1, ...), custom_call_target="tpu_custom_call", output_to_operand_aliasing={{1}: (9, {})} | custom-call | flops 100663296 | bytes 1048576 | tf_op jit(solution)/shard_map/second_own/pallas_call | solution.py:267
  51.0 0.0 collective-permute-done.4.near0
  51.0 0.0 collective-permute-done.6.near1
  51.0 2.8 %collective-permute-done.7.far1 = bf16[2,128,128]{2,1,0:T(8,128)(2,1)S(1)} collective-permute-done((bf16[2,128,128]{2,1,0:T(8,128)(2,1)S(1)}, bf16[2,128,128]{2,1,0:T(8,128)(2,1)S(1)}, u32[]{:S(2)}, u32[]{:S(2)}) %collective-permute-start.7) | collective-permute-done | bytes 65568 | tf_op jit(solution)/shard_map/ppermute | solution.py:25
  53.7 0.7 %sums.1 = (bf16[1,2,128,128]{3,2,1,0:T(8,128)(2,1)}, bf16[1,2,128,128]{3,2,1,0:T(8,128)(2,1)}) custom-call(f32[2,128,128]{2,1,0:T(8,128)S(1)} %get-tuple-element.39.own0, bf16[2,128,128]{2,1,0:T(8,128)(2,1)S(1)} %collective-permute-done.4.near0, bf16[2,128,128]{2,1,0:T(8,128)(2,1)S(1)} %collective-permute-done.5.far0, ...), custom_call_target="tpu_custom_call" | custom-call | flops 1006632 | bytes 1048576 | tf_op jit(solution)/shard_map/sums/pallas_call | solution.py:267
  (7 shorter events, 0.0 us)
Async XLA Ops:
  1.5 12.9 %collective-permute-start.1 = (bf16[2,2,128,128]{3,2,1,0:T(8,128)(2,1)S(1)}, bf16[2,2,128,128]{3,2,1,0:T(8,128)(2,1)S(1)}, u32[]{:S(2)}, u32[]{:S(2)}) collective-permute-start(bf16[2,2,128,128]{3,2,1,0:T(8,128)(2,1)S(1)} %pad_maximum_fusion.kv_ref.kv0), channel_id=1, source_target_pairs={{0,128},{64,192},{128,256},{192,320},{256,384},{320,448},{384,512}... | collective-permute-start | bytes 393224 | tf_op jit(solution)/shard_map/ppermute | solution.py:25
  5.7 8.7 %collective-permute-start = (bf16[2,2,128,128]{3,2,1,0:T(8,128)(2,1)S(1)}, bf16[2,2,128,128]{3,2,1,0:T(8,128)(2,1)S(1)}, u32[]{:S(2)}, u32[]{:S(2)}) collective-permute-start(bf16[2,2,128,128]{3,2,1,0:T(8,128)(2,1)S(1)} %pad_maximum_fusion.kv_ref.kv0), channel_id=1, source_target_pairs={{0,64},{64,128},{128,192},{192,256},{256,320},{320,384},{384,448},... | collective-permute-start | bytes 393224 | tf_op jit(solution)/shard_map/ppermute | solution.py:25
  7.6 1.0 %copy-start = (bf16[1,2,128,1024]{3,2,1,0:T(8,128)(2,1)S(1)}, bf16[1,2,128,1024]{3,2,1,0:T(8,128)(2,1)}, u32[]{:S(2)}) copy-start(bf16[1,2,128,1024]{3,2,1,0:T(8,128)(2,1)} %q_hbm.3) | copy-start | bytes 1572868
  8.7 1.0 %copy-start.1 = (bf16[1,2,128,1024]{3,2,1,0:T(8,128)(2,1)S(1)}, bf16[1,2,128,1024]{3,2,1,0:T(8,128)(2,1)}, u32[]{:S(2)}) copy-start(bf16[1,2,128,1024]{3,2,1,0:T(8,128)(2,1)} %g_hbm.3) | copy-start | bytes 1572868
  9.7 1.0 %copy-start.3 = (bf16[1,2,128,1024]{3,2,1,0:T(8,128)(2,1)S(1)}, bf16[1,2,128,1024]{3,2,1,0:T(8,128)(2,1)}, u32[]{:S(2)}) copy-start(bf16[1,2,128,1024]{3,2,1,0:T(8,128)(2,1)} %o_hbm.3) | copy-start | bytes 1572868
  10.8 0.7 %copy-start.5 = (f32[1,2,8,128]{3,2,1,0:T(8,128)S(1)}, f32[1,2,8,128]{3,2,1,0:T(8,128)}, u32[]{:S(2)}) copy-start(f32[1,2,8,128]{3,2,1,0:T(8,128)} %log_ref.7) | copy-start | bytes 24580
  11.5 0.7 %copy-start.6 = (s32[32]{0:T(128)S(1)}, s32[32]{0:T(128)}, u32[]{:S(2)}) copy-start(s32[32]{0:T(128)} %order_ref.7) | copy-start | bytes 388
  14.4 12.9 %copy-start.2 = (bf16[1,2,128,1024]{3,2,1,0:T(8,128)(2,1)S(1)}, bf16[1,2,128,1024]{3,2,1,0:T(8,128)(2,1)}, u32[]{:S(2)}) copy-start(bf16[1,2,128,1024]{3,2,1,0:T(8,128)(2,1)} %g_hbm.3) | copy-start | bytes 1572868
  14.4 12.9 %copy-start.4 = (bf16[1,2,128,1024]{3,2,1,0:T(8,128)(2,1)S(1)}, bf16[1,2,128,1024]{3,2,1,0:T(8,128)(2,1)}, u32[]{:S(2)}) copy-start(bf16[1,2,128,1024]{3,2,1,0:T(8,128)(2,1)} %o_hbm.3) | copy-start | bytes 1572868
  15.7 26.7 %collective-permute-start.2 = (bf16[128,512]{1,0:T(8,128)(2,1)S(1)}, bf16[128,512]{1,0:T(8,128)(2,1)S(1)}, u32[]{:S(2)}, u32[]{:S(2)}) collective-permute-start(bf16[128,512]{1,0:T(8,128)(2,1)S(1)} %query_part.2.dqa_ref), channel_id=1, source_target_pairs={{1,0},{2,1},{3,2},{4,3},{5,4},{6,5},{7,6},{8,7},{9,8},{10,9},{11,1... | collective-permute-start | bytes 393224 | tf_op jit(solution)/shard_map/ppermute | solution.py:30
  19.2 24.1 %collective-permute-start.3 = (bf16[128,512]{1,0:T(8,128)(2,1)S(1)}, bf16[128,512]{1,0:T(8,128)(2,1)S(1)}, u32[]{:S(2)}, u32[]{:S(2)}) collective-permute-start(bf16[128,512]{1,0:T(8,128)(2,1)S(1)} %query_part.3.dqb_ref), channel_id=1, source_target_pairs={{1,0},{2,1},{3,2},{4,3},{5,4},{6,5},{7,6},{8,7},{9,8},{10,9},{11,1... | collective-permute-start | bytes 393224 | tf_op jit(solution)/shard_map/ppermute | solution.py:30
  29.4 21.5 %collective-permute-start.4 = (bf16[2,128,128]{2,1,0:T(8,128)(2,1)S(1)}, bf16[2,128,128]{2,1,0:T(8,128)(2,1)S(1)}, u32[]{:S(2)}, u32[]{:S(2)}) collective-permute-start(bf16[2,128,128]{2,1,0:T(8,128)(2,1)S(1)} %get-tuple-element.40), channel_id=1, source_target_pairs={{0,960},{64,0},{128,64},{192,128},{256,192},{320,256},{384,320},{4... | collective-permute-start | bytes 196616 | tf_op jit(solution)/shard_map/ppermute | solution.py:25
  31.3 19.6 %collective-permute-start.5 = (bf16[2,128,128]{2,1,0:T(8,128)(2,1)S(1)}, bf16[2,128,128]{2,1,0:T(8,128)(2,1)S(1)}, u32[]{:S(2)}, u32[]{:S(2)}) collective-permute-start(bf16[2,128,128]{2,1,0:T(8,128)(2,1)S(1)} %get-tuple-element.41), channel_id=1, source_target_pairs={{0,896},{64,960},{128,0},{192,64},{256,128},{320,192},{384,256},{4... | collective-permute-start | bytes 196616 | tf_op jit(solution)/shard_map/ppermute | solution.py:25
  44.1 6.9 %collective-permute-start.6 = (bf16[2,128,128]{2,1,0:T(8,128)(2,1)S(1)}, bf16[2,128,128]{2,1,0:T(8,128)(2,1)S(1)}, u32[]{:S(2)}, u32[]{:S(2)}) collective-permute-start(bf16[2,128,128]{2,1,0:T(8,128)(2,1)S(1)} %get-tuple-element.43), channel_id=1, source_target_pairs={{0,960},{64,0},{128,64},{192,128},{256,192},{320,256},{384,320},{4... | collective-permute-start | bytes 196616 | tf_op jit(solution)/shard_map/ppermute | solution.py:25
  46.7 7.1 %collective-permute-start.7 = (bf16[2,128,128]{2,1,0:T(8,128)(2,1)S(1)}, bf16[2,128,128]{2,1,0:T(8,128)(2,1)S(1)}, u32[]{:S(2)}, u32[]{:S(2)}) collective-permute-start(bf16[2,128,128]{2,1,0:T(8,128)(2,1)S(1)} %get-tuple-element.44), channel_id=1, source_target_pairs={{0,896},{64,960},{128,0},{192,64},{256,128},{320,192},{384,256},{4... | collective-permute-start | bytes 196616 | tf_op jit(solution)/shard_map/ppermute | solution.py:25

commit v3 on v2

v3 whole, which is shorter than its diff:
```python
import functools
import math

import jax
import jax.numpy as jnp
from jax import lax
from jax.experimental import pallas as pl
from jax.experimental.pallas import tpu as pltpu
from jax.sharding import PartitionSpec as P

WINDOW = 3
PAIR = 2
NT = (((1,), (1,)), ((), ()))
NN = (((1,), (0,)), ((), ()))
LOW = jnp.bfloat16
WIDE = jnp.float32


def dot(a, b, dims=NN):
    return lax.dot_general(a, b, dims, preferred_element_type=WIDE)


def ring(value, steps, sections=None):
    count = lax.axis_size("ctx")
    if sections is None:
        return lax.ppermute(value, "ctx", [(i, (i + steps) % count) for i in range(count)])
    layers = lax.axis_size("section")
    route = [(i * layers + s, (i + steps) % count * layers + s) for s in sections for i in range(count)]
    return lax.ppermute(value, ("ctx", "section"), route)


def down(value):
    count = lax.axis_size("section")
    return lax.ppermute(value, "section", [(i, i - 1) for i in range(1, count)])


def mask_bias(order_ref, rows, offsets):
    half = rows // 2
    slots = order_ref.shape[0]
    own = lax.axis_index("ctx")
    lane = lax.broadcasted_iota(jnp.int32, (half, rows), 1)
    sub = lax.broadcasted_iota(jnp.int32, (half, rows), 0)
    query = jnp.where(
        lane < half,
        order_ref[2 * own] * half + lane,
        order_ref[2 * own + 1] * half + lane - half,
    )
    blocks = []
    for offset in offsets:
        for part in range(2):
            slot = lax.rem(2 * (own - offset) + part + slots, slots)
            blocks.append(jnp.where(order_ref[slot] * half + sub <= query, 0.0, -1e30))
    return jnp.concatenate(blocks, axis=0)


def wider(bias):
    return jnp.concatenate([bias] * PAIR, axis=1)


def stacked(block, size):
    return jnp.concatenate(
        [block[:, i * size : (i + 1) * size] for i in range(block.shape[1] // size)], axis=0
    )


def head_rows(table, first):
    return jnp.concatenate([table[first + i : first + i + 1] for i in range(PAIR)], axis=1)


def dots_of_rows(upstream, out, size):
    product = upstream.astype(WIDE) * out.astype(WIDE)
    high = product.astype(LOW)
    low = (product - high.astype(WIDE)).astype(LOW)
    shape = (8, product.shape[1])
    pick = (lax.broadcasted_iota(jnp.int32, shape, 1) // size == lax.broadcasted_iota(jnp.int32, shape, 0)).astype(WIDE).astype(LOW)
    return dot(pick, high, NT) + dot(pick, low, NT)


def turned(part, rows):
    count = part.shape[1] // rows
    return jnp.concatenate([part[:, i * rows : (i + 1) * rows].T for i in range(count)], axis=1)


def joined(refs, micro, which):
    return jnp.concatenate([ref[micro, which] for ref in refs], axis=0)


def own_kernel(
    factor, order_hbm, log_hbm, kv_ref, q_hbm, g_hbm, o_hbm,
    qs_ref, gs_ref, rd_ref, dqt_ref, own_ref, bias_ref, log_ref, order_s, q_v, g_v, o_v, sems,
):
    copies = [
        pltpu.make_async_copy(source, target, sems.at[i])
        for i, (source, target) in enumerate(
            (
                (order_hbm, order_s),
                (g_hbm.at[0, 0], g_v),
                (o_hbm.at[0, 0], o_v),
                (q_hbm.at[0, 0], q_v),
                (log_hbm.at[0], log_ref),
            )
        )
    ]
    for copy in copies:
        copy.start()
    rows, size = kv_ref.shape[2], kv_ref.shape[3]
    keys, values = kv_ref[0, 0], kv_ref[0, 1]
    keys_t = keys.T
    copies[0].wait()
    bias = mask_bias(order_s, rows, range(WINDOW))
    bias_ref[...] = bias
    bias = wider(bias[:rows])
    copies[1].wait()
    copies[2].wait()
    grad = stacked(g_v[...], size)
    gs_ref[...] = grad
    dot_rows = dots_of_rows(g_v[...], o_v[...], size)
    rd_ref[...] = dot_rows
    copies[3].wait()
    query = stacked(q_v[...], size)
    qs_ref[...] = query
    copies[4].wait()
    log_rows = log_ref[0]
    step = PAIR * rows
    key_sum = value_sum = 0.0
    for first in range(0, query.shape[0] // rows, PAIR):
        cut = slice(first * rows, first * rows + step)
        probs = jnp.exp(dot(keys, query[cut], NT) * factor + (bias - head_rows(log_rows, first)))
        grad_scores = (probs * (dot(values, grad[cut], NT) - head_rows(dot_rows, first))).astype(LOW)
        dqt_ref[:, cut] = dot(keys_t, grad_scores)
        key_sum += dot(grad_scores, query[cut])
        value_sum += dot(probs.astype(LOW), grad[cut])
    own_ref[0] = key_sum * factor
    own_ref[1] = value_sum


def query_kernel(factor, bias_ref, log_ref, kv1, kv2, qs_ref, gs_ref, rd_ref, dqt_ref, dq_ref):
    rows, size = kv1.shape[2], kv1.shape[3]
    keys, values = joined((kv1, kv2), 0, 0), joined((kv1, kv2), 0, 1)
    keys_t = keys.T
    bias = wider(bias_ref[rows:])
    log_rows, dot_rows = log_ref[0], rd_ref[...]
    step = PAIR * rows
    for first in range(0, dq_ref.shape[1] // size, PAIR):
        cut = slice(first * rows, first * rows + step)
        probs = jnp.exp(dot(keys, qs_ref[cut], NT) * factor + (bias - head_rows(log_rows, first)))
        grad_scores = (probs * (dot(values, gs_ref[cut], NT) - head_rows(dot_rows, first))).astype(LOW)
        part = (dot(keys_t, grad_scores) + dqt_ref[:, cut]) * factor
        dq_ref[:, first * size : (first + PAIR) * size] = turned(part, rows).astype(LOW)


def middle_kernel(
    factor, bias_ref, log_ref, kv0, kv1, kv2, kv1_first, kv2_first, qs_ref, gs_ref, rd_ref, dqt_ref, q_hbm, g_hbm, o_hbm,
    gq_hbm, near_ref, far_ref, qs1_ref, g1_ref, o1_ref, probs_ref, win_ref, q_v, dq_v, sems,
):
    copies = [
        pltpu.make_async_copy(q_hbm.at[0, 1], q_v, sems.at[0]),
        pltpu.make_async_copy(g_hbm.at[0, 1], g1_ref, sems.at[1]),
        pltpu.make_async_copy(o_hbm.at[0, 1], o1_ref, sems.at[2]),
    ]
    for copy in copies:
        copy.start()
    rows, size = kv1.shape[2], kv1.shape[3]
    heads = qs_ref.shape[0] // rows
    bottom = lax.axis_index("section") == 0

    def window(micro, which):
        near = jnp.where(bottom, kv1_first[micro, which], kv1[micro, which])
        far = jnp.where(bottom, kv2_first[micro, which], kv2[micro, which])
        return jnp.concatenate([near, far], axis=0)

    keys, values = window(0, 0), window(0, 1)
    keys_t = keys.T
    bias = wider(bias_ref[...])
    log_rows, dot_rows = log_ref[0], rd_ref[...]
    step = PAIR * rows
    key_sum = value_sum = 0.0
    for first in range(0, heads, PAIR):
        cut = slice(first * rows, first * rows + step)
        query, grad = qs_ref[cut], gs_ref[cut]
        probs = jnp.exp(dot(keys, query, NT) * factor + (bias[rows:] - head_rows(log_rows, first)))
        grad_scores = (probs * (dot(values, grad, NT) - head_rows(dot_rows, first))).astype(LOW)
        key_sum += dot(grad_scores, query)
        value_sum += dot(probs.astype(LOW), grad)
        part = (dot(keys_t, grad_scores) + dqt_ref[:, cut]) * factor
        dq_v[:, first * size : (first + PAIR) * size] = turned(part, rows).astype(LOW)
    back = pltpu.make_async_copy(dq_v, gq_hbm.at[0, 0], sems.at[3])
    back.start()
    key_sum = key_sum * factor
    for i, ref in enumerate((near_ref, far_ref)):
        ref[0] = key_sum[i * rows : (i + 1) * rows].astype(LOW)
        ref[1] = value_sum[i * rows : (i + 1) * rows].astype(LOW)
    copies[0].wait()
    query = stacked(q_v[...], size)
    qs1_ref[...] = query
    keys = jnp.concatenate([kv0[1, 0], window(1, 0)], axis=0)
    win_ref[0] = keys
    win_ref[1] = jnp.concatenate([kv0[1, 1], window(1, 1)], axis=0)
    log_rows = log_ref[1]
    for first in range(0, heads, PAIR):
        cut = slice(first * rows, first * rows + step)
        scores = dot(keys, query[cut], NT)
        probs_ref[:, cut] = jnp.exp(scores * factor + (bias - head_rows(log_rows, first)))
    copies[1].wait()
    copies[2].wait()
    back.wait()


def others_kernel(factor, win_ref, qs_ref, g_ref, o_ref, probs_ref, near0, far0, r_ref, near_ref, far_ref, up_ref, gs_ref):
    rows, size = win_ref.shape[1] // WINDOW, win_ref.shape[2]
    values = win_ref[1]
    upstream = (g_ref[...].astype(WIDE) + r_ref[...].astype(WIDE)).astype(LOW)
    dot_rows = dots_of_rows(upstream, o_ref[...], size)
    upstream = stacked(upstream, size)
    up_ref[...] = upstream
    step = PAIR * rows
    key_sum = value_sum = 0.0
    for first in range(0, upstream.shape[0] // rows, PAIR):
        cut = slice(first * rows, first * rows + step)
        probs, grad = probs_ref[:, cut], upstream[cut]
        grad_scores = (probs * (dot(values, grad, NT) - head_rows(dot_rows, first))).astype(LOW)
        gs_ref[:, cut] = grad_scores
        key_sum += dot(grad_scores[rows:], qs_ref[cut])
        value_sum += dot(probs[rows:].astype(LOW), grad)
    key_sum = key_sum * factor
    for i, (ref, before) in enumerate(((near_ref, near0), (far_ref, far0))):
        ref[0] = before[...]
        ref[1, 0] = key_sum[i * rows : (i + 1) * rows].astype(LOW)
        ref[1, 1] = value_sum[i * rows : (i + 1) * rows].astype(LOW)


def rest_kernel(factor, win_ref, qs_ref, probs_ref, up_ref, gs_ref, _, own_ref, gq_hbm, dq_v, sem):
    rows = win_ref.shape[1] // WINDOW
    dq_v[...] = turned(dot(win_ref[0].T, gs_ref[...]) * factor, rows).astype(LOW)
    back = pltpu.make_async_copy(dq_v, gq_hbm.at[0, 1], sem)
    back.start()
    own_ref[0] = dot(gs_ref[:rows], qs_ref[...]) * factor
    own_ref[1] = dot(probs_ref[:rows].astype(LOW), up_ref[...])
    back.wait()


def sum_kernel(own0, own1, near, far, gk_ref, gv_ref):
    for micro, own in enumerate((own0, own1)):
        for which, ref in ((0, gk_ref), (1, gv_ref)):
            total = own[which] + near[micro, which].astype(WIDE) + far[micro, which].astype(WIDE)
            ref[0, micro] = total.astype(LOW)


VM = pl.BlockSpec(memory_space=pltpu.VMEM)
HB = pl.BlockSpec(memory_space=pltpu.HBM)


def shards(query_in, key_in, value_in, forward_out, log_sum, grad_out, block_order):
    rows, width = query_in.shape[2:]
    size = key_in.shape[3]
    heads = width // size
    near_rows = WINDOW * rows
    factor = 1.0 / math.sqrt(size)

    def low(*shape):
        return jax.ShapeDtypeStruct(shape, LOW)

    def wide(*shape):
        return jax.ShapeDtypeStruct(shape, WIDE)

    def call(body, name, ins, outs, in_specs=None, out_specs=None, scratch=(), share=1.0, **more):
        flops = int(2 * near_rows * heads * rows * size * share)
        return pl.pallas_call(
            body,
            in_specs=in_specs or [VM] * len(ins),
            out_specs=out_specs or [VM] * len(outs),
            out_shape=outs,
            scratch_shapes=list(scratch),
            compiler_params=pltpu.CompilerParams(vmem_limit_bytes=40 * 2**20),
            cost_estimate=pl.CostEstimate(flops=flops, bytes_accessed=1024, transcendentals=0),
            name=name,
            **more,
        )(*ins)

    dma = pltpu.SemaphoreType.DMA
    query_in, grad_out, forward_out, log_sum, block_order = (
        pltpu.with_memory_space_constraint(x, pltpu.HBM)
        for x in (query_in, grad_out, forward_out, log_sum, block_order)
    )
    kv0 = jnp.stack([key_in[0], value_in[0]], axis=1)
    upper = range(1, lax.axis_size("section"))
    kv2, kv1 = ring(kv0, 2, upper), ring(kv0, 1, upper)
    pair = (2, rows, size)

    qs, gs, rd, dqt, own0, bias, log = call(
        functools.partial(own_kernel, factor),
        "own_terms",
        (block_order, log_sum, kv0, query_in, grad_out, forward_out),
        [
            low(heads * rows, size),
            low(heads * rows, size),
            wide(8, rows),
            wide(size, heads * rows),
            wide(*pair),
            wide(near_rows, rows),
            wide(2, heads, rows),
        ],
        in_specs=[HB, HB, VM, HB, HB, HB],
        scratch=[pltpu.SMEM(block_order.shape, jnp.int32)] + [pltpu.VMEM((rows, width), LOW)] * 3 + [dma((5,))],
        share=2,
    )
    (part,) = call(
        functools.partial(query_kernel, factor),
        "query_part",
        (bias, log, kv1, kv2, qs, gs, rd, dqt),
        [low(rows, width)],
    )
    received = down(part)
    late, _ = lax.optimization_barrier((kv0, part))
    kv2_first, kv1_first = ring(late, 2, (0,)), ring(late, 1, (0,))

    grad_query, near0, far0, qs1, g1, o1, probs, win = call(
        functools.partial(middle_kernel, factor),
        "middle_terms",
        (bias, log, kv0, kv1, kv2, kv1_first, kv2_first, qs, gs, rd, dqt, query_in, grad_out, forward_out),
        [
            low(*query_in.shape),
            low(*pair),
            low(*pair),
            low(heads * rows, size),
            low(rows, width),
            low(rows, width),
            wide(near_rows, heads * rows),
            low(2, near_rows, size),
        ],
        in_specs=[VM] * 11 + [HB] * 3,
        out_specs=[HB] + [VM] * 7,
        scratch=[pltpu.VMEM((rows, width), LOW)] * 2 + [dma((4,))],
        share=0.001,
    )

    near, far, up, grad_scores = call(
        functools.partial(others_kernel, factor),
        "second_others",
        (win, qs1, g1, o1, probs, near0, far0, received),
        [low(2, *pair), low(2, *pair), low(heads * rows, size), low(near_rows, heads * rows)],
        share=2,
    )
    far, near = ring(far, -2), ring(near, -1)
    own1, grad_query = call(
        functools.partial(rest_kernel, factor),
        "second_rest",
        (win, qs1, probs, up, grad_scores, grad_query),
        [wide(*pair), low(*query_in.shape)],
        in_specs=[VM] * 5 + [HB],
        out_specs=[VM, HB],
        scratch=[pltpu.VMEM((rows, width), LOW), dma],
        input_output_aliases={5: 1},
    )
    grad_key, grad_value = call(
        sum_kernel,
        "sums",
        (own0, own1, near, far),
        [low(1, 2, rows, size)] * 2,
        share=0.01,
    )
    return (grad_query, grad_key, grad_value)


def solution(mesh):
    split = P("section", None, "ctx", None)
    return jax.shard_map(
        shards,
        mesh=mesh,
        in_specs=(split, split, split, split, P("section", None, None, "ctx"), split, P()),
        out_specs=(split, split, split),
        check_vma=False,
    )
```

time: 55 us -> 50.9 us (0.925)
  the two profiles are of different devices: /device:TPU:40 before, /device:TPU:1 now
where the time goes in v3:
time: 50.9 us; the launch traced here: 50.5 us
  starting transfers between devices  24.4 us (48%)
  waiting for transfers between devices  14.9 us (29%)
  Pallas kernels  9.59 us (19%)
  other arithmetic  0.89 us (2%)
  between operations  0.76 us (1%)
    ppermute x2, starting transfers between devices, ring(): lax.ppermute(value, 'ctx', [(i, (i + steps) % count) for i in range(count)])  13.9 us
    ppermute x4, waiting for transfers between devices, ring(): return lax.ppermute(value, ('ctx', 'section'), route)  10.9 us
    pallas_call x6, Pallas kernels, call(): pl.pallas_call(body, in_specs=in_specs or [VM] * len(ins), out_specs=out_...  9.59 us
    ppermute x4, starting transfers between devices, ring(): return lax.ppermute(value, ('ctx', 'section'), route)  9.22 us
    ppermute x2, waiting for transfers between devices, ring(): lax.ppermute(value, 'ctx', [(i, (i + steps) % count) for i in range(count)])  3.93 us
    ppermute x1, starting transfers between devices, down(): return lax.ppermute(value, 'section', [(i, i - 1) for i in range(1, count)])  1.29 us
  transfers between devices with their start and end apart: 7, of which 3 were waited for; matrix products, arithmetic and copies ran while one was open for 0% of the time, Pallas kernels for 13%

profile of v3, /device:TPU:1, one launch (start us, length us, event | category | flops | bytes accessed | tf_op | source)
XLA Modules:
  0.0 50.5 jit_solution(4104104959962707094)
XLA Ops:
  0.6 0.9 %pad_maximum_fusion.kv_ref.kv0 = bf16[2,2,128,128]{3,2,1,0:T(8,128)(2,1)S(1)} fusion(bf16[2,1,128,128]{3,2,1,0:T(8,128)(2,1)} %bitcast.2, bf16[2,1,128,128]{3,2,1,0:T(8,128)(2,1)} %bitcast.3), kind=kLoop, calls=%fused_computation | loop fusion | flops 65536 | bytes 262144 | tf_op jit(solution)/shard_map/stack | solution.py:285
  1.5 0.7 %collective-permute-start.1 = (bf16[2,2,128,128]{3,2,1,0:T(8,128)(2,1)S(1)}, bf16[2,2,128,128]{3,2,1,0:T(8,128)(2,1)S(1)}, u32[]{:S(2)}, u32[]{:S(2)}) collective-permute-start(bf16[2,2,128,128]{3,2,1,0:T(8,128)(2,1)S(1)} %pad_maximum_fusion.kv_ref.kv0), channel_id=1, source_target_pairs={{1,129},{65,193},{129,257},{193,321},{257,385},{321,449},{385,513}... | collective-permute-start | bytes 393224 | tf_op jit(solution)/shard_map/ppermute | solution.py:29
  2.2 0.7 %collective-permute-start = (bf16[2,2,128,128]{3,2,1,0:T(8,128)(2,1)S(1)}, bf16[2,2,128,128]{3,2,1,0:T(8,128)(2,1)S(1)}, u32[]{:S(2)}, u32[]{:S(2)}) collective-permute-start(bf16[2,2,128,128]{3,2,1,0:T(8,128)(2,1)S(1)} %pad_maximum_fusion.kv_ref.kv0), channel_id=1, source_target_pairs={{1,65},{65,129},{129,193},{193,257},{257,321},{321,385},{385,449},... | collective-permute-start | bytes 393224 | tf_op jit(solution)/shard_map/ppermute | solution.py:29
  2.9 2.7 %own_terms.1 = (bf16[1024,128]{1,0:T(8,128)(2,1)S(1)}, bf16[1024,128]{1,0:T(8,128)(2,1)S(1)}, f32[8,128]{1,0:T(8,128)S(1)}, f32[128,1024]{1,0:T(8,128)S(1)}, f32...) custom-call(s32[32]{0:T(128)} %order_hbm.1, f32[1,2,8,128]{3,2,1,0:T(8,128)} %log_hbm.1, ...), custom_call_target="tpu_custom_call" | custom-call | flops 201326592 | bytes 1024 | tf_op jit(solution)/shard_map/own_terms/pallas_call | solution.py:268
  5.6 0.0 collective-permute-done.1.kv2
  5.6 0.0 collective-permute-done.kv1
  5.6 1.1 %query_part.1 = bf16[128,1024]{1,0:T(8,128)(2,1)S(1)} custom-call(f32[384,128]{1,0:T(8,128)S(1)} %get-tuple-element.27.bias_ref, f32[2,8,128]{2,1,0:T(8,128)S(1)} %get-tuple-element.28.log_ref, bf16[2,2,128,128]{3,2,1,0:T(8,128)(2,1)S(1)} %collective-permute-done.kv1, bf16[2,2,128,128]{3,2,1,0:T(8,128)(2,1)S(1)} %collective-permute-done.1.kv2, ...), custom_call_target="tpu_custom_call" | custom-call | flops 100663296 | bytes 1024 | tf_op jit(solution)/shard_map/query_part/pallas_call | solution.py:268
  6.8 1.3 %collective-permute-start.4 = (bf16[128,1024]{1,0:T(8,128)(2,1)S(1)}, bf16[128,1024]{1,0:T(8,128)(2,1)S(1)}, u32[]{:S(2)}, u32[]{:S(2)}) collective-permute-start(bf16[128,1024]{1,0:T(8,128)(2,1)S(1)} %query_part.1), channel_id=1, source_target_pairs={{1,0},{2,1},{3,2},{4,3},{5,4},{6,5},{7,6},{8,7},{9,8},{10,9},{11,1... | collective-permute-start | bytes 786440 | tf_op jit(solution)/shard_map/ppermute | solution.py:34
  8.1 4.0 %collective-permute-start.3 = (bf16[2,2,128,128]{3,2,1,0:T(8,128)(2,1)S(1)}, bf16[2,2,128,128]{3,2,1,0:T(8,128)(2,1)S(1)}, u32[]{:S(2)}, u32[]{:S(2)}) collective-permute-start(bf16[2,2,128,128]{3,2,1,0:T(8,128)(2,1)S(1)} %pad_maximum_fusion.kv_ref.kv0), channel_id=1, source_target_pairs={{0,128},{64,192},{128,256},{192,320},{256,384},{320,448},{384,512}... | collective-permute-start | bytes 393224 | tf_op jit(solution)/shard_map/ppermute | solution.py:29
  12.1 3.8 %collective-permute-start.2 = (bf16[2,2,128,128]{3,2,1,0:T(8,128)(2,1)S(1)}, bf16[2,2,128,128]{3,2,1,0:T(8,128)(2,1)S(1)}, u32[]{:S(2)}, u32[]{:S(2)}) collective-permute-start(bf16[2,2,128,128]{3,2,1,0:T(8,128)(2,1)S(1)} %pad_maximum_fusion.kv_ref.kv0), channel_id=1, source_target_pairs={{0,64},{64,128},{128,192},{192,256},{256,320},{320,384},{384,448},... | collective-permute-start | bytes 393224 | tf_op jit(solution)/shard_map/ppermute | solution.py:29
  16.0 0.7 %collective-permute-done.3.kv2_first = bf16[2,2,128,128]{3,2,1,0:T(8,128)(2,1)S(1)} collective-permute-done((bf16[2,2,128,128]{3,2,1,0:T(8,128)(2,1)S(1)}, bf16[2,2,128,128]{3,2,1,0:T(8,128)(2,1)S(1)}, u32[]{:S(2)}, u32[]{:S(2)}) %collective-permute-start.3) | collective-permute-done | bytes 131104 | tf_op jit(solution)/shard_map/ppermute | solution.py:29
  16.6 10.3 %collective-permute-done.2.kv1_first = bf16[2,2,128,128]{3,2,1,0:T(8,128)(2,1)S(1)} collective-permute-done((bf16[2,2,128,128]{3,2,1,0:T(8,128)(2,1)S(1)}, bf16[2,2,128,128]{3,2,1,0:T(8,128)(2,1)S(1)}, u32[]{:S(2)}, u32[]{:S(2)}) %collective-permute-start.2) | collective-permute-done | bytes 131104 | tf_op jit(solution)/shard_map/ppermute | solution.py:29
  26.9 2.6 %middle_terms.1 = (bf16[1,2,128,1024]{3,2,1,0:T(8,128)(2,1)}, bf16[2,128,128]{2,1,0:T(8,128)(2,1)S(1)}, bf16[2,128,128]{2,1,0:T(8,128)(2,1)S(1)}, bf16[1024,128]...) custom-call(f32[384,128]{1,0:T(8,128)S(1)} %get-tuple-element.27.bia, ...), custom_call_target="tpu_custom_call" | custom-call | flops 100663 | bytes 1024 | tf_op jit(solution)/shard_map/middle_terms/pallas_call | solution.py:268
  29.5 0.0 collective-permute-done.4.r_ref
  29.5 1.3 %second_others.1 = (bf16[2,2,128,128]{3,2,1,0:T(8,128)(2,1)S(1)}, bf16[2,2,128,128]{3,2,1,0:T(8,128)(2,1)S(1)}, bf16[1024,128]{1,0:T(8,128)(2,1)S(1)}, bf16[384,1024]{1,0:T(8,128)(2,1)S(1)}) custom-call(bf16[2,384,128]{2,1,0:T(8,128)(2,1)S(1)} %get-tuple-element.34.win_ref, bf16[1024,128]{1,0:T(8,128)(2,1)S(1)} %get-tuple-element.35.qs_ref, ...), custom_call_target="tpu_custom_call" | custom-call | flops 201326592 | bytes 1024 | tf_op jit(solution)/shard_map/second_others/pallas_call | solution.py:268
  30.8 12.0 %collective-permute-start.5 = (bf16[2,2,128,128]{3,2,1,0:T(8,128)(2,1)S(1)}, bf16[2,2,128,128]{3,2,1,0:T(8,128)(2,1)S(1)}, u32[]{:S(2)}, u32[]{:S(2)}) collective-permute-start(bf16[2,2,128,128]{3,2,1,0:T(8,128)(2,1)S(1)} %get-tuple-element.47), channel_id=1, source_target_pairs={{0,960},{64,0},{128,64},{192,128},{256,192},{320,256},{384,320},{4... | collective-permute-start | bytes 393224 | tf_op jit(solution)/shard_map/ppermute | solution.py:26
  42.8 1.9 %collective-permute-start.6 = (bf16[2,2,128,128]{3,2,1,0:T(8,128)(2,1)S(1)}, bf16[2,2,128,128]{3,2,1,0:T(8,128)(2,1)S(1)}, u32[]{:S(2)}, u32[]{:S(2)}) collective-permute-start(bf16[2,2,128,128]{3,2,1,0:T(8,128)(2,1)S(1)} %get-tuple-element.48), channel_id=1, source_target_pairs={{0,896},{64,960},{128,0},{192,64},{256,128},{320,192},{384,256},{4... | collective-permute-start | bytes 393224 | tf_op jit(solution)/shard_map/ppermute | solution.py:26
  44.8 1.1 %second_rest.1 = (f32[2,128,128]{2,1,0:T(8,128)S(1)}, bf16[1,2,128,1024]{3,2,1,0:T(8,128)(2,1)}) custom-call(bf16[2,384,128]{2,1,0:T(8,128)(2,1)S(1)} %get-tuple-element.34.win_ref, bf16[1024,128]{1,0:T(8,128)(2,1)S(1)} %get-tuple-element.35.qs_ref, f32[384,1024]{1,0:T(8,128)S(1)} %get-tuple-element.36.probs_ref, ...), custom_call_target="tpu_custom_call", output_to_operand_aliasing={{1}: (5, {})} | custom-call | flops 100663296 | bytes 1024 | tf_op jit(solution)/shard_map/second_rest/pallas_call | solution.py:268
  45.9 0.0 collective-permute-done.5.near
  45.9 3.9 %collective-permute-done.6.far = bf16[2,2,128,128]{3,2,1,0:T(8,128)(2,1)S(1)} collective-permute-done((bf16[2,2,128,128]{3,2,1,0:T(8,128)(2,1)S(1)}, bf16[2,2,128,128]{3,2,1,0:T(8,128)(2,1)S(1)}, u32[]{:S(2)}, u32[]{:S(2)}) %collective-permute-start.6) | collective-permute-done | bytes 131104 | tf_op jit(solution)/shard_map/ppermute | solution.py:26
  49.9 0.7 %sums.1 = (bf16[1,2,128,128]{3,2,1,0:T(8,128)(2,1)}, bf16[1,2,128,128]{3,2,1,0:T(8,128)(2,1)}) custom-call(f32[2,128,128]{2,1,0:T(8,128)S(1)} %get-tuple-element.45.own0, f32[2,128,128]{2,1,0:T(8,128)S(1)} %get-tuple-element.46.own1, bf16[2,2,128,128]{3,2,1,0:T(8,128)(2,1)S(1)} %collective-permute-done.5.near, ...), custom_call_target="tpu_custom_call" | custom-call | flops 1006632 | bytes 1024 | tf_op jit(solution)/shard_map/sums/pallas_call | solution.py:268
Async XLA Ops:
  1.5 4.1 %collective-permute-start.1 = (bf16[2,2,128,128]{3,2,1,0:T(8,128)(2,1)S(1)}, bf16[2,2,128,128]{3,2,1,0:T(8,128)(2,1)S(1)}, u32[]{:S(2)}, u32[]{:S(2)}) collective-permute-start(bf16[2,2,128,128]{3,2,1,0:T(8,128)(2,1)S(1)} %pad_maximum_fusion.kv_ref.kv0), channel_id=1, source_target_pairs={{1,129},{65,193},{129,257},{193,321},{257,385},{321,449},{385,513}... | collective-permute-start | bytes 393224 | tf_op jit(solution)/shard_map/ppermute | solution.py:29
  2.2 3.4 %collective-permute-start = (bf16[2,2,128,128]{3,2,1,0:T(8,128)(2,1)S(1)}, bf16[2,2,128,128]{3,2,1,0:T(8,128)(2,1)S(1)}, u32[]{:S(2)}, u32[]{:S(2)}) collective-permute-start(bf16[2,2,128,128]{3,2,1,0:T(8,128)(2,1)S(1)} %pad_maximum_fusion.kv_ref.kv0), channel_id=1, source_target_pairs={{1,65},{65,129},{129,193},{193,257},{257,321},{321,385},{385,449},... | collective-permute-start | bytes 393224 | tf_op jit(solution)/shard_map/ppermute | solution.py:29
  6.8 22.7 %collective-permute-start.4 = (bf16[128,1024]{1,0:T(8,128)(2,1)S(1)}, bf16[128,1024]{1,0:T(8,128)(2,1)S(1)}, u32[]{:S(2)}, u32[]{:S(2)}) collective-permute-start(bf16[128,1024]{1,0:T(8,128)(2,1)S(1)} %query_part.1), channel_id=1, source_target_pairs={{1,0},{2,1},{3,2},{4,3},{5,4},{6,5},{7,6},{8,7},{9,8},{10,9},{11,1... | collective-permute-start | bytes 786440 | tf_op jit(solution)/shard_map/ppermute | solution.py:34
  8.1 8.6 %collective-permute-start.3 = (bf16[2,2,128,128]{3,2,1,0:T(8,128)(2,1)S(1)}, bf16[2,2,128,128]{3,2,1,0:T(8,128)(2,1)S(1)}, u32[]{:S(2)}, u32[]{:S(2)}) collective-permute-start(bf16[2,2,128,128]{3,2,1,0:T(8,128)(2,1)S(1)} %pad_maximum_fusion.kv_ref.kv0), channel_id=1, source_target_pairs={{0,128},{64,192},{128,256},{192,320},{256,384},{320,448},{384,512}... | collective-permute-start | bytes 393224 | tf_op jit(solution)/shard_map/ppermute | solution.py:29
  12.1 14.8 %collective-permute-start.2 = (bf16[2,2,128,128]{3,2,1,0:T(8,128)(2,1)S(1)}, bf16[2,2,128,128]{3,2,1,0:T(8,128)(2,1)S(1)}, u32[]{:S(2)}, u32[]{:S(2)}) collective-permute-start(bf16[2,2,128,128]{3,2,1,0:T(8,128)(2,1)S(1)} %pad_maximum_fusion.kv_ref.kv0), channel_id=1, source_target_pairs={{0,64},{64,128},{128,192},{192,256},{256,320},{320,384},{384,448},... | collective-permute-start | bytes 393224 | tf_op jit(solution)/shard_map/ppermute | solution.py:29
  30.8 15.1 %collective-permute-start.5 = (bf16[2,2,128,128]{3,2,1,0:T(8,128)(2,1)S(1)}, bf16[2,2,128,128]{3,2,1,0:T(8,128)(2,1)S(1)}, u32[]{:S(2)}, u32[]{:S(2)}) collective-permute-start(bf16[2,2,128,128]{3,2,1,0:T(8,128)(2,1)S(1)} %get-tuple-element.47), channel_id=1, source_target_pairs={{0,960},{64,0},{128,64},{192,128},{256,192},{320,256},{384,320},{4... | collective-permute-start | bytes 393224 | tf_op jit(solution)/shard_map/ppermute | solution.py:26
  42.8 7.0 %collective-permute-start.6 = (bf16[2,2,128,128]{3,2,1,0:T(8,128)(2,1)S(1)}, bf16[2,2,128,128]{3,2,1,0:T(8,128)(2,1)S(1)}, u32[]{:S(2)}, u32[]{:S(2)}) collective-permute-start(bf16[2,2,128,128]{3,2,1,0:T(8,128)(2,1)S(1)} %get-tuple-element.48), channel_id=1, source_target_pairs={{0,896},{64,960},{128,0},{192,64},{256,128},{320,192},{384,256},{4... | collective-permute-start | bytes 393224 | tf_op jit(solution)/shard_map/ppermute | solution.py:26

commit v4 on v3

--- a/solution.py
+++ b/solution.py
@@ -20,13 +20,9 @@
     return lax.dot_general(a, b, dims, preferred_element_type=WIDE)
 
 
-def ring(value, steps, sections=None):
+def ring(value, steps):
     count = lax.axis_size("ctx")
-    if sections is None:
-        return lax.ppermute(value, "ctx", [(i, (i + steps) % count) for i in range(count)])
-    layers = lax.axis_size("section")
-    route = [(i * layers + s, (i + steps) % count * layers + s) for s in sections for i in range(count)]
-    return lax.ppermute(value, ("ctx", "section"), route)
+    return lax.ppermute(value, "ctx", [(i, (i + steps) % count) for i in range(count)])
 
 
 def down(value):
@@ -134,7 +130,7 @@
     own_ref[1] = value_sum
 
 
-def query_kernel(factor, bias_ref, log_ref, kv1, kv2, qs_ref, gs_ref, rd_ref, dqt_ref, dq_ref):
+def query_kernel(factor, bias_ref, log_ref, kv2, kv1, qs_ref, gs_ref, rd_ref, dqt_ref, dq_ref):
     rows, size = kv1.shape[2], kv1.shape[3]
     keys, values = joined((kv1, kv2), 0, 0), joined((kv1, kv2), 0, 1)
     keys_t = keys.T
@@ -150,27 +146,20 @@
 
 
 def middle_kernel(
-    factor, bias_ref, log_ref, kv0, kv1, kv2, kv1_first, kv2_first, qs_ref, gs_ref, rd_ref, dqt_ref, q_hbm, g_hbm, o_hbm,
-    gq_hbm, near_ref, far_ref, qs1_ref, g1_ref, o1_ref, probs_ref, win_ref, q_v, dq_v, sems,
+    factor, bias_ref, log_ref, kv0, kv2, kv1, qs_ref, gs_ref, rd_ref, dq_ref, q_hbm, g_hbm, o_hbm,
+    gq_hbm, near_ref, far_ref, qs1_ref, g1_ref, o1_ref, probs_ref, win_ref, q_v, sems,
 ):
     copies = [
         pltpu.make_async_copy(q_hbm.at[0, 1], q_v, sems.at[0]),
         pltpu.make_async_copy(g_hbm.at[0, 1], g1_ref, sems.at[1]),
         pltpu.make_async_copy(o_hbm.at[0, 1], o1_ref, sems.at[2]),
+        pltpu.make_async_copy(dq_ref, gq_hbm.at[0, 0], sems.at[3]),
     ]
     for copy in copies:
         copy.start()
     rows, size = kv1.shape[2], kv1.shape[3]
     heads = qs_ref.shape[0] // rows
-    bottom = lax.axis_index("section") == 0
-
-    def window(micro, which):
-        near = jnp.where(bottom, kv1_first[micro, which], kv1[micro, which])
-        far = jnp.where(bottom, kv2_first[micro, which], kv2[micro, which])
-        return jnp.concatenate([near, far], axis=0)
-
-    keys, values = window(0, 0), window(0, 1)
-    keys_t = keys.T
+    keys, values = joined((kv1, kv2), 0, 0), joined((kv1, kv2), 0, 1)
     bias = wider(bias_ref[...])
     log_rows, dot_rows = log_ref[0], rd_ref[...]
     step = PAIR * rows
@@ -182,10 +171,6 @@
         grad_scores = (probs * (dot(values, grad, NT) - head_rows(dot_rows, first))).astype(LOW)
         key_sum += dot(grad_scores, query)
         value_sum += dot(probs.astype(LOW), grad)
-        part = (dot(keys_t, grad_scores) + dqt_ref[:, cut]) * factor
-        dq_v[:, first * size : (first + PAIR) * size] = turned(part, rows).astype(LOW)
-    back = pltpu.make_async_copy(dq_v, gq_hbm.at[0, 0], sems.at[3])
-    back.start()
     key_sum = key_sum * factor
     for i, ref in enumerate((near_ref, far_ref)):
         ref[0] = key_sum[i * rows : (i + 1) * rows].astype(LOW)
@@ -193,17 +178,16 @@
     copies[0].wait()
     query = stacked(q_v[...], size)
     qs1_ref[...] = query
-    keys = jnp.concatenate([kv0[1, 0], window(1, 0)], axis=0)
+    keys = joined((kv0, kv1, kv2), 1, 0)
     win_ref[0] = keys
-    win_ref[1] = jnp.concatenate([kv0[1, 1], window(1, 1)], axis=0)
+    win_ref[1] = joined((kv0, kv1, kv2), 1, 1)
     log_rows = log_ref[1]
     for first in range(0, heads, PAIR):
         cut = slice(first * rows, first * rows + step)
         scores = dot(keys, query[cut], NT)
         probs_ref[:, cut] = jnp.exp(scores * factor + (bias - head_rows(log_rows, first)))
-    copies[1].wait()
-    copies[2].wait()
-    back.wait()
+    for copy in copies[1:]:
+        copy.wait()
 
 
 def others_kernel(factor, win_ref, qs_ref, g_ref, o_ref, probs_ref, near0, far0, r_ref, near_ref, far_ref, up_ref, gs_ref):
@@ -239,7 +223,7 @@
     back.wait()
 
 
-def sum_kernel(own0, own1, near, far, gk_ref, gv_ref):
+def sum_kernel(own0, own1, far, near, gk_ref, gv_ref):
     for micro, own in enumerate((own0, own1)):
         for which, ref in ((0, gk_ref), (1, gv_ref)):
             total = own[which] + near[micro, which].astype(WIDE) + far[micro, which].astype(WIDE)
@@ -283,8 +267,7 @@
         for x in (query_in, grad_out, forward_out, log_sum, block_order)
     )
     kv0 = jnp.stack([key_in[0], value_in[0]], axis=1)
-    upper = range(1, lax.axis_size("section"))
-    kv2, kv1 = ring(kv0, 2, upper), ring(kv0, 1, upper)
+    kv2, kv1 = ring(kv0, 2), ring(kv0, 1)
     pair = (2, rows, size)
 
     qs, gs, rd, dqt, own0, bias, log = call(
@@ -307,17 +290,14 @@
     (part,) = call(
         functools.partial(query_kernel, factor),
         "query_part",
-        (bias, log, kv1, kv2, qs, gs, rd, dqt),
+        (bias, log, kv2, kv1, qs, gs, rd, dqt),
         [low(rows, width)],
     )
     received = down(part)
-    late, _ = lax.optimization_barrier((kv0, part))
-    kv2_first, kv1_first = ring(late, 2, (0,)), ring(late, 1, (0,))
-
     grad_query, near0, far0, qs1, g1, o1, probs, win = call(
         functools.partial(middle_kernel, factor),
         "middle_terms",
-        (bias, log, kv0, kv1, kv2, kv1_first, kv2_first, qs, gs, rd, dqt, query_in, grad_out, forward_out),
+        (bias, log, kv0, kv2, kv1, qs, gs, rd, part, query_in, grad_out, forward_out),
         [
             low(*query_in.shape),
             low(*pair),
@@ -328,9 +308,9 @@
             wide(near_rows, heads * rows),
             low(2, near_rows, size),
         ],
-        in_specs=[VM] * 11 + [HB] * 3,
+        in_specs=[VM] * 9 + [HB] * 3,
         out_specs=[HB] + [VM] * 7,
-        scratch=[pltpu.VMEM((rows, width), LOW)] * 2 + [dma((4,))],
+        scratch=[pltpu.VMEM((rows, width), LOW), dma((4,))],
         share=0.001,
     )
 
@@ -355,7 +335,7 @@
     grad_key, grad_value = call(
         sum_kernel,
         "sums",
-        (own0, own1, near, far),
+        (own0, own1, far, near),
         [low(1, 2, rows, size)] * 2,
         share=0.01,
     )

time: 50.9 us -> 58.3 us (1.15)
  starting transfers between devices: 24.4 us -> 30.3 us
  waiting for transfers between devices: 14.9 us -> 16.8 us
    ppermute x2 -> x4, starting transfers between devices: 13.9 us -> 29 us  [ring(): lax.ppermute(value, 'ctx', [(i, (i + steps) % count) for i in range(count)])]
    ppermute x4 -> x0, waiting for transfers between devices: 10.9 us -> none  [ring(): return lax.ppermute(value, ('ctx', 'section'), route)]
    ppermute x4 -> x0, starting transfers between devices: 9.22 us -> none  [ring(): return lax.ppermute(value, ('ctx', 'section'), route)]
    ppermute x1, waiting for transfers between devices: 0.01 us -> 6.67 us  [down(): return lax.ppermute(value, 'section', [(i, i - 1) for i in range(1, count)])]
    ppermute x2 -> x4, waiting for transfers between devices: 3.93 us -> 10.1 us  [ring(): lax.ppermute(value, 'ctx', [(i, (i + steps) % count) for i in range(count)])]
  transfers between devices with their start and end apart: 7 -> 5, of which waited for: 3 -> 3; matrix products, arithmetic and copies ran while one was open for 0% -> 0% of each run, Pallas kernels for 13% -> 11%
where the time goes in v4:
time: 58.3 us; the launch traced here: 58 us
  starting transfers between devices  30.3 us (52%)
  waiting for transfers between devices  16.8 us (29%)
  Pallas kernels  9.37 us (16%)
  other arithmetic  0.89 us (2%)
  between operations  0.72 us (1%)
    ppermute x4, starting transfers between devices, ring(): lax.ppermute(value, 'ctx', [(i, (i + steps) % count) for i in range(count)])  29 us
    ppermute x4, waiting for transfers between devices, ring(): lax.ppermute(value, 'ctx', [(i, (i + steps) % count) for i in range(count)])  10.1 us
    pallas_call x6, Pallas kernels, call(): pl.pallas_call(body, in_specs=in_specs or [VM] * len(ins), out_specs=out_...  9.37 us
    ppermute x1, waiting for transfers between devices, down(): return lax.ppermute(value, 'section', [(i, i - 1) for i in range(1, count)])  6.67 us
    ppermute x1, starting transfers between devices, down(): return lax.ppermute(value, 'section', [(i, i - 1) for i in range(1, count)])  1.29 us
  transfers between devices with their start and end apart: 5, of which 3 were waited for; matrix products, arithmetic and copies ran while one was open for 0% of the time, Pallas kernels for 11%

profile of v4, /device:TPU:1, one launch (start us, length us, event | category | flops | bytes accessed | tf_op | source)
XLA Modules:
  0.0 58.0 jit_solution(10124936410801344851)
XLA Ops:
  0.6 0.9 %pad_maximum_fusion.kv_ref.kv0 = bf16[2,2,128,128]{3,2,1,0:T(8,128)(2,1)S(1)} fusion(bf16[2,1,128,128]{3,2,1,0:T(8,128)(2,1)} %bitcast.2, bf16[2,1,128,128]{3,2,1,0:T(8,128)(2,1)} %bitcast.3), kind=kLoop, calls=%fused_computation | loop fusion | flops 65536 | bytes 262144 | tf_op jit(solution)/shard_map/stack | solution.py:269
  1.5 4.0 %collective-permute-start = (bf16[2,2,128,128]{3,2,1,0:T(8,128)(2,1)S(1)}, bf16[2,2,128,128]{3,2,1,0:T(8,128)(2,1)S(1)}, u32[]{:S(2)}, u32[]{:S(2)}) collective-permute-start(bf16[2,2,128,128]{3,2,1,0:T(8,128)(2,1)S(1)} %pad_maximum_fusion.kv_ref.kv0), channel_id=1, source_target_pairs={{0,128},{64,192},{128,256},{192,320},{256,384},{320,448},{384,512}... | collective-permute-start | bytes 393224 | tf_op jit(solution)/shard_map/ppermute | solution.py:25
  5.6 3.8 %collective-permute-start.1 = (bf16[2,2,128,128]{3,2,1,0:T(8,128)(2,1)S(1)}, bf16[2,2,128,128]{3,2,1,0:T(8,128)(2,1)S(1)}, u32[]{:S(2)}, u32[]{:S(2)}) collective-permute-start(bf16[2,2,128,128]{3,2,1,0:T(8,128)(2,1)S(1)} %pad_maximum_fusion.kv_ref.kv0), channel_id=1, source_target_pairs={{0,64},{64,128},{128,192},{192,256},{256,320},{320,384},{384,448},... | collective-permute-start | bytes 393224 | tf_op jit(solution)/shard_map/ppermute | solution.py:25
  9.4 2.7 %own_terms.1 = (bf16[1024,128]{1,0:T(8,128)(2,1)S(1)}, bf16[1024,128]{1,0:T(8,128)(2,1)S(1)}, f32[8,128]{1,0:T(8,128)S(1)}, f32[128,1024]{1,0:T(8,128)S(1)}, f32...) custom-call(s32[32]{0:T(128)} %order_hbm.1, f32[1,2,8,128]{3,2,1,0:T(8,128)} %log_hbm.1, ...), custom_call_target="tpu_custom_call" | custom-call | flops 201326592 | bytes 1024 | tf_op jit(solution)/shard_map/own_terms/pallas_call | solution.py:252
  12.1 0.0 collective-permute-done.kv2
  12.2 8.2 %collective-permute-done.1.kv1 = bf16[2,2,128,128]{3,2,1,0:T(8,128)(2,1)S(1)} collective-permute-done((bf16[2,2,128,128]{3,2,1,0:T(8,128)(2,1)S(1)}, bf16[2,2,128,128]{3,2,1,0:T(8,128)(2,1)S(1)}, u32[]{:S(2)}, u32[]{:S(2)}) %collective-permute-start.1) | collective-permute-done | bytes 131104 | tf_op jit(solution)/shard_map/ppermute | solution.py:25
  20.4 1.1 %query_part.1.dq_ref = bf16[128,1024]{1,0:T(8,128)(2,1)S(1)} custom-call(f32[384,128]{1,0:T(8,128)S(1)} %get-tuple-element.26.bias_ref, f32[2,8,128]{2,1,0:T(8,128)S(1)} %get-tuple-element.27.log_ref, bf16[2,2,128,128]{3,2,1,0:T(8,128)(2,1)S(1)} %collective-permute-done.kv2, bf16[2,2,128,128]{3,2,1,0:T(8,128)(2,1)S(1)} %collective-permute-done.1.kv1, ...), custom_call_target="tpu_custom_call" | custom-call | flops 100663296 | bytes 1024 | tf_op jit(solution)/shard_map/query_part/pallas_call | solution.py:252
  21.5 1.3 %collective-permute-start.2 = (bf16[128,1024]{1,0:T(8,128)(2,1)S(1)}, bf16[128,1024]{1,0:T(8,128)(2,1)S(1)}, u32[]{:S(2)}, u32[]{:S(2)}) collective-permute-start(bf16[128,1024]{1,0:T(8,128)(2,1)S(1)} %query_part.1.dq_ref), channel_id=1, source_target_pairs={{1,0},{2,1},{3,2},{4,3},{5,4},{6,5},{7,6},{8,7},{9,8},{10,9},{11,1... | collective-permute-start | bytes 786440 | tf_op jit(solution)/shard_map/ppermute | solution.py:30
  22.8 2.4 %middle_terms.1 = (bf16[1,2,128,1024]{3,2,1,0:T(8,128)(2,1)}, bf16[2,128,128]{2,1,0:T(8,128)(2,1)S(1)}, bf16[2,128,128]{2,1,0:T(8,128)(2,1)S(1)}, bf16[1024,128]...) custom-call(f32[384,128]{1,0:T(8,128)S(1)} %get-tuple-element.26.bia, ...), custom_call_target="tpu_custom_call" | custom-call | flops 100663 | bytes 1024 | tf_op jit(solution)/shard_map/middle_terms/pallas_call | solution.py:252
  25.2 6.7 %collective-permute-done.2.r_ref = bf16[128,1024]{1,0:T(8,128)(2,1)S(1)} collective-permute-done((bf16[128,1024]{1,0:T(8,128)(2,1)S(1)}, bf16[128,1024]{1,0:T(8,128)(2,1)S(1)}, u32[]{:S(2)}, u32[]{:S(2)}) %collective-permute-start.2) | collective-permute-done | bytes 262176 | tf_op jit(solution)/shard_map/ppermute | solution.py:30
  31.8 1.3 %second_others.1 = (bf16[2,2,128,128]{3,2,1,0:T(8,128)(2,1)S(1)}, bf16[2,2,128,128]{3,2,1,0:T(8,128)(2,1)S(1)}, bf16[1024,128]{1,0:T(8,128)(2,1)S(1)}, bf16[384,1024]{1,0:T(8,128)(2,1)S(1)}) custom-call(bf16[2,384,128]{2,1,0:T(8,128)(2,1)S(1)} %get-tuple-element.32.win_ref, bf16[1024,128]{1,0:T(8,128)(2,1)S(1)} %get-tuple-element.33.qs_ref, ...), custom_call_target="tpu_custom_call" | custom-call | flops 201326592 | bytes 1024 | tf_op jit(solution)/shard_map/second_others/pallas_call | solution.py:252
  33.2 17.9 %collective-permute-start.3 = (bf16[2,2,128,128]{3,2,1,0:T(8,128)(2,1)S(1)}, bf16[2,2,128,128]{3,2,1,0:T(8,128)(2,1)S(1)}, u32[]{:S(2)}, u32[]{:S(2)}) collective-permute-start(bf16[2,2,128,128]{3,2,1,0:T(8,128)(2,1)S(1)} %get-tuple-element.45), channel_id=1, source_target_pairs={{0,896},{64,960},{128,0},{192,64},{256,128},{320,192},{384,256},{4... | collective-permute-start | bytes 393224 | tf_op jit(solution)/shard_map/ppermute | solution.py:25
  51.0 3.2 %collective-permute-start.4 = (bf16[2,2,128,128]{3,2,1,0:T(8,128)(2,1)S(1)}, bf16[2,2,128,128]{3,2,1,0:T(8,128)(2,1)S(1)}, u32[]{:S(2)}, u32[]{:S(2)}) collective-permute-start(bf16[2,2,128,128]{3,2,1,0:T(8,128)(2,1)S(1)} %get-tuple-element.46), channel_id=1, source_target_pairs={{0,960},{64,0},{128,64},{192,128},{256,192},{320,256},{384,320},{4... | collective-permute-start | bytes 393224 | tf_op jit(solution)/shard_map/ppermute | solution.py:25
  54.3 1.1 %second_rest.1 = (f32[2,128,128]{2,1,0:T(8,128)S(1)}, bf16[1,2,128,1024]{3,2,1,0:T(8,128)(2,1)}) custom-call(bf16[2,384,128]{2,1,0:T(8,128)(2,1)S(1)} %get-tuple-element.32.win_ref, bf16[1024,128]{1,0:T(8,128)(2,1)S(1)} %get-tuple-element.33.qs_ref, f32[384,1024]{1,0:T(8,128)S(1)} %get-tuple-element.34.probs_ref, ...), custom_call_target="tpu_custom_call", output_to_operand_aliasing={{1}: (5, {})} | custom-call | flops 100663296 | bytes 1024 | tf_op jit(solution)/shard_map/second_rest/pallas_call | solution.py:252
  55.4 0.0 collective-permute-done.3.far
  55.5 1.9 %collective-permute-done.4.near = bf16[2,2,128,128]{3,2,1,0:T(8,128)(2,1)S(1)} collective-permute-done((bf16[2,2,128,128]{3,2,1,0:T(8,128)(2,1)S(1)}, bf16[2,2,128,128]{3,2,1,0:T(8,128)(2,1)S(1)}, u32[]{:S(2)}, u32[]{:S(2)}) %collective-permute-start.4) | collective-permute-done | bytes 131104 | tf_op jit(solution)/shard_map/ppermute | solution.py:25
  57.3 0.7 %sums.1 = (bf16[1,2,128,128]{3,2,1,0:T(8,128)(2,1)}, bf16[1,2,128,128]{3,2,1,0:T(8,128)(2,1)}) custom-call(f32[2,128,128]{2,1,0:T(8,128)S(1)} %get-tuple-element.43.own0, f32[2,128,128]{2,1,0:T(8,128)S(1)} %get-tuple-element.44.own1, bf16[2,2,128,128]{3,2,1,0:T(8,128)(2,1)S(1)} %collective-permute-done.3.far, ...), custom_call_target="tpu_custom_call" | custom-call | flops 1006632 | bytes 1024 | tf_op jit(solution)/shard_map/sums/pallas_call | solution.py:252
Async XLA Ops:
  1.5 10.6 %collective-permute-start = (bf16[2,2,128,128]{3,2,1,0:T(8,128)(2,1)S(1)}, bf16[2,2,128,128]{3,2,1,0:T(8,128)(2,1)S(1)}, u32[]{:S(2)}, u32[]{:S(2)}) collective-permute-start(bf16[2,2,128,128]{3,2,1,0:T(8,128)(2,1)S(1)} %pad_maximum_fusion.kv_ref.kv0), channel_id=1, source_target_pairs={{0,128},{64,192},{128,256},{192,320},{256,384},{320,448},{384,512}... | collective-permute-start | bytes 393224 | tf_op jit(solution)/shard_map/ppermute | solution.py:25
  5.6 14.8 %collective-permute-start.1 = (bf16[2,2,128,128]{3,2,1,0:T(8,128)(2,1)S(1)}, bf16[2,2,128,128]{3,2,1,0:T(8,128)(2,1)S(1)}, u32[]{:S(2)}, u32[]{:S(2)}) collective-permute-start(bf16[2,2,128,128]{3,2,1,0:T(8,128)(2,1)S(1)} %pad_maximum_fusion.kv_ref.kv0), channel_id=1, source_target_pairs={{0,64},{64,128},{128,192},{192,256},{256,320},{320,384},{384,448},... | collective-permute-start | bytes 393224 | tf_op jit(solution)/shard_map/ppermute | solution.py:25
  21.5 10.3 %collective-permute-start.2 = (bf16[128,1024]{1,0:T(8,128)(2,1)S(1)}, bf16[128,1024]{1,0:T(8,128)(2,1)S(1)}, u32[]{:S(2)}, u32[]{:S(2)}) collective-permute-start(bf16[128,1024]{1,0:T(8,128)(2,1)S(1)} %query_part.1.dq_ref), channel_id=1, source_target_pairs={{1,0},{2,1},{3,2},{4,3},{5,4},{6,5},{7,6},{8,7},{9,8},{10,9},{11,1... | collective-permute-start | bytes 786440 | tf_op jit(solution)/shard_map/ppermute | solution.py:30
  33.2 22.3 %collective-permute-start.3 = (bf16[2,2,128,128]{3,2,1,0:T(8,128)(2,1)S(1)}, bf16[2,2,128,128]{3,2,1,0:T(8,128)(2,1)S(1)}, u32[]{:S(2)}, u32[]{:S(2)}) collective-permute-start(bf16[2,2,128,128]{3,2,1,0:T(8,128)(2,1)S(1)} %get-tuple-element.45), channel_id=1, source_target_pairs={{0,896},{64,960},{128,0},{192,64},{256,128},{320,192},{384,256},{4... | collective-permute-start | bytes 393224 | tf_op jit(solution)/shard_map/ppermute | solution.py:25
  51.0 6.3 %collective-permute-start.4 = (bf16[2,2,128,128]{3,2,1,0:T(8,128)(2,1)S(1)}, bf16[2,2,128,128]{3,2,1,0:T(8,128)(2,1)S(1)}, u32[]{:S(2)}, u32[]{:S(2)}) collective-permute-start(bf16[2,2,128,128]{3,2,1,0:T(8,128)(2,1)S(1)} %get-tuple-element.46), channel_id=1, source_target_pairs={{0,960},{64,0},{128,64},{192,128},{256,192},{320,256},{384,320},{4... | collective-permute-start | bytes 393224 | tf_op jit(solution)/shard_map/ppermute | solution.py:25

commit v5 on v3

--- a/solution.py
+++ b/solution.py
@@ -87,7 +87,7 @@
 
 def own_kernel(
     factor, order_hbm, log_hbm, kv_ref, q_hbm, g_hbm, o_hbm,
-    qs_ref, gs_ref, rd_ref, dqt_ref, own_ref, bias_ref, log_ref, order_s, q_v, g_v, o_v, sems,
+    qs_ref, gs_ref, rd_ref, dqt_ref, bias_ref, log_ref, order_s, q_v, g_v, o_v, sems,
 ):
     copies = [
         pltpu.make_async_copy(source, target, sems.at[i])
@@ -120,38 +120,38 @@
     query = stacked(q_v[...], size)
     qs_ref[...] = query
     copies[4].wait()
-    log_rows = log_ref[0]
-    step = PAIR * rows
-    key_sum = value_sum = 0.0
-    for first in range(0, query.shape[0] // rows, PAIR):
-        cut = slice(first * rows, first * rows + step)
-        probs = jnp.exp(dot(keys, query[cut], NT) * factor + (bias - head_rows(log_rows, first)))
-        grad_scores = (probs * (dot(values, grad[cut], NT) - head_rows(dot_rows, first))).astype(LOW)
-        dqt_ref[:, cut] = dot(keys_t, grad_scores)
-        key_sum += dot(grad_scores, query[cut])
-        value_sum += dot(probs.astype(LOW), grad[cut])
-    own_ref[0] = key_sum * factor
-    own_ref[1] = value_sum
+
+    @pl.when(lax.axis_index("section") > 0)
+    def _():
+        log_rows = log_ref[0]
+        step = PAIR * rows
+        for first in range(0, query.shape[0] // rows, PAIR):
+            cut = slice(first * rows, first * rows + step)
+            probs = jnp.exp(dot(keys, query[cut], NT) * factor + (bias - head_rows(log_rows, first)))
+            grad_scores = (probs * (dot(values, grad[cut], NT) - head_rows(dot_rows, first))).astype(LOW)
+            dqt_ref[:, cut] = dot(keys_t, grad_scores)
 
 
 def query_kernel(factor, bias_ref, log_ref, kv1, kv2, qs_ref, gs_ref, rd_ref, dqt_ref, dq_ref):
-    rows, size = kv1.shape[2], kv1.shape[3]
-    keys, values = joined((kv1, kv2), 0, 0), joined((kv1, kv2), 0, 1)
-    keys_t = keys.T
-    bias = wider(bias_ref[rows:])
-    log_rows, dot_rows = log_ref[0], rd_ref[...]
-    step = PAIR * rows
-    for first in range(0, dq_ref.shape[1] // size, PAIR):
-        cut = slice(first * rows, first * rows + step)
-        probs = jnp.exp(dot(keys, qs_ref[cut], NT) * factor + (bias - head_rows(log_rows, first)))
-        grad_scores = (probs * (dot(values, gs_ref[cut], NT) - head_rows(dot_rows, first))).astype(LOW)
-        part = (dot(keys_t, grad_scores) + dqt_ref[:, cut]) * factor
-        dq_ref[:, first * size : (first + PAIR) * size] = turned(part, rows).astype(LOW)
+    @pl.when(lax.axis_index("section") > 0)
+    def _():
+        rows, size = kv1.shape[2], kv1.shape[3]
+        keys, values = joined((kv1, kv2), 0, 0), joined((kv1, kv2), 0, 1)
+        keys_t = keys.T
+        bias = wider(bias_ref[rows:])
+        log_rows, dot_rows = log_ref[0], rd_ref[...]
+        step = PAIR * rows
+        for first in range(0, dq_ref.shape[1] // size, PAIR):
+            cut = slice(first * rows, first * rows + step)
+            probs = jnp.exp(dot(keys, qs_ref[cut], NT) * factor + (bias - head_rows(log_rows, first)))
+            grad_scores = (probs * (dot(values, gs_ref[cut], NT) - head_rows(dot_rows, first))).astype(LOW)
+            part = (dot(keys_t, grad_scores) + dqt_ref[:, cut]) * factor
+            dq_ref[:, first * size : (first + PAIR) * size] = turned(part, rows).astype(LOW)
 
 
 def middle_kernel(
-    factor, bias_ref, log_ref, kv0, kv1, kv2, kv1_first, kv2_first, qs_ref, gs_ref, rd_ref, dqt_ref, q_hbm, g_hbm, o_hbm,
-    gq_hbm, near_ref, far_ref, qs1_ref, g1_ref, o1_ref, probs_ref, win_ref, q_v, dq_v, sems,
+    factor, bias_ref, log_ref, kv0, kv1, kv2, kv1_first, kv2_first, qs_ref, gs_ref, rd_ref, q_hbm, g_hbm, o_hbm,
+    gq_hbm, own_ref, near_ref, far_ref, qs1_ref, g1_ref, o1_ref, probs_ref, win_ref, q_v, dq_v, sems,
 ):
     copies = [
         pltpu.make_async_copy(q_hbm.at[0, 1], q_v, sems.at[0]),
@@ -167,7 +167,7 @@
     def window(micro, which):
         near = jnp.where(bottom, kv1_first[micro, which], kv1[micro, which])
         far = jnp.where(bottom, kv2_first[micro, which], kv2[micro, which])
-        return jnp.concatenate([near, far], axis=0)
+        return jnp.concatenate([kv0[micro, which], near, far], axis=0)
 
     keys, values = window(0, 0), window(0, 1)
     keys_t = keys.T
@@ -178,24 +178,24 @@
     for first in range(0, heads, PAIR):
         cut = slice(first * rows, first * rows + step)
         query, grad = qs_ref[cut], gs_ref[cut]
-        probs = jnp.exp(dot(keys, query, NT) * factor + (bias[rows:] - head_rows(log_rows, first)))
+        probs = jnp.exp(dot(keys, query, NT) * factor + (bias - head_rows(log_rows, first)))
         grad_scores = (probs * (dot(values, grad, NT) - head_rows(dot_rows, first))).astype(LOW)
         key_sum += dot(grad_scores, query)
         value_sum += dot(probs.astype(LOW), grad)
-        part = (dot(keys_t, grad_scores) + dqt_ref[:, cut]) * factor
+        part = dot(keys_t, grad_scores) * factor
         dq_v[:, first * size : (first + PAIR) * size] = turned(part, rows).astype(LOW)
     back = pltpu.make_async_copy(dq_v, gq_hbm.at[0, 0], sems.at[3])
     back.start()
     key_sum = key_sum * factor
-    for i, ref in enumerate((near_ref, far_ref)):
-        ref[0] = key_sum[i * rows : (i + 1) * rows].astype(LOW)
-        ref[1] = value_sum[i * rows : (i + 1) * rows].astype(LOW)
+    for i, ref in enumerate((own_ref, near_ref, far_ref)):
+        ref[0] = key_sum[i * rows : (i + 1) * rows].astype(ref.dtype)
+        ref[1] = value_sum[i * rows : (i + 1) * rows].astype(ref.dtype)
     copies[0].wait()
     query = stacked(q_v[...], size)
     qs1_ref[...] = query
-    keys = jnp.concatenate([kv0[1, 0], window(1, 0)], axis=0)
+    keys = window(1, 0)
     win_ref[0] = keys
-    win_ref[1] = jnp.concatenate([kv0[1, 1], window(1, 1)], axis=0)
+    win_ref[1] = window(1, 1)
     log_rows = log_ref[1]
     for first in range(0, heads, PAIR):
         cut = slice(first * rows, first * rows + step)
@@ -239,7 +239,7 @@
     back.wait()
 
 
-def sum_kernel(own0, own1, near, far, gk_ref, gv_ref):
+def sum_kernel(own0, own1, far, near, gk_ref, gv_ref):
     for micro, own in enumerate((own0, own1)):
         for which, ref in ((0, gk_ref), (1, gv_ref)):
             total = own[which] + near[micro, which].astype(WIDE) + far[micro, which].astype(WIDE)
@@ -285,9 +285,10 @@
     kv0 = jnp.stack([key_in[0], value_in[0]], axis=1)
     upper = range(1, lax.axis_size("section"))
     kv2, kv1 = ring(kv0, 2, upper), ring(kv0, 1, upper)
+    kv2_first, kv1_first = ring(kv0, 2, (0,)), ring(kv0, 1, (0,))
     pair = (2, rows, size)
 
-    qs, gs, rd, dqt, own0, bias, log = call(
+    qs, gs, rd, dqt, bias, log = call(
         functools.partial(own_kernel, factor),
         "own_terms",
         (block_order, log_sum, kv0, query_in, grad_out, forward_out),
@@ -296,7 +297,6 @@
             low(heads * rows, size),
             wide(8, rows),
             wide(size, heads * rows),
-            wide(*pair),
             wide(near_rows, rows),
             wide(2, heads, rows),
         ],
@@ -311,15 +311,14 @@
         [low(rows, width)],
     )
     received = down(part)
-    late, _ = lax.optimization_barrier((kv0, part))
-    kv2_first, kv1_first = ring(late, 2, (0,)), ring(late, 1, (0,))
-
-    grad_query, near0, far0, qs1, g1, o1, probs, win = call(
+
+    grad_query, own0, near0, far0, qs1, g1, o1, probs, win = call(
         functools.partial(middle_kernel, factor),
         "middle_terms",
-        (bias, log, kv0, kv1, kv2, kv1_first, kv2_first, qs, gs, rd, dqt, query_in, grad_out, forward_out),
+        (bias, log, kv0, kv1, kv2, kv1_first, kv2_first, qs, gs, rd, query_in, grad_out, forward_out),
         [
             low(*query_in.shape),
+            wide(*pair),
             low(*pair),
             low(*pair),
             low(heads * rows, size),
@@ -328,8 +327,8 @@
             wide(near_rows, heads * rows),
             low(2, near_rows, size),
         ],
-        in_specs=[VM] * 11 + [HB] * 3,
-        out_specs=[HB] + [VM] * 7,
+        in_specs=[VM] * 10 + [HB] * 3,
+        out_specs=[HB] + [VM] * 8,
         scratch=[pltpu.VMEM((rows, width), LOW)] * 2 + [dma((4,))],
         share=0.001,
     )
@@ -355,7 +354,7 @@
     grad_key, grad_value = call(
         sum_kernel,
         "sums",
-        (own0, own1, near, far),
+        (own0, own1, far, near),
         [low(1, 2, rows, size)] * 2,
         share=0.01,
     )

time: 50.9 us -> 49.3 us (0.969)
  Pallas kernels: 9.59 us -> 7.02 us
  starting transfers between devices: 24.4 us -> 25.2 us
    pallas_call x6, Pallas kernels: 9.59 us -> 7.02 us  [call(): pl.pallas_call(body, in_specs=in_specs or [VM] * len(ins), out_specs=out_...]
    ppermute x1, waiting for transfers between devices: 0.01 us -> 1.03 us  [down(): return lax.ppermute(value, 'section', [(i, i - 1) for i in range(1, count)])]
    ppermute x2, waiting for transfers between devices: 3.93 us -> 3.1 us  [ring(): lax.ppermute(value, 'ctx', [(i, (i + steps) % count) for i in range(count)])]
    ppermute x2, starting transfers between devices: 13.9 us -> 14.7 us  [ring(): lax.ppermute(value, 'ctx', [(i, (i + steps) % count) for i in range(count)])]
  transfers between devices with their start and end apart: 7 -> 7, of which waited for: 3 -> 4; matrix products, arithmetic and copies ran while one was open for 0% -> 0% of each run, Pallas kernels for 13% -> 10%
where the time goes in v5:
time: 49.3 us; the launch traced here: 49 us
  starting transfers between devices  25.2 us (51%)
  waiting for transfers between devices  15.1 us (31%)
  Pallas kernels  7.02 us (14%)
  other arithmetic  0.89 us (2%)
  between operations  0.75 us (2%)
    ppermute x2, starting transfers between devices, ring(): lax.ppermute(value, 'ctx', [(i, (i + steps) % count) for i in range(count)])  14.7 us
    ppermute x4, waiting for transfers between devices, ring(): return lax.ppermute(value, ('ctx', 'section'), route)  10.9 us
    ppermute x4, starting transfers between devices, ring(): return lax.ppermute(value, ('ctx', 'section'), route)  9.22 us
    pallas_call x6, Pallas kernels, call(): pl.pallas_call(body, in_specs=in_specs or [VM] * len(ins), out_specs=out_...  7.02 us
    ppermute x2, waiting for transfers between devices, ring(): lax.ppermute(value, 'ctx', [(i, (i + steps) % count) for i in range(count)])  3.1 us
    ppermute x1, starting transfers between devices, down(): return lax.ppermute(value, 'section', [(i, i - 1) for i in range(1, count)])  1.29 us
    ppermute x1, waiting for transfers between devices, down(): return lax.ppermute(value, 'section', [(i, i - 1) for i in range(1, count)])  1.03 us
  transfers between devices with their start and end apart: 7, of which 4 were waited for; matrix products, arithmetic and copies ran while one was open for 0% of the time, Pallas kernels for 10%

profile of v5, /device:TPU:1, one launch (start us, length us, event | category | flops | bytes accessed | tf_op | source)
XLA Modules:
  0.0 49.0 jit_solution(17129810168650438767)
XLA Ops:
  0.6 0.9 %pad_maximum_fusion.kv_ref.kv0 = bf16[2,2,128,128]{3,2,1,0:T(8,128)(2,1)S(1)} fusion(bf16[2,1,128,128]{3,2,1,0:T(8,128)(2,1)} %bitcast.2, bf16[2,1,128,128]{3,2,1,0:T(8,128)(2,1)} %bitcast.3), kind=kLoop, calls=%fused_computation | loop fusion | flops 65536 | bytes 262144 | tf_op jit(solution)/shard_map/stack | solution.py:285
  1.5 0.7 %collective-permute-start.1 = (bf16[2,2,128,128]{3,2,1,0:T(8,128)(2,1)S(1)}, bf16[2,2,128,128]{3,2,1,0:T(8,128)(2,1)S(1)}, u32[]{:S(2)}, u32[]{:S(2)}) collective-permute-start(bf16[2,2,128,128]{3,2,1,0:T(8,128)(2,1)S(1)} %pad_maximum_fusion.kv_ref.kv0), channel_id=1, source_target_pairs={{1,129},{65,193},{129,257},{193,321},{257,385},{321,449},{385,513}... | collective-permute-start | bytes 393224 | tf_op jit(solution)/shard_map/ppermute | solution.py:29
  2.2 0.7 %collective-permute-start = (bf16[2,2,128,128]{3,2,1,0:T(8,128)(2,1)S(1)}, bf16[2,2,128,128]{3,2,1,0:T(8,128)(2,1)S(1)}, u32[]{:S(2)}, u32[]{:S(2)}) collective-permute-start(bf16[2,2,128,128]{3,2,1,0:T(8,128)(2,1)S(1)} %pad_maximum_fusion.kv_ref.kv0), channel_id=1, source_target_pairs={{1,65},{65,129},{129,193},{193,257},{257,321},{321,385},{385,449},... | collective-permute-start | bytes 393224 | tf_op jit(solution)/shard_map/ppermute | solution.py:29
  2.9 1.4 %own_terms.1 = (bf16[1024,128]{1,0:T(8,128)(2,1)S(1)}, bf16[1024,128]{1,0:T(8,128)(2,1)S(1)}, f32[8,128]{1,0:T(8,128)S(1)}, f32[128,1024]{1,0:T(8,128)S(1)}, f32...) custom-call(s32[32]{0:T(128)} %order_hbm.1, f32[1,2,8,128]{3,2,1,0:T(8,128)} %log_hbm.1, ...), custom_call_target="tpu_custom_call" | custom-call | flops 201326592 | bytes 1024 | tf_op jit(solution)/shard_map/own_terms/pallas_call | solution.py:268
  4.3 0.0 collective-permute-done.1.kv2
  4.3 0.0 collective-permute-done.kv1
  4.4 1.3 %collective-permute-start.4 = (bf16[128,1024]{1,0:T(8,128)(2,1)S(1)}, bf16[128,1024]{1,0:T(8,128)(2,1)S(1)}, u32[]{:S(2)}, u32[]{:S(2)}) collective-permute-start(bf16[128,1024]{1,0:T(8,128)(2,1)S(1)} %query_part.1), channel_id=1, source_target_pairs={{1,0},{2,1},{3,2},{4,3},{5,4},{6,5},{7,6},{8,7},{9,8},{10,9},{11,1... | collective-permute-start | bytes 786440 | tf_op jit(solution)/shard_map/ppermute | solution.py:34
  5.7 4.0 %collective-permute-start.3 = (bf16[2,2,128,128]{3,2,1,0:T(8,128)(2,1)S(1)}, bf16[2,2,128,128]{3,2,1,0:T(8,128)(2,1)S(1)}, u32[]{:S(2)}, u32[]{:S(2)}) collective-permute-start(bf16[2,2,128,128]{3,2,1,0:T(8,128)(2,1)S(1)} %pad_maximum_fusion.kv_ref.kv0), channel_id=1, source_target_pairs={{0,128},{64,192},{128,256},{192,320},{256,384},{320,448},{384,512}... | collective-permute-start | bytes 393224 | tf_op jit(solution)/shard_map/ppermute | solution.py:29
  9.7 3.8 %collective-permute-start.2 = (bf16[2,2,128,128]{3,2,1,0:T(8,128)(2,1)S(1)}, bf16[2,2,128,128]{3,2,1,0:T(8,128)(2,1)S(1)}, u32[]{:S(2)}, u32[]{:S(2)}) collective-permute-start(bf16[2,2,128,128]{3,2,1,0:T(8,128)(2,1)S(1)} %pad_maximum_fusion.kv_ref.kv0), channel_id=1, source_target_pairs={{0,64},{64,128},{128,192},{192,256},{256,320},{320,384},{384,448},... | collective-permute-start | bytes 393224 | tf_op jit(solution)/shard_map/ppermute | solution.py:29
  13.6 0.7 %collective-permute-done.3.kv2_first = bf16[2,2,128,128]{3,2,1,0:T(8,128)(2,1)S(1)} collective-permute-done((bf16[2,2,128,128]{3,2,1,0:T(8,128)(2,1)S(1)}, bf16[2,2,128,128]{3,2,1,0:T(8,128)(2,1)S(1)}, u32[]{:S(2)}, u32[]{:S(2)}) %collective-permute-start.3) | collective-permute-done | bytes 131104 | tf_op jit(solution)/shard_map/ppermute | solution.py:29
  14.2 10.2 %collective-permute-done.2.kv1_first = bf16[2,2,128,128]{3,2,1,0:T(8,128)(2,1)S(1)} collective-permute-done((bf16[2,2,128,128]{3,2,1,0:T(8,128)(2,1)S(1)}, bf16[2,2,128,128]{3,2,1,0:T(8,128)(2,1)S(1)}, u32[]{:S(2)}, u32[]{:S(2)}) %collective-permute-start.2) | collective-permute-done | bytes 131104 | tf_op jit(solution)/shard_map/ppermute | solution.py:29
  24.5 2.4 %middle_terms.1 = (bf16[1,2,128,1024]{3,2,1,0:T(8,128)(2,1)}, f32[2,128,128]{2,1,0:T(8,128)S(1)}, bf16[2,128,128]{2,1,0:T(8,128)(2,1)S(1)}, bf16[2,128,128]{2,1,...) custom-call(f32[384,128]{1,0:T(8,128)S(1)} %get-tuple-element.26.bia, ...), custom_call_target="tpu_custom_call" | custom-call | flops 100663 | bytes 1024 | tf_op jit(solution)/shard_map/middle_terms/pallas_call | solution.py:268
  26.9 1.0 %collective-permute-done.4.r_ref = bf16[128,1024]{1,0:T(8,128)(2,1)S(1)} collective-permute-done((bf16[128,1024]{1,0:T(8,128)(2,1)S(1)}, bf16[128,1024]{1,0:T(8,128)(2,1)S(1)}, u32[]{:S(2)}, u32[]{:S(2)}) %collective-permute-start.4) | collective-permute-done | bytes 262176 | tf_op jit(solution)/shard_map/ppermute | solution.py:34
  27.9 1.3 %second_others.1 = (bf16[2,2,128,128]{3,2,1,0:T(8,128)(2,1)S(1)}, bf16[2,2,128,128]{3,2,1,0:T(8,128)(2,1)S(1)}, bf16[1024,128]{1,0:T(8,128)(2,1)S(1)}, bf16[384,1024]{1,0:T(8,128)(2,1)S(1)}) custom-call(bf16[2,384,128]{2,1,0:T(8,128)(2,1)S(1)} %get-tuple-element.31.win_ref, bf16[1024,128]{1,0:T(8,128)(2,1)S(1)} %get-tuple-element.32.qs_ref, ...), custom_call_target="tpu_custom_call" | custom-call | flops 201326592 | bytes 1024 | tf_op jit(solution)/shard_map/second_others/pallas_call | solution.py:268
  29.3 11.7 %collective-permute-start.5 = (bf16[2,2,128,128]{3,2,1,0:T(8,128)(2,1)S(1)}, bf16[2,2,128,128]{3,2,1,0:T(8,128)(2,1)S(1)}, u32[]{:S(2)}, u32[]{:S(2)}) collective-permute-start(bf16[2,2,128,128]{3,2,1,0:T(8,128)(2,1)S(1)} %get-tuple-element.45), channel_id=1, source_target_pairs={{0,896},{64,960},{128,0},{192,64},{256,128},{320,192},{384,256},{4... | collective-permute-start | bytes 393224 | tf_op jit(solution)/shard_map/ppermute | solution.py:26
  41.0 3.1 %collective-permute-start.6 = (bf16[2,2,128,128]{3,2,1,0:T(8,128)(2,1)S(1)}, bf16[2,2,128,128]{3,2,1,0:T(8,128)(2,1)S(1)}, u32[]{:S(2)}, u32[]{:S(2)}) collective-permute-start(bf16[2,2,128,128]{3,2,1,0:T(8,128)(2,1)S(1)} %get-tuple-element.46), channel_id=1, source_target_pairs={{0,960},{64,0},{128,64},{192,128},{256,192},{320,256},{384,320},{4... | collective-permute-start | bytes 393224 | tf_op jit(solution)/shard_map/ppermute | solution.py:26
  44.0 1.1 %second_rest.1 = (f32[2,128,128]{2,1,0:T(8,128)S(1)}, bf16[1,2,128,1024]{3,2,1,0:T(8,128)(2,1)}) custom-call(bf16[2,384,128]{2,1,0:T(8,128)(2,1)S(1)} %get-tuple-element.31.win_ref, bf16[1024,128]{1,0:T(8,128)(2,1)S(1)} %get-tuple-element.32.qs_ref, f32[384,1024]{1,0:T(8,128)S(1)} %get-tuple-element.33.probs_ref, ...), custom_call_target="tpu_custom_call", output_to_operand_aliasing={{1}: (5, {})} | custom-call | flops 100663296 | bytes 1024 | tf_op jit(solution)/shard_map/second_rest/pallas_call | solution.py:268
  45.2 0.0 collective-permute-done.5.far
  45.2 3.1 %collective-permute-done.6.near = bf16[2,2,128,128]{3,2,1,0:T(8,128)(2,1)S(1)} collective-permute-done((bf16[2,2,128,128]{3,2,1,0:T(8,128)(2,1)S(1)}, bf16[2,2,128,128]{3,2,1,0:T(8,128)(2,1)S(1)}, u32[]{:S(2)}, u32[]{:S(2)}) %collective-permute-start.6) | collective-permute-done | bytes 131104 | tf_op jit(solution)/shard_map/ppermute | solution.py:26
  48.3 0.7 %sums.1 = (bf16[1,2,128,128]{3,2,1,0:T(8,128)(2,1)}, bf16[1,2,128,128]{3,2,1,0:T(8,128)(2,1)}) custom-call(f32[2,128,128]{2,1,0:T(8,128)S(1)} %get-tuple-element.43.own0, f32[2,128,128]{2,1,0:T(8,128)S(1)} %get-tuple-element.44.own1, bf16[2,2,128,128]{3,2,1,0:T(8,128)(2,1)S(1)} %collective-permute-done.5.far, ...), custom_call_target="tpu_custom_call" | custom-call | flops 1006632 | bytes 1024 | tf_op jit(solution)/shard_map/sums/pallas_call | solution.py:268
  (1 shorter events, 0.0 us)
Async XLA Ops:
  1.5 2.8 %collective-permute-start.1 = (bf16[2,2,128,128]{3,2,1,0:T(8,128)(2,1)S(1)}, bf16[2,2,128,128]{3,2,1,0:T(8,128)(2,1)S(1)}, u32[]{:S(2)}, u32[]{:S(2)}) collective-permute-start(bf16[2,2,128,128]{3,2,1,0:T(8,128)(2,1)S(1)} %pad_maximum_fusion.kv_ref.kv0), channel_id=1, source_target_pairs={{1,129},{65,193},{129,257},{193,321},{257,385},{321,449},{385,513}... | collective-permute-start | bytes 393224 | tf_op jit(solution)/shard_map/ppermute | solution.py:29
  2.2 2.1 %collective-permute-start = (bf16[2,2,128,128]{3,2,1,0:T(8,128)(2,1)S(1)}, bf16[2,2,128,128]{3,2,1,0:T(8,128)(2,1)S(1)}, u32[]{:S(2)}, u32[]{:S(2)}) collective-permute-start(bf16[2,2,128,128]{3,2,1,0:T(8,128)(2,1)S(1)} %pad_maximum_fusion.kv_ref.kv0), channel_id=1, source_target_pairs={{1,65},{65,129},{129,193},{193,257},{257,321},{321,385},{385,449},... | collective-permute-start | bytes 393224 | tf_op jit(solution)/shard_map/ppermute | solution.py:29
  4.4 23.6 %collective-permute-start.4 = (bf16[128,1024]{1,0:T(8,128)(2,1)S(1)}, bf16[128,1024]{1,0:T(8,128)(2,1)S(1)}, u32[]{:S(2)}, u32[]{:S(2)}) collective-permute-start(bf16[128,1024]{1,0:T(8,128)(2,1)S(1)} %query_part.1), channel_id=1, source_target_pairs={{1,0},{2,1},{3,2},{4,3},{5,4},{6,5},{7,6},{8,7},{9,8},{10,9},{11,1... | collective-permute-start | bytes 786440 | tf_op jit(solution)/shard_map/ppermute | solution.py:34
  5.7 8.6 %collective-permute-start.3 = (bf16[2,2,128,128]{3,2,1,0:T(8,128)(2,1)S(1)}, bf16[2,2,128,128]{3,2,1,0:T(8,128)(2,1)S(1)}, u32[]{:S(2)}, u32[]{:S(2)}) collective-permute-start(bf16[2,2,128,128]{3,2,1,0:T(8,128)(2,1)S(1)} %pad_maximum_fusion.kv_ref.kv0), channel_id=1, source_target_pairs={{0,128},{64,192},{128,256},{192,320},{256,384},{320,448},{384,512}... | collective-permute-start | bytes 393224 | tf_op jit(solution)/shard_map/ppermute | solution.py:29
  9.7 14.8 %collective-permute-start.2 = (bf16[2,2,128,128]{3,2,1,0:T(8,128)(2,1)S(1)}, bf16[2,2,128,128]{3,2,1,0:T(8,128)(2,1)S(1)}, u32[]{:S(2)}, u32[]{:S(2)}) collective-permute-start(bf16[2,2,128,128]{3,2,1,0:T(8,128)(2,1)S(1)} %pad_maximum_fusion.kv_ref.kv0), channel_id=1, source_target_pairs={{0,64},{64,128},{128,192},{192,256},{256,320},{320,384},{384,448},... | collective-permute-start | bytes 393224 | tf_op jit(solution)/shard_map/ppermute | solution.py:29
  29.3 15.9 %collective-permute-start.5 = (bf16[2,2,128,128]{3,2,1,0:T(8,128)(2,1)S(1)}, bf16[2,2,128,128]{3,2,1,0:T(8,128)(2,1)S(1)}, u32[]{:S(2)}, u32[]{:S(2)}) collective-permute-start(bf16[2,2,128,128]{3,2,1,0:T(8,128)(2,1)S(1)} %get-tuple-element.45), channel_id=1, source_target_pairs={{0,896},{64,960},{128,0},{192,64},{256,128},{320,192},{384,256},{4... | collective-permute-start | bytes 393224 | tf_op jit(solution)/shard_map/ppermute | solution.py:26
  41.0 7.3 %collective-permute-start.6 = (bf16[2,2,128,128]{3,2,1,0:T(8,128)(2,1)S(1)}, bf16[2,2,128,128]{3,2,1,0:T(8,128)(2,1)S(1)}, u32[]{:S(2)}, u32[]{:S(2)}) collective-permute-start(bf16[2,2,128,128]{3,2,1,0:T(8,128)(2,1)S(1)} %get-tuple-element.46), channel_id=1, source_target_pairs={{0,960},{64,0},{128,64},{192,128},{256,192},{320,256},{384,320},{4... | collective-permute-start | bytes 393224 | tf_op jit(solution)/shard_map/ppermute | solution.py:26

commit v6 on v5

--- a/solution.py
+++ b/solution.py
@@ -20,12 +20,14 @@
     return lax.dot_general(a, b, dims, preferred_element_type=WIDE)
 
 
-def ring(value, steps, sections=None):
+def ring(value, steps, sections=None, cores=(0, 1)):
     count = lax.axis_size("ctx")
+    steps = (steps, steps) if isinstance(steps, int) else steps
+    moves = [(i, (i + steps[i % 2]) % count) for i in range(count) if i % 2 in cores]
     if sections is None:
-        return lax.ppermute(value, "ctx", [(i, (i + steps) % count) for i in range(count)])
+        return lax.ppermute(value, "ctx", moves)
     layers = lax.axis_size("section")
-    route = [(i * layers + s, (i + steps) % count * layers + s) for s in sections for i in range(count)]
+    route = [(i * layers + s, j * layers + s) for s in sections for i, j in moves]
     return lax.ppermute(value, ("ctx", "section"), route)
 
 
@@ -149,9 +151,29 @@
             dq_ref[:, first * size : (first + PAIR) * size] = turned(part, rows).astype(LOW)
 
 
+def own_part(factor, bias_ref, log_rows, kv0, qs_ref, gs_ref, dot_rows, keys_ref, scores_ref, own_ref, dq_v):
+    rows, size = kv0.shape[2], kv0.shape[3]
+    keys, values = kv0[0, 0], kv0[0, 1]
+    keys_t, others_t = keys.T, keys_ref[...].T
+    bias = wider(bias_ref[:rows])
+    step = PAIR * rows
+    key_sum = value_sum = 0.0
+    for first in range(0, qs_ref.shape[0] // rows, PAIR):
+        cut = slice(first * rows, first * rows + step)
+        query, grad = qs_ref[cut], gs_ref[cut]
+        probs = jnp.exp(dot(keys, query, NT) * factor + (bias - head_rows(log_rows, first)))
+        grad_scores = (probs * (dot(values, grad, NT) - head_rows(dot_rows, first))).astype(LOW)
+        key_sum += dot(grad_scores, query)
+        value_sum += dot(probs.astype(LOW), grad)
+        part = (dot(keys_t, grad_scores) + dot(others_t, scores_ref[:, cut])) * factor
+        dq_v[:, first * size : (first + PAIR) * size] = turned(part, rows).astype(LOW)
+    own_ref[0] = key_sum * factor
+    own_ref[1] = value_sum
+
+
 def middle_kernel(
-    factor, bias_ref, log_ref, kv0, kv1, kv2, kv1_first, kv2_first, qs_ref, gs_ref, rd_ref, q_hbm, g_hbm, o_hbm,
-    gq_hbm, own_ref, near_ref, far_ref, qs1_ref, g1_ref, o1_ref, probs_ref, win_ref, q_v, dq_v, sems,
+    factor, bias_ref, log_ref, kv0, kv1, kv2, inner_near, inner_far, to_odd, qs_ref, gs_ref, rd_ref, q_hbm, g_hbm, o_hbm,
+    gq_hbm, own_ref, near_ref, far_ref, scores_ref, keys_ref, qs1_ref, g1_ref, o1_ref, probs_ref, win_ref, q_v, dq_v, sems,
 ):
     copies = [
         pltpu.make_async_copy(q_hbm.at[0, 1], q_v, sems.at[0]),
@@ -163,14 +185,16 @@
     rows, size = kv1.shape[2], kv1.shape[3]
     heads = qs_ref.shape[0] // rows
     bottom = lax.axis_index("section") == 0
+    odd = lax.rem(lax.axis_index("ctx"), 2) == 1
 
     def window(micro, which):
-        near = jnp.where(bottom, kv1_first[micro, which], kv1[micro, which])
-        far = jnp.where(bottom, kv2_first[micro, which], kv2[micro, which])
-        return jnp.concatenate([kv0[micro, which], near, far], axis=0)
+        near = jnp.where(bottom, inner_near[micro, which], kv1[micro, which])
+        far = jnp.where(odd, to_odd[micro, which], inner_far[micro, which])
+        far = jnp.where(bottom, far, kv2[micro, which])
+        return jnp.concatenate([near, far], axis=0)
 
     keys, values = window(0, 0), window(0, 1)
-    keys_t = keys.T
+    keys_ref[...] = keys
     bias = wider(bias_ref[...])
     log_rows, dot_rows = log_ref[0], rd_ref[...]
     step = PAIR * rows
@@ -178,24 +202,29 @@
     for first in range(0, heads, PAIR):
         cut = slice(first * rows, first * rows + step)
         query, grad = qs_ref[cut], gs_ref[cut]
-        probs = jnp.exp(dot(keys, query, NT) * factor + (bias - head_rows(log_rows, first)))
+        probs = jnp.exp(dot(keys, query, NT) * factor + (bias[rows:] - head_rows(log_rows, first)))
         grad_scores = (probs * (dot(values, grad, NT) - head_rows(dot_rows, first))).astype(LOW)
+        scores_ref[:, cut] = grad_scores
         key_sum += dot(grad_scores, query)
         value_sum += dot(probs.astype(LOW), grad)
-        part = dot(keys_t, grad_scores) * factor
-        dq_v[:, first * size : (first + PAIR) * size] = turned(part, rows).astype(LOW)
-    back = pltpu.make_async_copy(dq_v, gq_hbm.at[0, 0], sems.at[3])
-    back.start()
     key_sum = key_sum * factor
-    for i, ref in enumerate((own_ref, near_ref, far_ref)):
-        ref[0] = key_sum[i * rows : (i + 1) * rows].astype(ref.dtype)
-        ref[1] = value_sum[i * rows : (i + 1) * rows].astype(ref.dtype)
+    for i, ref in enumerate((near_ref, far_ref)):
+        ref[0] = key_sum[i * rows : (i + 1) * rows].astype(LOW)
+        ref[1] = value_sum[i * rows : (i + 1) * rows].astype(LOW)
+
+    @pl.when(jnp.logical_not(bottom))
+    def _():
+        own_part(factor, bias_ref, log_rows, kv0, qs_ref, gs_ref, dot_rows, keys_ref, scores_ref, own_ref, dq_v)
+        back = pltpu.make_async_copy(dq_v, gq_hbm.at[0, 0], sems.at[3])
+        back.start()
+        back.wait()
+
     copies[0].wait()
     query = stacked(q_v[...], size)
     qs1_ref[...] = query
-    keys = window(1, 0)
+    keys = jnp.concatenate([kv0[1, 0], window(1, 0)], axis=0)
     win_ref[0] = keys
-    win_ref[1] = window(1, 1)
+    win_ref[1] = jnp.concatenate([kv0[1, 1], window(1, 1)], axis=0)
     log_rows = log_ref[1]
     for first in range(0, heads, PAIR):
         cut = slice(first * rows, first * rows + step)
@@ -203,7 +232,6 @@
         probs_ref[:, cut] = jnp.exp(scores * factor + (bias - head_rows(log_rows, first)))
     copies[1].wait()
     copies[2].wait()
-    back.wait()
 
 
 def others_kernel(factor, win_ref, qs_ref, g_ref, o_ref, probs_ref, near0, far0, r_ref, near_ref, far_ref, up_ref, gs_ref):
@@ -229,17 +257,33 @@
         ref[1, 1] = value_sum[i * rows : (i + 1) * rows].astype(LOW)
 
 
-def rest_kernel(factor, win_ref, qs_ref, probs_ref, up_ref, gs_ref, _, own_ref, gq_hbm, dq_v, sem):
+def rest_kernel(
+    factor, bias_ref, log_ref, kv0, qs0_ref, gs0_ref, rd_ref, keys_ref, scores_ref, own0, win_ref, qs_ref, probs_ref, up_ref, gs_ref, _,
+    own0_ref, own_ref, gq_hbm, dq0_v, dq_v, sems,
+):
     rows = win_ref.shape[1] // WINDOW
     dq_v[...] = turned(dot(win_ref[0].T, gs_ref[...]) * factor, rows).astype(LOW)
-    back = pltpu.make_async_copy(dq_v, gq_hbm.at[0, 1], sem)
+    back = pltpu.make_async_copy(dq_v, gq_hbm.at[0, 1], sems.at[0])
     back.start()
     own_ref[0] = dot(gs_ref[:rows], qs_ref[...]) * factor
     own_ref[1] = dot(probs_ref[:rows].astype(LOW), up_ref[...])
+    bottom = lax.axis_index("section") == 0
+
+    @pl.when(jnp.logical_not(bottom))
+    def _():
+        own0_ref[...] = own0[...]
+
+    @pl.when(bottom)
+    def _():
+        own_part(factor, bias_ref, log_ref[0], kv0, qs0_ref, gs0_ref, rd_ref[...], keys_ref, scores_ref, own0_ref, dq0_v)
+        first = pltpu.make_async_copy(dq0_v, gq_hbm.at[0, 0], sems.at[1])
+        first.start()
+        first.wait()
+
     back.wait()
 
 
-def sum_kernel(own0, own1, far, near, gk_ref, gv_ref):
+def sum_kernel(own0, own1, near, far, gk_ref, gv_ref):
     for micro, own in enumerate((own0, own1)):
         for which, ref in ((0, gk_ref), (1, gv_ref)):
             total = own[which] + near[micro, which].astype(WIDE) + far[micro, which].astype(WIDE)
@@ -285,7 +329,6 @@
     kv0 = jnp.stack([key_in[0], value_in[0]], axis=1)
     upper = range(1, lax.axis_size("section"))
     kv2, kv1 = ring(kv0, 2, upper), ring(kv0, 1, upper)
-    kv2_first, kv1_first = ring(kv0, 2, (0,)), ring(kv0, 1, (0,))
     pair = (2, rows, size)
 
     qs, gs, rd, dqt, bias, log = call(
@@ -312,23 +355,32 @@
     )
     received = down(part)
 
-    grad_query, own0, near0, far0, qs1, g1, o1, probs, win = call(
+    odd = lax.rem(lax.axis_index("ctx"), 2) == 1
+    late, _ = lax.optimization_barrier((kv0, rd))
+    to_odd, even_to_odd = ring(late, 2, (0,), (1,)), ring(late, 3, (0,), (0,))
+    to_odd, even_to_odd, _ = lax.optimization_barrier((to_odd, even_to_odd, part))
+    inner_far = ring(even_to_odd, -1, (0,), (1,))
+    inner_near = ring(jnp.where(odd, to_odd, kv0), (1, -1), (0,))
+
+    grad_query, own0, near0, far0, scores0, keys0, qs1, g1, o1, probs, win = call(
         functools.partial(middle_kernel, factor),
         "middle_terms",
-        (bias, log, kv0, kv1, kv2, kv1_first, kv2_first, qs, gs, rd, query_in, grad_out, forward_out),
+        (bias, log, kv0, kv1, kv2, inner_near, inner_far, to_odd, qs, gs, rd, query_in, grad_out, forward_out),
         [
             low(*query_in.shape),
             wide(*pair),
             low(*pair),
             low(*pair),
+            low((WINDOW - 1) * rows, heads * rows),
+            low((WINDOW - 1) * rows, size),
             low(heads * rows, size),
             low(rows, width),
             low(rows, width),
             wide(near_rows, heads * rows),
             low(2, near_rows, size),
         ],
-        in_specs=[VM] * 10 + [HB] * 3,
-        out_specs=[HB] + [VM] * 8,
+        in_specs=[VM] * 11 + [HB] * 3,
+        out_specs=[HB] + [VM] * 10,
         scratch=[pltpu.VMEM((rows, width), LOW)] * 2 + [dma((4,))],
         share=0.001,
     )
@@ -341,20 +393,20 @@
         share=2,
     )
     far, near = ring(far, -2), ring(near, -1)
-    own1, grad_query = call(
+    own0, own1, grad_query = call(
         functools.partial(rest_kernel, factor),
         "second_rest",
-        (win, qs1, probs, up, grad_scores, grad_query),
-        [wide(*pair), low(*query_in.shape)],
-        in_specs=[VM] * 5 + [HB],
-        out_specs=[VM, HB],
-        scratch=[pltpu.VMEM((rows, width), LOW), dma],
-        input_output_aliases={5: 1},
+        (bias, log, kv0, qs, gs, rd, keys0, scores0, own0, win, qs1, probs, up, grad_scores, grad_query),
+        [wide(*pair), wide(*pair), low(*query_in.shape)],
+        in_specs=[VM] * 14 + [HB],
+        out_specs=[VM, VM, HB],
+        scratch=[pltpu.VMEM((rows, width), LOW)] * 2 + [dma((2,))],
+        input_output_aliases={14: 2},
     )
     grad_key, grad_value = call(
         sum_kernel,
         "sums",
-        (own0, own1, far, near),
+        (own0, own1, near, far),
         [low(1, 2, rows, size)] * 2,
         share=0.01,
     )

time: 49.3 us -> 46.6 us (0.945)
  the two profiles are of different devices: /device:TPU:1 before, /device:TPU:510 now
where the time goes in v6:
time: 46.6 us; the launch traced here: 46.1 us
  waiting for transfers between devices  17.4 us (37%)
  starting transfers between devices  17.3 us (37%)
  Pallas kernels  9.74 us (21%)
  other arithmetic  0.91 us (2%)
  between operations  0.83 us (2%)
    ppermute x1, waiting for transfers between devices, down(): return lax.ppermute(value, 'section', [(i, i - 1) for i in range(1, count)])  11.4 us
    pallas_call x6, Pallas kernels, call(): pl.pallas_call(body, in_specs=in_specs or [VM] * len(ins), out_specs=out_...  9.74 us
    ppermute x6, starting transfers between devices, ring(): return lax.ppermute(value, ('ctx', 'section'), route)  7.9 us
    ppermute x2, waiting for transfers between devices, ring(): return lax.ppermute(value, 'ctx', moves)  5.33 us
    ppermute x2, starting transfers between devices, ring(): return lax.ppermute(value, 'ctx', moves)  5.31 us
    ppermute x1, starting transfers between devices, down(): return lax.ppermute(value, 'section', [(i, i - 1) for i in range(1, count)])  4.04 us
  transfers between devices with their start and end apart: 9, of which 3 were waited for; matrix products, arithmetic and copies ran while one was open for 0% of the time, Pallas kernels for 17%

profile of v6, /device:TPU:510, one launch (start us, length us, event | category | flops | bytes accessed | tf_op | source)
XLA Modules:
  0.0 46.1 jit_solution(12007701802403279911)
XLA Ops:
  0.6 0.9 %pad_maximum_fusion.kv_ref.kv0 = bf16[2,2,128,128]{3,2,1,0:T(8,128)(2,1)S(1)} fusion(bf16[2,1,128,128]{3,2,1,0:T(8,128)(2,1)} %bitcast.2, bf16[2,1,128,128]{3,2,1,0:T(8,128)(2,1)} %bitcast.4), kind=kLoop, calls=%fused_computation | loop fusion | flops 65536 | bytes 262144 | tf_op jit(solution)/shard_map/stack | solution.py:329
  1.5 0.0 copy-start
  1.5 0.0 copy-start.1
  1.5 3.3 %collective-permute-start.1 = (bf16[2,2,128,128]{3,2,1,0:T(8,128)(2,1)S(1)}, bf16[2,2,128,128]{3,2,1,0:T(8,128)(2,1)S(1)}, u32[]{:S(2)}, u32[]{:S(2)}) collective-permute-start(bf16[2,2,128,128]{3,2,1,0:T(8,128)(2,1)S(1)} %pad_maximum_fusion.kv_ref.kv0), channel_id=1, source_target_pairs={{1,129},{65,193},{129,257},{193,321},{257,385},{321,449},{385,513}... | collective-permute-start | bytes 393224 | tf_op jit(solution)/shard_map/ppermute | solution.py:31
  4.9 1.9 %collective-permute-start = (bf16[2,2,128,128]{3,2,1,0:T(8,128)(2,1)S(1)}, bf16[2,2,128,128]{3,2,1,0:T(8,128)(2,1)S(1)}, u32[]{:S(2)}, u32[]{:S(2)}) collective-permute-start(bf16[2,2,128,128]{3,2,1,0:T(8,128)(2,1)S(1)} %pad_maximum_fusion.kv_ref.kv0), channel_id=1, source_target_pairs={{1,65},{65,129},{129,193},{193,257},{257,321},{321,385},{385,449},... | collective-permute-start | bytes 393224 | tf_op jit(solution)/shard_map/ppermute | solution.py:31
  6.8 2.4 %own_terms.1 = (bf16[1024,128]{1,0:T(8,128)(2,1)S(1)}, bf16[1024,128]{1,0:T(8,128)(2,1)S(1)}, f32[8,128]{1,0:T(8,128)S(1)}, f32[128,1024]{1,0:T(8,128)S(1)}, f32...) custom-call(s32[32]{0:T(128)} %order_hbm.1, f32[1,2,8,128]{3,2,1,0:T(8,128)} %log_hbm.1, ...), custom_call_target="tpu_custom_call" | custom-call | flops 201326592 | bytes 1024 | tf_op jit(solution)/shard_map/own_terms/pallas_call | solution.py:312
  9.1 0.7 %collective-permute-start.3 = (bf16[2,2,128,128]{3,2,1,0:T(8,128)(2,1)S(1)}, bf16[2,2,128,128]{3,2,1,0:T(8,128)(2,1)S(1)}, u32[]{:S(2)}, u32[]{:S(2)}) collective-permute-start(bf16[2,2,128,128]{3,2,1,0:T(8,128)(2,1)S(1)} %pad_maximum_fusion.kv_ref.kv0), channel_id=1, source_target_pairs={{0,192},{128,320},{256,448},{384,576},{512,704},{640,832},{768,960... | collective-permute-start | bytes 393224 | tf_op jit(solution)/shard_map/ppermute | solution.py:31
  9.8 0.7 %collective-permute-start.2 = (bf16[2,2,128,128]{3,2,1,0:T(8,128)(2,1)S(1)}, bf16[2,2,128,128]{3,2,1,0:T(8,128)(2,1)S(1)}, u32[]{:S(2)}, u32[]{:S(2)}) collective-permute-start(bf16[2,2,128,128]{3,2,1,0:T(8,128)(2,1)S(1)} %pad_maximum_fusion.kv_ref.kv0), channel_id=1, source_target_pairs={{64,192},{192,320},{320,448},{448,576},{576,704},{704,832},{832,96... | collective-permute-start | bytes 393224 | tf_op jit(solution)/shard_map/ppermute | solution.py:31
  10.5 0.0 collective-permute-done.1.kv2
  10.5 0.6 %collective-permute-done.kv1 = bf16[2,2,128,128]{3,2,1,0:T(8,128)(2,1)S(1)} collective-permute-done((bf16[2,2,128,128]{3,2,1,0:T(8,128)(2,1)S(1)}, bf16[2,2,128,128]{3,2,1,0:T(8,128)(2,1)S(1)}, u32[]{:S(2)}, u32[]{:S(2)}) %collective-permute-start) | collective-permute-done | bytes 131104 | tf_op jit(solution)/shard_map/ppermute | solution.py:31
  11.1 1.1 %query_part.1 = bf16[128,1024]{1,0:T(8,128)(2,1)S(1)} custom-call(f32[384,128]{1,0:T(8,128)S(1)} %get-tuple-element.32.bias_ref, f32[2,8,128]{2,1,0:T(8,128)S(1)} %get-tuple-element.33.log_ref, bf16[2,2,128,128]{3,2,1,0:T(8,128)(2,1)S(1)} %collective-permute-done.kv1, bf16[2,2,128,128]{3,2,1,0:T(8,128)(2,1)S(1)} %collective-permute-done.1.kv2, ...), custom_call_target="tpu_custom_call" | custom-call | flops 100663296 | bytes 1024 | tf_op jit(solution)/shard_map/query_part/pallas_call | solution.py:312
  12.3 4.0 %collective-permute-start.6 = (bf16[128,1024]{1,0:T(8,128)(2,1)S(1)}, bf16[128,1024]{1,0:T(8,128)(2,1)S(1)}, u32[]{:S(2)}, u32[]{:S(2)}) collective-permute-start(bf16[128,1024]{1,0:T(8,128)(2,1)S(1)} %query_part.1), channel_id=1, source_target_pairs={{1,0},{2,1},{3,2},{4,3},{5,4},{6,5},{7,6},{8,7},{9,8},{10,9},{11,1... | collective-permute-start | bytes 786440 | tf_op jit(solution)/shard_map/ppermute | solution.py:36
  16.3 0.0 collective-permute-done.3
  16.3 0.0 collective-permute-done.2.to_odd
  16.4 0.0 copy-done
  16.4 0.0 copy-done.1
  16.4 0.7 %collective-permute-start.4 = (bf16[2,2,128,128]{3,2,1,0:T(8,128)(2,1)S(1)}, bf16[2,2,128,128]{3,2,1,0:T(8,128)(2,1)S(1)}, u32[]{:S(2)}, u32[]{:S(2)}) collective-permute-start(bf16[2,2,128,128]{3,2,1,0:T(8,128)(2,1)S(1)} %broadcast_select_fusion), channel_id=1, source_target_pairs={{0,64},{64,0},{128,192},{192,128},{256,320},{320,256},{384,448},{4... | collective-permute-start | bytes 393224 | tf_op jit(solution)/shard_map/ppermute | solution.py:31
  17.1 0.7 %collective-permute-start.5 = (bf16[2,2,128,128]{3,2,1,0:T(8,128)(2,1)S(1)}, bf16[2,2,128,128]{3,2,1,0:T(8,128)(2,1)S(1)}, u32[]{:S(2)}, u32[]{:S(2)}) collective-permute-start(bf16[2,2,128,128]{3,2,1,0:T(8,128)(2,1)S(1)} %collective-permute-done.3), channel_id=1, source_target_pairs={{64,0},{192,128},{320,256},{448,384},{576,512},{704,640},{832,768}... | collective-permute-start | bytes 393224 | tf_op jit(solution)/shard_map/ppermute | solution.py:31
  17.8 0.0 collective-permute-done.4.inner_near
  17.8 0.0 collective-permute-done.5.inner_far
  17.8 3.1 %middle_terms.1 = (bf16[1,2,128,1024]{3,2,1,0:T(8,128)(2,1)}, f32[2,128,128]{2,1,0:T(8,128)S(1)}, bf16[2,128,128]{2,1,0:T(8,128)(2,1)S(1)}, bf16[2,128,128]{2,1,...) custom-call(f32[384,128]{1,0:T(8,128)S(1)} %get-tuple-element.32.bia, ...), custom_call_target="tpu_custom_call" | custom-call | flops 100663 | bytes 1024 | tf_op jit(solution)/shard_map/middle_terms/pallas_call | solution.py:312
  20.9 11.4 %collective-permute-done.6.r_ref = bf16[128,1024]{1,0:T(8,128)(2,1)S(1)} collective-permute-done((bf16[128,1024]{1,0:T(8,128)(2,1)S(1)}, bf16[128,1024]{1,0:T(8,128)(2,1)S(1)}, u32[]{:S(2)}, u32[]{:S(2)}) %collective-permute-start.6) | collective-permute-done | bytes 262176 | tf_op jit(solution)/shard_map/ppermute | solution.py:36
  32.3 1.3 %second_others.1 = (bf16[2,2,128,128]{3,2,1,0:T(8,128)(2,1)S(1)}, bf16[2,2,128,128]{3,2,1,0:T(8,128)(2,1)S(1)}, bf16[1024,128]{1,0:T(8,128)(2,1)S(1)}, bf16[384,1024]{1,0:T(8,128)(2,1)S(1)}) custom-call(bf16[2,384,128]{2,1,0:T(8,128)(2,1)S(1)} %get-tuple-element.44.win_ref, bf16[1024,128]{1,0:T(8,128)(2,1)S(1)} %get-tuple-element.45.qs_ref, ...), custom_call_target="tpu_custom_call" | custom-call | flops 201326592 | bytes 1024 | tf_op jit(solution)/shard_map/second_others/pallas_call | solution.py:312
  33.6 1.9 %collective-permute-start.7 = (bf16[2,2,128,128]{3,2,1,0:T(8,128)(2,1)S(1)}, bf16[2,2,128,128]{3,2,1,0:T(8,128)(2,1)S(1)}, u32[]{:S(2)}, u32[]{:S(2)}) collective-permute-start(bf16[2,2,128,128]{3,2,1,0:T(8,128)(2,1)S(1)} %get-tuple-element.57), channel_id=1, source_target_pairs={{0,960},{64,0},{128,64},{192,128},{256,192},{320,256},{384,320},{4... | collective-permute-start | bytes 393224 | tf_op jit(solution)/shard_map/ppermute | solution.py:28
  35.6 3.4 %collective-permute-start.8 = (bf16[2,2,128,128]{3,2,1,0:T(8,128)(2,1)S(1)}, bf16[2,2,128,128]{3,2,1,0:T(8,128)(2,1)S(1)}, u32[]{:S(2)}, u32[]{:S(2)}) collective-permute-start(bf16[2,2,128,128]{3,2,1,0:T(8,128)(2,1)S(1)} %get-tuple-element.58), channel_id=1, source_target_pairs={{0,896},{64,960},{128,0},{192,64},{256,128},{320,192},{384,256},{4... | collective-permute-start | bytes 393224 | tf_op jit(solution)/shard_map/ppermute | solution.py:28
  39.0 1.2 %second_rest.1 = (f32[2,128,128]{2,1,0:T(8,128)S(1)}, f32[2,128,128]{2,1,0:T(8,128)S(1)}, bf16[1,2,128,1024]{3,2,1,0:T(8,128)(2,1)}) custom-call(f32[384,128]{1,0:T(8,128)S(1)} %get-tuple-element.32.bias_ref, f32[2,8,128]{2,1,0:T(8,128)S(1)} %get-tuple-element.33.log_ref, ...), custom_call_target="tpu_custom_call", output_to_operand_aliasing={{2}: (14, {})} | custom-call | flops 100663296 | bytes 1024 | tf_op jit(solution)/shard_map/second_rest/pallas_call | solution.py:312
  40.1 0.0 collective-permute-done.7.near
  40.1 5.3 %collective-permute-done.8.far = bf16[2,2,128,128]{3,2,1,0:T(8,128)(2,1)S(1)} collective-permute-done((bf16[2,2,128,128]{3,2,1,0:T(8,128)(2,1)S(1)}, bf16[2,2,128,128]{3,2,1,0:T(8,128)(2,1)S(1)}, u32[]{:S(2)}, u32[]{:S(2)}) %collective-permute-start.8) | collective-permute-done | bytes 131104 | tf_op jit(solution)/shard_map/ppermute | solution.py:28
  45.5 0.7 %sums.1 = (bf16[1,2,128,128]{3,2,1,0:T(8,128)(2,1)}, bf16[1,2,128,128]{3,2,1,0:T(8,128)(2,1)}) custom-call(f32[2,128,128]{2,1,0:T(8,128)S(1)} %get-tuple-element.55.own0, f32[2,128,128]{2,1,0:T(8,128)S(1)} %get-tuple-element.56.own1, bf16[2,2,128,128]{3,2,1,0:T(8,128)(2,1)S(1)} %collective-permute-done.7.near, ...), custom_call_target="tpu_custom_call" | custom-call | flops 1006632 | bytes 1024 | tf_op jit(solution)/shard_map/sums/pallas_call | solution.py:312
  (1 shorter events, 0.0 us)
Async XLA Ops:
  1.5 14.8 %copy-start = (bf16[1,2,128,128]{3,2,1,0:T(8,128)(2,1)S(1)}, bf16[1,2,128,128]{3,2,1,0:T(8,128)(2,1)}, u32[]{:S(2)}) copy-start(bf16[1,2,128,128]{3,2,1,0:T(8,128)(2,1)} %param.9) | copy-start | bytes 196612
  1.5 14.8 %copy-start.1 = (bf16[1,2,128,128]{3,2,1,0:T(8,128)(2,1)S(1)}, bf16[1,2,128,128]{3,2,1,0:T(8,128)(2,1)}, u32[]{:S(2)}) copy-start(bf16[1,2,128,128]{3,2,1,0:T(8,128)(2,1)} %param.8) | copy-start | bytes 196612
  1.5 9.0 %collective-permute-start.1 = (bf16[2,2,128,128]{3,2,1,0:T(8,128)(2,1)S(1)}, bf16[2,2,128,128]{3,2,1,0:T(8,128)(2,1)S(1)}, u32[]{:S(2)}, u32[]{:S(2)}) collective-permute-start(bf16[2,2,128,128]{3,2,1,0:T(8,128)(2,1)S(1)} %pad_maximum_fusion.kv_ref.kv0), channel_id=1, source_target_pairs={{1,129},{65,193},{129,257},{193,321},{257,385},{321,449},{385,513}... | collective-permute-start | bytes 393224 | tf_op jit(solution)/shard_map/ppermute | solution.py:31
  4.9 6.3 %collective-permute-start = (bf16[2,2,128,128]{3,2,1,0:T(8,128)(2,1)S(1)}, bf16[2,2,128,128]{3,2,1,0:T(8,128)(2,1)S(1)}, u32[]{:S(2)}, u32[]{:S(2)}) collective-permute-start(bf16[2,2,128,128]{3,2,1,0:T(8,128)(2,1)S(1)} %pad_maximum_fusion.kv_ref.kv0), channel_id=1, source_target_pairs={{1,65},{65,129},{129,193},{193,257},{257,321},{321,385},{385,449},... | collective-permute-start | bytes 393224 | tf_op jit(solution)/shard_map/ppermute | solution.py:31
  9.1 7.2 %collective-permute-start.3 = (bf16[2,2,128,128]{3,2,1,0:T(8,128)(2,1)S(1)}, bf16[2,2,128,128]{3,2,1,0:T(8,128)(2,1)S(1)}, u32[]{:S(2)}, u32[]{:S(2)}) collective-permute-start(bf16[2,2,128,128]{3,2,1,0:T(8,128)(2,1)S(1)} %pad_maximum_fusion.kv_ref.kv0), channel_id=1, source_target_pairs={{0,192},{128,320},{256,448},{384,576},{512,704},{640,832},{768,960... | collective-permute-start | bytes 393224 | tf_op jit(solution)/shard_map/ppermute | solution.py:31
  9.8 6.5 %collective-permute-start.2 = (bf16[2,2,128,128]{3,2,1,0:T(8,128)(2,1)S(1)}, bf16[2,2,128,128]{3,2,1,0:T(8,128)(2,1)S(1)}, u32[]{:S(2)}, u32[]{:S(2)}) collective-permute-start(bf16[2,2,128,128]{3,2,1,0:T(8,128)(2,1)S(1)} %pad_maximum_fusion.kv_ref.kv0), channel_id=1, source_target_pairs={{64,192},{192,320},{320,448},{448,576},{576,704},{704,832},{832,96... | collective-permute-start | bytes 393224 | tf_op jit(solution)/shard_map/ppermute | solution.py:31
  12.3 20.0 %collective-permute-start.6 = (bf16[128,1024]{1,0:T(8,128)(2,1)S(1)}, bf16[128,1024]{1,0:T(8,128)(2,1)S(1)}, u32[]{:S(2)}, u32[]{:S(2)}) collective-permute-start(bf16[128,1024]{1,0:T(8,128)(2,1)S(1)} %query_part.1), channel_id=1, source_target_pairs={{1,0},{2,1},{3,2},{4,3},{5,4},{6,5},{7,6},{8,7},{9,8},{10,9},{11,1... | collective-permute-start | bytes 786440 | tf_op jit(solution)/shard_map/ppermute | solution.py:36
  16.4 1.4 %collective-permute-start.4 = (bf16[2,2,128,128]{3,2,1,0:T(8,128)(2,1)S(1)}, bf16[2,2,128,128]{3,2,1,0:T(8,128)(2,1)S(1)}, u32[]{:S(2)}, u32[]{:S(2)}) collective-permute-start(bf16[2,2,128,128]{3,2,1,0:T(8,128)(2,1)S(1)} %broadcast_select_fusion), channel_id=1, source_target_pairs={{0,64},{64,0},{128,192},{192,128},{256,320},{320,256},{384,448},{4... | collective-permute-start | bytes 393224 | tf_op jit(solution)/shard_map/ppermute | solution.py:31
  17.1 0.7 %collective-permute-start.5 = (bf16[2,2,128,128]{3,2,1,0:T(8,128)(2,1)S(1)}, bf16[2,2,128,128]{3,2,1,0:T(8,128)(2,1)S(1)}, u32[]{:S(2)}, u32[]{:S(2)}) collective-permute-start(bf16[2,2,128,128]{3,2,1,0:T(8,128)(2,1)S(1)} %collective-permute-done.3), channel_id=1, source_target_pairs={{64,0},{192,128},{320,256},{448,384},{576,512},{704,640},{832,768}... | collective-permute-start | bytes 393224 | tf_op jit(solution)/shard_map/ppermute | solution.py:31
  33.6 6.5 %collective-permute-start.7 = (bf16[2,2,128,128]{3,2,1,0:T(8,128)(2,1)S(1)}, bf16[2,2,128,128]{3,2,1,0:T(8,128)(2,1)S(1)}, u32[]{:S(2)}, u32[]{:S(2)}) collective-permute-start(bf16[2,2,128,128]{3,2,1,0:T(8,128)(2,1)S(1)} %get-tuple-element.57), channel_id=1, source_target_pairs={{0,960},{64,0},{128,64},{192,128},{256,192},{320,256},{384,320},{4... | collective-permute-start | bytes 393224 | tf_op jit(solution)/shard_map/ppermute | solution.py:28
  35.6 9.9 %collective-permute-start.8 = (bf16[2,2,128,128]{3,2,1,0:T(8,128)(2,1)S(1)}, bf16[2,2,128,128]{3,2,1,0:T(8,128)(2,1)S(1)}, u32[]{:S(2)}, u32[]{:S(2)}) collective-permute-start(bf16[2,2,128,128]{3,2,1,0:T(8,128)(2,1)S(1)} %get-tuple-element.58), channel_id=1, source_target_pairs={{0,896},{64,960},{128,0},{192,64},{256,128},{320,192},{384,256},{4... | collective-permute-start | bytes 393224 | tf_op jit(solution)/shard_map/ppermute | solution.py:28

commit v7 on v6

--- a/solution.py
+++ b/solution.py
@@ -283,7 +283,7 @@
     back.wait()
 
 
-def sum_kernel(own0, own1, near, far, gk_ref, gv_ref):
+def sum_kernel(own0, own1, far, near, gk_ref, gv_ref):
     for micro, own in enumerate((own0, own1)):
         for which, ref in ((0, gk_ref), (1, gv_ref)):
             total = own[which] + near[micro, which].astype(WIDE) + far[micro, which].astype(WIDE)
@@ -406,7 +406,7 @@
     grad_key, grad_value = call(
         sum_kernel,
         "sums",
-        (own0, own1, near, far),
+        (own0, own1, far, near),
         [low(1, 2, rows, size)] * 2,
         share=0.01,
     )

time: 46.6 us -> 45.6 us (0.979)
  the two profiles are of different devices: /device:TPU:510 before, /device:TPU:511 now
where the time goes in v7:
time: 45.6 us; the launch traced here: 45.2 us
  starting transfers between devices  18.9 us (41%)
  waiting for transfers between devices  14.8 us (32%)
  Pallas kernels  9.73 us (21%)
  other arithmetic  0.91 us (2%)
  between operations  0.83 us (2%)
    ppermute x1, waiting for transfers between devices, down(): return lax.ppermute(value, 'section', [(i, i - 1) for i in range(1, count)])  10.4 us
    pallas_call x6, Pallas kernels, call(): pl.pallas_call(body, in_specs=in_specs or [VM] * len(ins), out_specs=out_...  9.73 us
    ppermute x6, starting transfers between devices, ring(): return lax.ppermute(value, ('ctx', 'section'), route)  8.85 us
    ppermute x2, starting transfers between devices, ring(): return lax.ppermute(value, 'ctx', moves)  6.33 us
    ppermute x2, waiting for transfers between devices, ring(): return lax.ppermute(value, 'ctx', moves)  4.33 us
    ppermute x1, starting transfers between devices, down(): return lax.ppermute(value, 'section', [(i, i - 1) for i in range(1, count)])  3.76 us
  transfers between devices with their start and end apart: 9, of which 3 were waited for; matrix products, arithmetic and copies ran while one was open for 0% of the time, Pallas kernels for 17%

profile of v7, /device:TPU:511, one launch (start us, length us, event | category | flops | bytes accessed | tf_op | source)
XLA Modules:
  0.0 45.2 jit_solution(5782891753562524965)
XLA Ops:
  0.6 0.9 %pad_maximum_fusion.kv_ref.kv0 = bf16[2,2,128,128]{3,2,1,0:T(8,128)(2,1)S(1)} fusion(bf16[2,1,128,128]{3,2,1,0:T(8,128)(2,1)} %bitcast.2, bf16[2,1,128,128]{3,2,1,0:T(8,128)(2,1)} %bitcast.4), kind=kLoop, calls=%fused_computation | loop fusion | flops 65536 | bytes 262144 | tf_op jit(solution)/shard_map/stack | solution.py:329
  1.5 0.0 copy-start
  1.5 0.0 copy-start.1
  1.5 3.0 %collective-permute-start.1 = (bf16[2,2,128,128]{3,2,1,0:T(8,128)(2,1)S(1)}, bf16[2,2,128,128]{3,2,1,0:T(8,128)(2,1)S(1)}, u32[]{:S(2)}, u32[]{:S(2)}) collective-permute-start(bf16[2,2,128,128]{3,2,1,0:T(8,128)(2,1)S(1)} %pad_maximum_fusion.kv_ref.kv0), channel_id=1, source_target_pairs={{1,129},{65,193},{129,257},{193,321},{257,385},{321,449},{385,513}... | collective-permute-start | bytes 393224 | tf_op jit(solution)/shard_map/ppermute | solution.py:31
  4.6 3.1 %collective-permute-start = (bf16[2,2,128,128]{3,2,1,0:T(8,128)(2,1)S(1)}, bf16[2,2,128,128]{3,2,1,0:T(8,128)(2,1)S(1)}, u32[]{:S(2)}, u32[]{:S(2)}) collective-permute-start(bf16[2,2,128,128]{3,2,1,0:T(8,128)(2,1)S(1)} %pad_maximum_fusion.kv_ref.kv0), channel_id=1, source_target_pairs={{1,65},{65,129},{129,193},{193,257},{257,321},{321,385},{385,449},... | collective-permute-start | bytes 393224 | tf_op jit(solution)/shard_map/ppermute | solution.py:31
  7.7 2.4 %own_terms.1 = (bf16[1024,128]{1,0:T(8,128)(2,1)S(1)}, bf16[1024,128]{1,0:T(8,128)(2,1)S(1)}, f32[8,128]{1,0:T(8,128)S(1)}, f32[128,1024]{1,0:T(8,128)S(1)}, f32...) custom-call(s32[32]{0:T(128)} %order_hbm.1, f32[1,2,8,128]{3,2,1,0:T(8,128)} %log_hbm.1, ...), custom_call_target="tpu_custom_call" | custom-call | flops 201326592 | bytes 1024 | tf_op jit(solution)/shard_map/own_terms/pallas_call | solution.py:312
  10.1 0.7 %collective-permute-start.3 = (bf16[2,2,128,128]{3,2,1,0:T(8,128)(2,1)S(1)}, bf16[2,2,128,128]{3,2,1,0:T(8,128)(2,1)S(1)}, u32[]{:S(2)}, u32[]{:S(2)}) collective-permute-start(bf16[2,2,128,128]{3,2,1,0:T(8,128)(2,1)S(1)} %pad_maximum_fusion.kv_ref.kv0), channel_id=1, source_target_pairs={{0,192},{128,320},{256,448},{384,576},{512,704},{640,832},{768,960... | collective-permute-start | bytes 393224 | tf_op jit(solution)/shard_map/ppermute | solution.py:31
  10.8 0.7 %collective-permute-start.2 = (bf16[2,2,128,128]{3,2,1,0:T(8,128)(2,1)S(1)}, bf16[2,2,128,128]{3,2,1,0:T(8,128)(2,1)S(1)}, u32[]{:S(2)}, u32[]{:S(2)}) collective-permute-start(bf16[2,2,128,128]{3,2,1,0:T(8,128)(2,1)S(1)} %pad_maximum_fusion.kv_ref.kv0), channel_id=1, source_target_pairs={{64,192},{192,320},{320,448},{448,576},{576,704},{704,832},{832,96... | collective-permute-start | bytes 393224 | tf_op jit(solution)/shard_map/ppermute | solution.py:31
  11.4 0.0 collective-permute-done.1.kv2
  11.5 0.0 collective-permute-done.kv1
  11.5 1.1 %query_part.1 = bf16[128,1024]{1,0:T(8,128)(2,1)S(1)} custom-call(f32[384,128]{1,0:T(8,128)S(1)} %get-tuple-element.32.bias_ref, f32[2,8,128]{2,1,0:T(8,128)S(1)} %get-tuple-element.33.log_ref, bf16[2,2,128,128]{3,2,1,0:T(8,128)(2,1)S(1)} %collective-permute-done.kv1, bf16[2,2,128,128]{3,2,1,0:T(8,128)(2,1)S(1)} %collective-permute-done.1.kv2, ...), custom_call_target="tpu_custom_call" | custom-call | flops 100663296 | bytes 1024 | tf_op jit(solution)/shard_map/query_part/pallas_call | solution.py:312
  12.6 3.8 %collective-permute-start.6 = (bf16[128,1024]{1,0:T(8,128)(2,1)S(1)}, bf16[128,1024]{1,0:T(8,128)(2,1)S(1)}, u32[]{:S(2)}, u32[]{:S(2)}) collective-permute-start(bf16[128,1024]{1,0:T(8,128)(2,1)S(1)} %query_part.1), channel_id=1, source_target_pairs={{1,0},{2,1},{3,2},{4,3},{5,4},{6,5},{7,6},{8,7},{9,8},{10,9},{11,1... | collective-permute-start | bytes 786440 | tf_op jit(solution)/shard_map/ppermute | solution.py:36
  16.4 0.0 collective-permute-done.3
  16.4 0.0 collective-permute-done.2.to_odd
  16.4 0.0 copy-done
  16.4 0.0 copy-done.1
  16.5 0.7 %collective-permute-start.4 = (bf16[2,2,128,128]{3,2,1,0:T(8,128)(2,1)S(1)}, bf16[2,2,128,128]{3,2,1,0:T(8,128)(2,1)S(1)}, u32[]{:S(2)}, u32[]{:S(2)}) collective-permute-start(bf16[2,2,128,128]{3,2,1,0:T(8,128)(2,1)S(1)} %broadcast_select_fusion), channel_id=1, source_target_pairs={{0,64},{64,0},{128,192},{192,128},{256,320},{320,256},{384,448},{4... | collective-permute-start | bytes 393224 | tf_op jit(solution)/shard_map/ppermute | solution.py:31
  17.1 0.7 %collective-permute-start.5 = (bf16[2,2,128,128]{3,2,1,0:T(8,128)(2,1)S(1)}, bf16[2,2,128,128]{3,2,1,0:T(8,128)(2,1)S(1)}, u32[]{:S(2)}, u32[]{:S(2)}) collective-permute-start(bf16[2,2,128,128]{3,2,1,0:T(8,128)(2,1)S(1)} %collective-permute-done.3), channel_id=1, source_target_pairs={{64,0},{192,128},{320,256},{448,384},{576,512},{704,640},{832,768}... | collective-permute-start | bytes 393224 | tf_op jit(solution)/shard_map/ppermute | solution.py:31
  17.8 0.0 collective-permute-done.4.inner_near
  17.8 0.0 collective-permute-done.5.inner_far
  17.8 3.1 %middle_terms.1 = (bf16[1,2,128,1024]{3,2,1,0:T(8,128)(2,1)}, f32[2,128,128]{2,1,0:T(8,128)S(1)}, bf16[2,128,128]{2,1,0:T(8,128)(2,1)S(1)}, bf16[2,128,128]{2,1,...) custom-call(f32[384,128]{1,0:T(8,128)S(1)} %get-tuple-element.32.bia, ...), custom_call_target="tpu_custom_call" | custom-call | flops 100663 | bytes 1024 | tf_op jit(solution)/shard_map/middle_terms/pallas_call | solution.py:312
  20.9 10.4 %collective-permute-done.6.r_ref = bf16[128,1024]{1,0:T(8,128)(2,1)S(1)} collective-permute-done((bf16[128,1024]{1,0:T(8,128)(2,1)S(1)}, bf16[128,1024]{1,0:T(8,128)(2,1)S(1)}, u32[]{:S(2)}, u32[]{:S(2)}) %collective-permute-start.6) | collective-permute-done | bytes 262176 | tf_op jit(solution)/shard_map/ppermute | solution.py:36
  31.3 1.3 %second_others.1 = (bf16[2,2,128,128]{3,2,1,0:T(8,128)(2,1)S(1)}, bf16[2,2,128,128]{3,2,1,0:T(8,128)(2,1)S(1)}, bf16[1024,128]{1,0:T(8,128)(2,1)S(1)}, bf16[384,1024]{1,0:T(8,128)(2,1)S(1)}) custom-call(bf16[2,384,128]{2,1,0:T(8,128)(2,1)S(1)} %get-tuple-element.44.win_ref, bf16[1024,128]{1,0:T(8,128)(2,1)S(1)} %get-tuple-element.45.qs_ref, ...), custom_call_target="tpu_custom_call" | custom-call | flops 201326592 | bytes 1024 | tf_op jit(solution)/shard_map/second_others/pallas_call | solution.py:312
  32.7 1.9 %collective-permute-start.7 = (bf16[2,2,128,128]{3,2,1,0:T(8,128)(2,1)S(1)}, bf16[2,2,128,128]{3,2,1,0:T(8,128)(2,1)S(1)}, u32[]{:S(2)}, u32[]{:S(2)}) collective-permute-start(bf16[2,2,128,128]{3,2,1,0:T(8,128)(2,1)S(1)} %get-tuple-element.57), channel_id=1, source_target_pairs={{0,896},{64,960},{128,0},{192,64},{256,128},{320,192},{384,256},{4... | collective-permute-start | bytes 393224 | tf_op jit(solution)/shard_map/ppermute | solution.py:28
  34.6 4.4 %collective-permute-start.8 = (bf16[2,2,128,128]{3,2,1,0:T(8,128)(2,1)S(1)}, bf16[2,2,128,128]{3,2,1,0:T(8,128)(2,1)S(1)}, u32[]{:S(2)}, u32[]{:S(2)}) collective-permute-start(bf16[2,2,128,128]{3,2,1,0:T(8,128)(2,1)S(1)} %get-tuple-element.58), channel_id=1, source_target_pairs={{0,960},{64,0},{128,64},{192,128},{256,192},{320,256},{384,320},{4... | collective-permute-start | bytes 393224 | tf_op jit(solution)/shard_map/ppermute | solution.py:28
  39.0 1.2 %second_rest.1 = (f32[2,128,128]{2,1,0:T(8,128)S(1)}, f32[2,128,128]{2,1,0:T(8,128)S(1)}, bf16[1,2,128,1024]{3,2,1,0:T(8,128)(2,1)}) custom-call(f32[384,128]{1,0:T(8,128)S(1)} %get-tuple-element.32.bias_ref, f32[2,8,128]{2,1,0:T(8,128)S(1)} %get-tuple-element.33.log_ref, ...), custom_call_target="tpu_custom_call", output_to_operand_aliasing={{2}: (14, {})} | custom-call | flops 100663296 | bytes 1024 | tf_op jit(solution)/shard_map/second_rest/pallas_call | solution.py:312
  40.2 0.3 collective-permute-done.7.far
  40.5 4.0 %collective-permute-done.8.near = bf16[2,2,128,128]{3,2,1,0:T(8,128)(2,1)S(1)} collective-permute-done((bf16[2,2,128,128]{3,2,1,0:T(8,128)(2,1)S(1)}, bf16[2,2,128,128]{3,2,1,0:T(8,128)(2,1)S(1)}, u32[]{:S(2)}, u32[]{:S(2)}) %collective-permute-start.8) | collective-permute-done | bytes 131104 | tf_op jit(solution)/shard_map/ppermute | solution.py:28
  44.5 0.7 %sums.1 = (bf16[1,2,128,128]{3,2,1,0:T(8,128)(2,1)}, bf16[1,2,128,128]{3,2,1,0:T(8,128)(2,1)}) custom-call(f32[2,128,128]{2,1,0:T(8,128)S(1)} %get-tuple-element.55.own0, f32[2,128,128]{2,1,0:T(8,128)S(1)} %get-tuple-element.56.own1, bf16[2,2,128,128]{3,2,1,0:T(8,128)(2,1)S(1)} %collective-permute-done.7.far, ...), custom_call_target="tpu_custom_call" | custom-call | flops 1006632 | bytes 1024 | tf_op jit(solution)/shard_map/sums/pallas_call | solution.py:312
  (1 shorter events, 0.0 us)
Async XLA Ops:
  1.5 14.9 %copy-start = (bf16[1,2,128,128]{3,2,1,0:T(8,128)(2,1)S(1)}, bf16[1,2,128,128]{3,2,1,0:T(8,128)(2,1)}, u32[]{:S(2)}) copy-start(bf16[1,2,128,128]{3,2,1,0:T(8,128)(2,1)} %param.9) | copy-start | bytes 196612
  1.5 14.9 %copy-start.1 = (bf16[1,2,128,128]{3,2,1,0:T(8,128)(2,1)S(1)}, bf16[1,2,128,128]{3,2,1,0:T(8,128)(2,1)}, u32[]{:S(2)}) copy-start(bf16[1,2,128,128]{3,2,1,0:T(8,128)(2,1)} %param.8) | copy-start | bytes 196612
  1.5 9.9 %collective-permute-start.1 = (bf16[2,2,128,128]{3,2,1,0:T(8,128)(2,1)S(1)}, bf16[2,2,128,128]{3,2,1,0:T(8,128)(2,1)S(1)}, u32[]{:S(2)}, u32[]{:S(2)}) collective-permute-start(bf16[2,2,128,128]{3,2,1,0:T(8,128)(2,1)S(1)} %pad_maximum_fusion.kv_ref.kv0), channel_id=1, source_target_pairs={{1,129},{65,193},{129,257},{193,321},{257,385},{321,449},{385,513}... | collective-permute-start | bytes 393224 | tf_op jit(solution)/shard_map/ppermute | solution.py:31
  4.6 6.9 %collective-permute-start = (bf16[2,2,128,128]{3,2,1,0:T(8,128)(2,1)S(1)}, bf16[2,2,128,128]{3,2,1,0:T(8,128)(2,1)S(1)}, u32[]{:S(2)}, u32[]{:S(2)}) collective-permute-start(bf16[2,2,128,128]{3,2,1,0:T(8,128)(2,1)S(1)} %pad_maximum_fusion.kv_ref.kv0), channel_id=1, source_target_pairs={{1,65},{65,129},{129,193},{193,257},{257,321},{321,385},{385,449},... | collective-permute-start | bytes 393224 | tf_op jit(solution)/shard_map/ppermute | solution.py:31
  10.1 6.3 %collective-permute-start.3 = (bf16[2,2,128,128]{3,2,1,0:T(8,128)(2,1)S(1)}, bf16[2,2,128,128]{3,2,1,0:T(8,128)(2,1)S(1)}, u32[]{:S(2)}, u32[]{:S(2)}) collective-permute-start(bf16[2,2,128,128]{3,2,1,0:T(8,128)(2,1)S(1)} %pad_maximum_fusion.kv_ref.kv0), channel_id=1, source_target_pairs={{0,192},{128,320},{256,448},{384,576},{512,704},{640,832},{768,960... | collective-permute-start | bytes 393224 | tf_op jit(solution)/shard_map/ppermute | solution.py:31
  10.8 5.6 %collective-permute-start.2 = (bf16[2,2,128,128]{3,2,1,0:T(8,128)(2,1)S(1)}, bf16[2,2,128,128]{3,2,1,0:T(8,128)(2,1)S(1)}, u32[]{:S(2)}, u32[]{:S(2)}) collective-permute-start(bf16[2,2,128,128]{3,2,1,0:T(8,128)(2,1)S(1)} %pad_maximum_fusion.kv_ref.kv0), channel_id=1, source_target_pairs={{64,192},{192,320},{320,448},{448,576},{576,704},{704,832},{832,96... | collective-permute-start | bytes 393224 | tf_op jit(solution)/shard_map/ppermute | solution.py:31
  12.6 18.7 %collective-permute-start.6 = (bf16[128,1024]{1,0:T(8,128)(2,1)S(1)}, bf16[128,1024]{1,0:T(8,128)(2,1)S(1)}, u32[]{:S(2)}, u32[]{:S(2)}) collective-permute-start(bf16[128,1024]{1,0:T(8,128)(2,1)S(1)} %query_part.1), channel_id=1, source_target_pairs={{1,0},{2,1},{3,2},{4,3},{5,4},{6,5},{7,6},{8,7},{9,8},{10,9},{11,1... | collective-permute-start | bytes 786440 | tf_op jit(solution)/shard_map/ppermute | solution.py:36
  16.5 1.4 %collective-permute-start.4 = (bf16[2,2,128,128]{3,2,1,0:T(8,128)(2,1)S(1)}, bf16[2,2,128,128]{3,2,1,0:T(8,128)(2,1)S(1)}, u32[]{:S(2)}, u32[]{:S(2)}) collective-permute-start(bf16[2,2,128,128]{3,2,1,0:T(8,128)(2,1)S(1)} %broadcast_select_fusion), channel_id=1, source_target_pairs={{0,64},{64,0},{128,192},{192,128},{256,320},{320,256},{384,448},{4... | collective-permute-start | bytes 393224 | tf_op jit(solution)/shard_map/ppermute | solution.py:31
  17.1 0.7 %collective-permute-start.5 = (bf16[2,2,128,128]{3,2,1,0:T(8,128)(2,1)S(1)}, bf16[2,2,128,128]{3,2,1,0:T(8,128)(2,1)S(1)}, u32[]{:S(2)}, u32[]{:S(2)}) collective-permute-start(bf16[2,2,128,128]{3,2,1,0:T(8,128)(2,1)S(1)} %collective-permute-done.3), channel_id=1, source_target_pairs={{64,0},{192,128},{320,256},{448,384},{576,512},{704,640},{832,768}... | collective-permute-start | bytes 393224 | tf_op jit(solution)/shard_map/ppermute | solution.py:31
  32.7 7.8 %collective-permute-start.7 = (bf16[2,2,128,128]{3,2,1,0:T(8,128)(2,1)S(1)}, bf16[2,2,128,128]{3,2,1,0:T(8,128)(2,1)S(1)}, u32[]{:S(2)}, u32[]{:S(2)}) collective-permute-start(bf16[2,2,128,128]{3,2,1,0:T(8,128)(2,1)S(1)} %get-tuple-element.57), channel_id=1, source_target_pairs={{0,896},{64,960},{128,0},{192,64},{256,128},{320,192},{384,256},{4... | collective-permute-start | bytes 393224 | tf_op jit(solution)/shard_map/ppermute | solution.py:28
  34.6 9.9 %collective-permute-start.8 = (bf16[2,2,128,128]{3,2,1,0:T(8,128)(2,1)S(1)}, bf16[2,2,128,128]{3,2,1,0:T(8,128)(2,1)S(1)}, u32[]{:S(2)}, u32[]{:S(2)}) collective-permute-start(bf16[2,2,128,128]{3,2,1,0:T(8,128)(2,1)S(1)} %get-tuple-element.58), channel_id=1, source_target_pairs={{0,960},{64,0},{128,64},{192,128},{256,192},{320,256},{384,320},{4... | collective-permute-start | bytes 393224 | tf_op jit(solution)/shard_map/ppermute | solution.py:28

commit v8 on v7

--- a/solution.py
+++ b/solution.py
@@ -151,10 +151,10 @@
             dq_ref[:, first * size : (first + PAIR) * size] = turned(part, rows).astype(LOW)
 
 
-def own_part(factor, bias_ref, log_rows, kv0, qs_ref, gs_ref, dot_rows, keys_ref, scores_ref, own_ref, dq_v):
+def own_part(factor, micro, bias_ref, log_rows, kv0, qs_ref, gs_ref, dot_rows, other_keys, scores_ref, own_ref, dq_v):
     rows, size = kv0.shape[2], kv0.shape[3]
-    keys, values = kv0[0, 0], kv0[0, 1]
-    keys_t, others_t = keys.T, keys_ref[...].T
+    keys, values = kv0[micro, 0], kv0[micro, 1]
+    keys_t, others_t = keys.T, other_keys.T
     bias = wider(bias_ref[:rows])
     step = PAIR * rows
     key_sum = value_sum = 0.0
@@ -214,7 +214,7 @@
 
     @pl.when(jnp.logical_not(bottom))
     def _():
-        own_part(factor, bias_ref, log_rows, kv0, qs_ref, gs_ref, dot_rows, keys_ref, scores_ref, own_ref, dq_v)
+        own_part(factor, 0, bias_ref, log_rows, kv0, qs_ref, gs_ref, dot_rows, keys, scores_ref, own_ref, dq_v)
         back = pltpu.make_async_copy(dq_v, gq_hbm.at[0, 0], sems.at[3])
         back.start()
         back.wait()
@@ -222,23 +222,24 @@
     copies[0].wait()
     query = stacked(q_v[...], size)
     qs1_ref[...] = query
-    keys = jnp.concatenate([kv0[1, 0], window(1, 0)], axis=0)
+    keys = window(1, 0)
     win_ref[0] = keys
-    win_ref[1] = jnp.concatenate([kv0[1, 1], window(1, 1)], axis=0)
+    win_ref[1] = window(1, 1)
     log_rows = log_ref[1]
     for first in range(0, heads, PAIR):
         cut = slice(first * rows, first * rows + step)
         scores = dot(keys, query[cut], NT)
-        probs_ref[:, cut] = jnp.exp(scores * factor + (bias - head_rows(log_rows, first)))
+        probs_ref[:, cut] = jnp.exp(scores * factor + (bias[rows:] - head_rows(log_rows, first)))
     copies[1].wait()
     copies[2].wait()
 
 
-def others_kernel(factor, win_ref, qs_ref, g_ref, o_ref, probs_ref, near0, far0, r_ref, near_ref, far_ref, up_ref, gs_ref):
-    rows, size = win_ref.shape[1] // WINDOW, win_ref.shape[2]
+def others_kernel(factor, win_ref, qs_ref, g_ref, o_ref, probs_ref, near0, far0, r_ref, near_ref, far_ref, up_ref, rd_ref, gs_ref):
+    rows, size = g_ref.shape[0], win_ref.shape[2]
     values = win_ref[1]
     upstream = (g_ref[...].astype(WIDE) + r_ref[...].astype(WIDE)).astype(LOW)
     dot_rows = dots_of_rows(upstream, o_ref[...], size)
+    rd_ref[...] = dot_rows
     upstream = stacked(upstream, size)
     up_ref[...] = upstream
     step = PAIR * rows
@@ -248,8 +249,8 @@
         probs, grad = probs_ref[:, cut], upstream[cut]
         grad_scores = (probs * (dot(values, grad, NT) - head_rows(dot_rows, first))).astype(LOW)
         gs_ref[:, cut] = grad_scores
-        key_sum += dot(grad_scores[rows:], qs_ref[cut])
-        value_sum += dot(probs[rows:].astype(LOW), grad)
+        key_sum += dot(grad_scores, qs_ref[cut])
+        value_sum += dot(probs.astype(LOW), grad)
     key_sum = key_sum * factor
     for i, (ref, before) in enumerate(((near_ref, near0), (far_ref, far0))):
         ref[0] = before[...]
@@ -258,15 +259,12 @@
 
 
 def rest_kernel(
-    factor, bias_ref, log_ref, kv0, qs0_ref, gs0_ref, rd_ref, keys_ref, scores_ref, own0, win_ref, qs_ref, probs_ref, up_ref, gs_ref, _,
+    factor, bias_ref, log_ref, kv0, qs0_ref, gs0_ref, rd_ref, keys_ref, scores_ref, own0, win_ref, qs_ref, up_ref, rd1_ref, gs_ref, _,
     own0_ref, own_ref, gq_hbm, dq0_v, dq_v, sems,
 ):
-    rows = win_ref.shape[1] // WINDOW
-    dq_v[...] = turned(dot(win_ref[0].T, gs_ref[...]) * factor, rows).astype(LOW)
+    own_part(factor, 1, bias_ref, log_ref[1], kv0, qs_ref, up_ref, rd1_ref[...], win_ref[0], gs_ref, own_ref, dq_v)
     back = pltpu.make_async_copy(dq_v, gq_hbm.at[0, 1], sems.at[0])
     back.start()
-    own_ref[0] = dot(gs_ref[:rows], qs_ref[...]) * factor
-    own_ref[1] = dot(probs_ref[:rows].astype(LOW), up_ref[...])
     bottom = lax.axis_index("section") == 0
 
     @pl.when(jnp.logical_not(bottom))
@@ -275,7 +273,7 @@
 
     @pl.when(bottom)
     def _():
-        own_part(factor, bias_ref, log_ref[0], kv0, qs0_ref, gs0_ref, rd_ref[...], keys_ref, scores_ref, own0_ref, dq0_v)
+        own_part(factor, 0, bias_ref, log_ref[0], kv0, qs0_ref, gs0_ref, rd_ref[...], keys_ref[...], scores_ref, own0_ref, dq0_v)
         first = pltpu.make_async_copy(dq0_v, gq_hbm.at[0, 0], sems.at[1])
         first.start()
         first.wait()
@@ -376,8 +374,8 @@
             low(heads * rows, size),
             low(rows, width),
             low(rows, width),
-            wide(near_rows, heads * rows),
-            low(2, near_rows, size),
+            wide((WINDOW - 1) * rows, heads * rows),
+            low(2, (WINDOW - 1) * rows, size),
         ],
         in_specs=[VM] * 11 + [HB] * 3,
         out_specs=[HB] + [VM] * 10,
@@ -385,18 +383,18 @@
         share=0.001,
     )
 
-    near, far, up, grad_scores = call(
+    near, far, up, rd1, grad_scores = call(
         functools.partial(others_kernel, factor),
         "second_others",
         (win, qs1, g1, o1, probs, near0, far0, received),
-        [low(2, *pair), low(2, *pair), low(heads * rows, size), low(near_rows, heads * rows)],
+        [low(2, *pair), low(2, *pair), low(heads * rows, size), wide(8, rows), low((WINDOW - 1) * rows, heads * rows)],
         share=2,
     )
     far, near = ring(far, -2), ring(near, -1)
     own0, own1, grad_query = call(
         functools.partial(rest_kernel, factor),
         "second_rest",
-        (bias, log, kv0, qs, gs, rd, keys0, scores0, own0, win, qs1, probs, up, grad_scores, grad_query),
+        (bias, log, kv0, qs, gs, rd, keys0, scores0, own0, win, qs1, up, rd1, grad_scores, grad_query),
         [wide(*pair), wide(*pair), low(*query_in.shape)],
         in_specs=[VM] * 14 + [HB],
         out_specs=[VM, VM, HB],

time: 45.6 us -> 45.3 us (level)
  the two profiles are of different devices: /device:TPU:511 before, /device:TPU:255 now
where the time goes in v8:
time: 45.3 us; the launch traced here: 44.9 us
  starting transfers between devices  18.8 us (42%)
  waiting for transfers between devices  14.4 us (32%)
  Pallas kernels  9.89 us (22%)
  other arithmetic  0.91 us (2%)
  between operations  0.84 us (2%)
    ppermute x1, waiting for transfers between devices, down(): return lax.ppermute(value, 'section', [(i, i - 1) for i in range(1, count)])  10.5 us
    pallas_call x6, Pallas kernels, call(): pl.pallas_call(body, in_specs=in_specs or [VM] * len(ins), out_specs=out_...  9.89 us
    ppermute x6, starting transfers between devices, ring(): return lax.ppermute(value, ('ctx', 'section'), route)  8.71 us
    ppermute x2, starting transfers between devices, ring(): return lax.ppermute(value, 'ctx', moves)  6.32 us
    ppermute x2, waiting for transfers between devices, ring(): return lax.ppermute(value, 'ctx', moves)  3.86 us
    ppermute x1, starting transfers between devices, down(): return lax.ppermute(value, 'section', [(i, i - 1) for i in range(1, count)])  3.76 us
  transfers between devices with their start and end apart: 9, of which 2 were waited for; matrix products, arithmetic and copies ran while one was open for 0% of the time, Pallas kernels for 18%

profile of v8, /device:TPU:255, one launch (start us, length us, event | category | flops | bytes accessed | tf_op | source)
XLA Modules:
  0.0 44.9 jit_solution(2563177603531163698)
XLA Ops:
  0.6 0.9 %pad_maximum_fusion.kv_ref.kv0 = bf16[2,2,128,128]{3,2,1,0:T(8,128)(2,1)S(1)} fusion(bf16[2,1,128,128]{3,2,1,0:T(8,128)(2,1)} %bitcast.2, bf16[2,1,128,128]{3,2,1,0:T(8,128)(2,1)} %bitcast.4), kind=kLoop, calls=%fused_computation | loop fusion | flops 65536 | bytes 262144 | tf_op jit(solution)/shard_map/stack | solution.py:327
  1.5 2.9 %collective-permute-start.1 = (bf16[2,2,128,128]{3,2,1,0:T(8,128)(2,1)S(1)}, bf16[2,2,128,128]{3,2,1,0:T(8,128)(2,1)S(1)}, u32[]{:S(2)}, u32[]{:S(2)}) collective-permute-start(bf16[2,2,128,128]{3,2,1,0:T(8,128)(2,1)S(1)} %pad_maximum_fusion.kv_ref.kv0), channel_id=1, source_target_pairs={{1,129},{65,193},{129,257},{193,321},{257,385},{321,449},{385,513}... | collective-permute-start | bytes 393224 | tf_op jit(solution)/shard_map/ppermute | solution.py:31
  4.4 3.1 %collective-permute-start = (bf16[2,2,128,128]{3,2,1,0:T(8,128)(2,1)S(1)}, bf16[2,2,128,128]{3,2,1,0:T(8,128)(2,1)S(1)}, u32[]{:S(2)}, u32[]{:S(2)}) collective-permute-start(bf16[2,2,128,128]{3,2,1,0:T(8,128)(2,1)S(1)} %pad_maximum_fusion.kv_ref.kv0), channel_id=1, source_target_pairs={{1,65},{65,129},{129,193},{193,257},{257,321},{321,385},{385,449},... | collective-permute-start | bytes 393224 | tf_op jit(solution)/shard_map/ppermute | solution.py:31
  7.6 2.3 %own_terms.1 = (bf16[1024,128]{1,0:T(8,128)(2,1)S(1)}, bf16[1024,128]{1,0:T(8,128)(2,1)S(1)}, f32[8,128]{1,0:T(8,128)S(1)}, f32[128,1024]{1,0:T(8,128)S(1)}, f32...) custom-call(s32[32]{0:T(128)} %order_hbm.1, f32[1,2,8,128]{3,2,1,0:T(8,128)} %log_hbm.1, ...), custom_call_target="tpu_custom_call" | custom-call | flops 201326592 | bytes 1024 | tf_op jit(solution)/shard_map/own_terms/pallas_call | solution.py:310
  9.9 0.7 %collective-permute-start.3 = (bf16[2,2,128,128]{3,2,1,0:T(8,128)(2,1)S(1)}, bf16[2,2,128,128]{3,2,1,0:T(8,128)(2,1)S(1)}, u32[]{:S(2)}, u32[]{:S(2)}) collective-permute-start(bf16[2,2,128,128]{3,2,1,0:T(8,128)(2,1)S(1)} %pad_maximum_fusion.kv_ref.kv0), channel_id=1, source_target_pairs={{0,192},{128,320},{256,448},{384,576},{512,704},{640,832},{768,960... | collective-permute-start | bytes 393224 | tf_op jit(solution)/shard_map/ppermute | solution.py:31
  10.6 0.7 %collective-permute-start.2 = (bf16[2,2,128,128]{3,2,1,0:T(8,128)(2,1)S(1)}, bf16[2,2,128,128]{3,2,1,0:T(8,128)(2,1)S(1)}, u32[]{:S(2)}, u32[]{:S(2)}) collective-permute-start(bf16[2,2,128,128]{3,2,1,0:T(8,128)(2,1)S(1)} %pad_maximum_fusion.kv_ref.kv0), channel_id=1, source_target_pairs={{64,192},{192,320},{320,448},{448,576},{576,704},{704,832},{832,96... | collective-permute-start | bytes 393224 | tf_op jit(solution)/shard_map/ppermute | solution.py:31
  11.3 0.0 collective-permute-done.1.kv2
  11.3 0.0 collective-permute-done.kv1
  11.3 0.0 copy-start
  11.3 0.0 copy-start.1
  11.3 1.1 %query_part.1 = bf16[128,1024]{1,0:T(8,128)(2,1)S(1)} custom-call(f32[384,128]{1,0:T(8,128)S(1)} %get-tuple-element.33.bias_ref, f32[2,8,128]{2,1,0:T(8,128)S(1)} %get-tuple-element.34.log_ref, bf16[2,2,128,128]{3,2,1,0:T(8,128)(2,1)S(1)} %collective-permute-done.kv1, bf16[2,2,128,128]{3,2,1,0:T(8,128)(2,1)S(1)} %collective-permute-done.1.kv2, ...), custom_call_target="tpu_custom_call" | custom-call | flops 100663296 | bytes 1024 | tf_op jit(solution)/shard_map/query_part/pallas_call | solution.py:310
  12.5 3.8 %collective-permute-start.6 = (bf16[128,1024]{1,0:T(8,128)(2,1)S(1)}, bf16[128,1024]{1,0:T(8,128)(2,1)S(1)}, u32[]{:S(2)}, u32[]{:S(2)}) collective-permute-start(bf16[128,1024]{1,0:T(8,128)(2,1)S(1)} %query_part.1), channel_id=1, source_target_pairs={{1,0},{2,1},{3,2},{4,3},{5,4},{6,5},{7,6},{8,7},{9,8},{10,9},{11,1... | collective-permute-start | bytes 786440 | tf_op jit(solution)/shard_map/ppermute | solution.py:36
  16.3 0.0 collective-permute-done.3
  16.3 0.0 collective-permute-done.2.to_odd
  16.3 0.0 copy-done
  16.3 0.0 copy-done.1
  16.3 0.7 %collective-permute-start.4 = (bf16[2,2,128,128]{3,2,1,0:T(8,128)(2,1)S(1)}, bf16[2,2,128,128]{3,2,1,0:T(8,128)(2,1)S(1)}, u32[]{:S(2)}, u32[]{:S(2)}) collective-permute-start(bf16[2,2,128,128]{3,2,1,0:T(8,128)(2,1)S(1)} %broadcast_select_fusion), channel_id=1, source_target_pairs={{0,64},{64,0},{128,192},{192,128},{256,320},{320,256},{384,448},{4... | collective-permute-start | bytes 393224 | tf_op jit(solution)/shard_map/ppermute | solution.py:31
  17.0 0.7 %collective-permute-start.5 = (bf16[2,2,128,128]{3,2,1,0:T(8,128)(2,1)S(1)}, bf16[2,2,128,128]{3,2,1,0:T(8,128)(2,1)S(1)}, u32[]{:S(2)}, u32[]{:S(2)}) collective-permute-start(bf16[2,2,128,128]{3,2,1,0:T(8,128)(2,1)S(1)} %collective-permute-done.3), channel_id=1, source_target_pairs={{64,0},{192,128},{320,256},{448,384},{576,512},{704,640},{832,768}... | collective-permute-start | bytes 393224 | tf_op jit(solution)/shard_map/ppermute | solution.py:31
  17.7 0.0 collective-permute-done.4.inner_near
  17.7 0.0 collective-permute-done.5.inner_far
  17.7 3.0 %middle_terms.1 = (bf16[1,2,128,1024]{3,2,1,0:T(8,128)(2,1)}, f32[2,128,128]{2,1,0:T(8,128)S(1)}, bf16[2,128,128]{2,1,0:T(8,128)(2,1)S(1)}, bf16[2,128,128]{2,1,...) custom-call(f32[384,128]{1,0:T(8,128)S(1)} %get-tuple-element.33.bia, ...), custom_call_target="tpu_custom_call" | custom-call | flops 100663 | bytes 1024 | tf_op jit(solution)/shard_map/middle_terms/pallas_call | solution.py:310
  20.7 10.5 %collective-permute-done.6.r_ref = bf16[128,1024]{1,0:T(8,128)(2,1)S(1)} collective-permute-done((bf16[128,1024]{1,0:T(8,128)(2,1)S(1)}, bf16[128,1024]{1,0:T(8,128)(2,1)S(1)}, u32[]{:S(2)}, u32[]{:S(2)}) %collective-permute-start.6) | collective-permute-done | bytes 262176 | tf_op jit(solution)/shard_map/ppermute | solution.py:36
  31.2 1.1 %second_others.1 = (bf16[2,2,128,128]{3,2,1,0:T(8,128)(2,1)S(1)}, bf16[2,2,128,128]{3,2,1,0:T(8,128)(2,1)S(1)}, bf16[1024,128]{1,0:T(8,128)(2,1)S(1)}, f32[8,128]{1,0:T(8,128)S(1)}, bf16[256,1024]{1,0:T(8,128)(2,1)S(1)}) custom-call(bf16[2,256,128]{2,1,0:T(8,128)(2,1)S(1)} %get-tuple-element.45.win_ref, bf16[1024,128]{1,0:T(8,128)(2,1)S(1)} %get-tuple-element.46.qs_ref, ...), custom_call_target="tpu_custom_call" | custom-call | flops 201326592 | bytes 1024 | tf_op jit(solution)/shard_map/second_others/pallas_call | solution.py:310
  32.3 1.9 %collective-permute-start.7 = (bf16[2,2,128,128]{3,2,1,0:T(8,128)(2,1)S(1)}, bf16[2,2,128,128]{3,2,1,0:T(8,128)(2,1)S(1)}, u32[]{:S(2)}, u32[]{:S(2)}) collective-permute-start(bf16[2,2,128,128]{3,2,1,0:T(8,128)(2,1)S(1)} %get-tuple-element.59), channel_id=1, source_target_pairs={{0,896},{64,960},{128,0},{192,64},{256,128},{320,192},{384,256},{4... | collective-permute-start | bytes 393224 | tf_op jit(solution)/shard_map/ppermute | solution.py:28
  34.3 4.4 %collective-permute-start.8 = (bf16[2,2,128,128]{3,2,1,0:T(8,128)(2,1)S(1)}, bf16[2,2,128,128]{3,2,1,0:T(8,128)(2,1)S(1)}, u32[]{:S(2)}, u32[]{:S(2)}) collective-permute-start(bf16[2,2,128,128]{3,2,1,0:T(8,128)(2,1)S(1)} %get-tuple-element.60), channel_id=1, source_target_pairs={{0,960},{64,0},{128,64},{192,128},{256,192},{320,256},{384,320},{4... | collective-permute-start | bytes 393224 | tf_op jit(solution)/shard_map/ppermute | solution.py:28
  38.7 1.6 %second_rest.1 = (f32[2,128,128]{2,1,0:T(8,128)S(1)}, f32[2,128,128]{2,1,0:T(8,128)S(1)}, bf16[1,2,128,1024]{3,2,1,0:T(8,128)(2,1)}) custom-call(f32[384,128]{1,0:T(8,128)S(1)} %get-tuple-element.33.bias_ref, f32[2,8,128]{2,1,0:T(8,128)S(1)} %get-tuple-element.34.log_ref, ...), custom_call_target="tpu_custom_call", output_to_operand_aliasing={{2}: (14, {})} | custom-call | flops 100663296 | bytes 1024 | tf_op jit(solution)/shard_map/second_rest/pallas_call | solution.py:310
  40.3 0.0 collective-permute-done.7.far
  40.3 3.9 %collective-permute-done.8.near = bf16[2,2,128,128]{3,2,1,0:T(8,128)(2,1)S(1)} collective-permute-done((bf16[2,2,128,128]{3,2,1,0:T(8,128)(2,1)S(1)}, bf16[2,2,128,128]{3,2,1,0:T(8,128)(2,1)S(1)}, u32[]{:S(2)}, u32[]{:S(2)}) %collective-permute-start.8) | collective-permute-done | bytes 131104 | tf_op jit(solution)/shard_map/ppermute | solution.py:28
  44.2 0.7 %sums.1 = (bf16[1,2,128,128]{3,2,1,0:T(8,128)(2,1)}, bf16[1,2,128,128]{3,2,1,0:T(8,128)(2,1)}) custom-call(f32[2,128,128]{2,1,0:T(8,128)S(1)} %get-tuple-element.57.own0, f32[2,128,128]{2,1,0:T(8,128)S(1)} %get-tuple-element.58.own1, bf16[2,2,128,128]{3,2,1,0:T(8,128)(2,1)S(1)} %collective-permute-done.7.far, ...), custom_call_target="tpu_custom_call" | custom-call | flops 1006632 | bytes 1024 | tf_op jit(solution)/shard_map/sums/pallas_call | solution.py:310
  (1 shorter events, 0.0 us)
Async XLA Ops:
  1.5 9.8 %collective-permute-start.1 = (bf16[2,2,128,128]{3,2,1,0:T(8,128)(2,1)S(1)}, bf16[2,2,128,128]{3,2,1,0:T(8,128)(2,1)S(1)}, u32[]{:S(2)}, u32[]{:S(2)}) collective-permute-start(bf16[2,2,128,128]{3,2,1,0:T(8,128)(2,1)S(1)} %pad_maximum_fusion.kv_ref.kv0), channel_id=1, source_target_pairs={{1,129},{65,193},{129,257},{193,321},{257,385},{321,449},{385,513}... | collective-permute-start | bytes 393224 | tf_op jit(solution)/shard_map/ppermute | solution.py:31
  4.4 6.9 %collective-permute-start = (bf16[2,2,128,128]{3,2,1,0:T(8,128)(2,1)S(1)}, bf16[2,2,128,128]{3,2,1,0:T(8,128)(2,1)S(1)}, u32[]{:S(2)}, u32[]{:S(2)}) collective-permute-start(bf16[2,2,128,128]{3,2,1,0:T(8,128)(2,1)S(1)} %pad_maximum_fusion.kv_ref.kv0), channel_id=1, source_target_pairs={{1,65},{65,129},{129,193},{193,257},{257,321},{321,385},{385,449},... | collective-permute-start | bytes 393224 | tf_op jit(solution)/shard_map/ppermute | solution.py:31
  9.9 6.3 %collective-permute-start.3 = (bf16[2,2,128,128]{3,2,1,0:T(8,128)(2,1)S(1)}, bf16[2,2,128,128]{3,2,1,0:T(8,128)(2,1)S(1)}, u32[]{:S(2)}, u32[]{:S(2)}) collective-permute-start(bf16[2,2,128,128]{3,2,1,0:T(8,128)(2,1)S(1)} %pad_maximum_fusion.kv_ref.kv0), channel_id=1, source_target_pairs={{0,192},{128,320},{256,448},{384,576},{512,704},{640,832},{768,960... | collective-permute-start | bytes 393224 | tf_op jit(solution)/shard_map/ppermute | solution.py:31
  10.6 5.7 %collective-permute-start.2 = (bf16[2,2,128,128]{3,2,1,0:T(8,128)(2,1)S(1)}, bf16[2,2,128,128]{3,2,1,0:T(8,128)(2,1)S(1)}, u32[]{:S(2)}, u32[]{:S(2)}) collective-permute-start(bf16[2,2,128,128]{3,2,1,0:T(8,128)(2,1)S(1)} %pad_maximum_fusion.kv_ref.kv0), channel_id=1, source_target_pairs={{64,192},{192,320},{320,448},{448,576},{576,704},{704,832},{832,96... | collective-permute-start | bytes 393224 | tf_op jit(solution)/shard_map/ppermute | solution.py:31
  11.3 5.0 %copy-start = (bf16[1,2,128,128]{3,2,1,0:T(8,128)(2,1)S(1)}, bf16[1,2,128,128]{3,2,1,0:T(8,128)(2,1)}, u32[]{:S(2)}) copy-start(bf16[1,2,128,128]{3,2,1,0:T(8,128)(2,1)} %param.9) | copy-start | bytes 196612
  11.3 5.0 %copy-start.1 = (bf16[1,2,128,128]{3,2,1,0:T(8,128)(2,1)S(1)}, bf16[1,2,128,128]{3,2,1,0:T(8,128)(2,1)}, u32[]{:S(2)}) copy-start(bf16[1,2,128,128]{3,2,1,0:T(8,128)(2,1)} %param.8) | copy-start | bytes 196612
  12.5 18.7 %collective-permute-start.6 = (bf16[128,1024]{1,0:T(8,128)(2,1)S(1)}, bf16[128,1024]{1,0:T(8,128)(2,1)S(1)}, u32[]{:S(2)}, u32[]{:S(2)}) collective-permute-start(bf16[128,1024]{1,0:T(8,128)(2,1)S(1)} %query_part.1), channel_id=1, source_target_pairs={{1,0},{2,1},{3,2},{4,3},{5,4},{6,5},{7,6},{8,7},{9,8},{10,9},{11,1... | collective-permute-start | bytes 786440 | tf_op jit(solution)/shard_map/ppermute | solution.py:36
  16.3 1.4 %collective-permute-start.4 = (bf16[2,2,128,128]{3,2,1,0:T(8,128)(2,1)S(1)}, bf16[2,2,128,128]{3,2,1,0:T(8,128)(2,1)S(1)}, u32[]{:S(2)}, u32[]{:S(2)}) collective-permute-start(bf16[2,2,128,128]{3,2,1,0:T(8,128)(2,1)S(1)} %broadcast_select_fusion), channel_id=1, source_target_pairs={{0,64},{64,0},{128,192},{192,128},{256,320},{320,256},{384,448},{4... | collective-permute-start | bytes 393224 | tf_op jit(solution)/shard_map/ppermute | solution.py:31
  17.0 0.7 %collective-permute-start.5 = (bf16[2,2,128,128]{3,2,1,0:T(8,128)(2,1)S(1)}, bf16[2,2,128,128]{3,2,1,0:T(8,128)(2,1)S(1)}, u32[]{:S(2)}, u32[]{:S(2)}) collective-permute-start(bf16[2,2,128,128]{3,2,1,0:T(8,128)(2,1)S(1)} %collective-permute-done.3), channel_id=1, source_target_pairs={{64,0},{192,128},{320,256},{448,384},{576,512},{704,640},{832,768}... | collective-permute-start | bytes 393224 | tf_op jit(solution)/shard_map/ppermute | solution.py:31
  32.3 8.0 %collective-permute-start.7 = (bf16[2,2,128,128]{3,2,1,0:T(8,128)(2,1)S(1)}, bf16[2,2,128,128]{3,2,1,0:T(8,128)(2,1)S(1)}, u32[]{:S(2)}, u32[]{:S(2)}) collective-permute-start(bf16[2,2,128,128]{3,2,1,0:T(8,128)(2,1)S(1)} %get-tuple-element.59), channel_id=1, source_target_pairs={{0,896},{64,960},{128,0},{192,64},{256,128},{320,192},{384,256},{4... | collective-permute-start | bytes 393224 | tf_op jit(solution)/shard_map/ppermute | solution.py:28
  34.3 9.9 %collective-permute-start.8 = (bf16[2,2,128,128]{3,2,1,0:T(8,128)(2,1)S(1)}, bf16[2,2,128,128]{3,2,1,0:T(8,128)(2,1)S(1)}, u32[]{:S(2)}, u32[]{:S(2)}) collective-permute-start(bf16[2,2,128,128]{3,2,1,0:T(8,128)(2,1)S(1)} %get-tuple-element.60), channel_id=1, source_target_pairs={{0,960},{64,0},{128,64},{192,128},{256,192},{320,256},{384,320},{4... | collective-permute-start | bytes 393224 | tf_op jit(solution)/shard_map/ppermute | solution.py:28
